TPU v7x, 128 devices: a whole 4x4x4 slice. The times are simulated.
128 devices in a mesh: row: 16 (over x, y_hi, core), col: 8 (over y_lo, z).
Axes of the slice: x: 4, y: 4 (y_hi: 2, y_lo: 2; y = y_hi * 2 + y_lo), z: 4, core: 2. Of those that a mesh axis runs over, the one named last changes fastest.
Arguments:
- pair: bfloat16 [1024, 1024, 128], P('row', 'col'), may hold values from -3 to 3
- norm_gain: float32 [128], replicated, may hold values from 0.5 to 1.5
- norm_shift: float32 [128], replicated, may hold values from -3 to 3
- proj_weight: bfloat16 [128, 384], replicated, may hold values from -0.5 to 0.5
- proj_bias: float32 [384], replicated, may hold values from -3 to 3
- mid_gain: float32 [64], replicated, may hold values from 0.5 to 1.5
- mid_shift: float32 [64], replicated, may hold values from -3 to 3
- out_weight: bfloat16 [64, 128], replicated, may hold values from -1.5 to 1.5
- out_bias: float32 [128], replicated, may hold values from -3 to 3
- conv_gain: float32 [2, 128], replicated, may hold values from 0.5 to 1.5
- conv_shift: float32 [2, 128], replicated, may hold values from -3 to 3
- convolution_weight: bfloat16 [2, 9, 128, 128], replicated, may hold values from -0.375 to 0.375
- convolution_bias: float32 [2, 128], replicated, may hold values from -2 to 2
Outputs:
- refined: bfloat16 [1024, 1024, 128], P('row', 'col')
All inputs are finite; a program needn't handle non-finite values.
Results may differ from a plain program's by a relative error of at most 0.008.
Values may be sent and summed in bfloat16 or wider, within the bound.
No kernel may reach another device: no remote copies, remote signals or barrier semaphores. Data moves between devices by JAX's collectives and lax.ppermute only.
A program may use at most 128 MiB of HBM per device.

v0:
```python
import jax
import jax.numpy as jnp
from jax import lax
from jax.sharding import PartitionSpec as P

FIRST_DILATION = 2
SECOND_DILATION = 4


EPS = 1e-05


def padded(block, sides, width):
    for axis, dim in sides:
        count = lax.axis_size(axis)
        forward = [(i, i + 1) for i in range(count - 1)]
        backward = [(target, source) for source, target in forward]
        low = lax.ppermute(
            lax.slice_in_dim(block, block.shape[dim] - width, None, axis=dim), axis, forward
        )
        high = lax.ppermute(lax.slice_in_dim(block, 0, width, axis=dim), axis, backward)
        block = jnp.concatenate([low, block, high], axis=dim)
    return block


def normalize(values, gain, shift):
    mean = jnp.mean(values, axis=-1, keepdims=True)
    centred = values - mean
    spread = jnp.mean(centred * centred, axis=-1, keepdims=True)
    return centred * lax.rsqrt(spread + EPS) * gain + shift


def regroup(block, row_count, col_count):
    total_rows, width_cols, last = block.shape
    ratio = row_count // col_count
    tile = total_rows // (col_count * ratio)
    shaped = block.reshape(col_count, ratio, tile, width_cols, last)
    return jnp.transpose(shaped, (1, 0, 2, 3, 4)).reshape(total_rows, width_cols, last)


def dilated_output(source, kernel, spacing, out_rows, out_cols):
    width = source.shape[2]
    total = jnp.zeros((out_rows * out_cols, kernel.shape[2]), jnp.float32)
    for tap in range(9):
        down = spacing + (tap // 3 - 1) * spacing
        across = spacing + (tap % 3 - 1) * spacing
        window = lax.slice(source, (down, across, 0), (down + out_rows, across + out_cols, width))
        total = total + jnp.dot(
            window.reshape(out_rows * out_cols, width),
            kernel[tap],
            preferred_element_type=jnp.float32,
        )
    return total.reshape(out_rows, out_cols, kernel.shape[2])


def local(
    pair,
    norm_gain,
    norm_shift,
    proj_weight,
    proj_bias,
    mid_gain,
    mid_shift,
    out_weight,
    out_bias,
    conv_gain,
    conv_shift,
    convolution_weight,
    convolution_bias,
):
    row_total, column_total, width = pair.shape
    hidden = mid_gain.shape[0]
    row_count = lax.axis_size("row")
    col_count = lax.axis_size("col")
    pair_wide = pair.astype(jnp.float32)
    normed = normalize(pair_wide, norm_gain, norm_shift).astype(jnp.bfloat16)
    projected = (
        jnp.dot(
            normed.reshape(row_total * column_total, width),
            proj_weight,
            preferred_element_type=jnp.float32,
        )
        + proj_bias
    )
    left = (
        (jax.nn.sigmoid(projected[:, :hidden]) * projected[:, hidden : 2 * hidden])
        .astype(jnp.bfloat16)
        .reshape(row_total, column_total, hidden)
    )
    right = (
        (
            jax.nn.sigmoid(projected[:, 2 * hidden : 3 * hidden])
            * projected[:, 3 * hidden : 4 * hidden]
        )
        .astype(jnp.bfloat16)
        .reshape(row_total, column_total, hidden)
    )
    out_gate = jax.nn.sigmoid(projected[:, 4 * hidden :])
    left_full = lax.all_gather(left, "col", axis=1, tiled=True)
    right_one = lax.all_to_all(right, "col", split_axis=0, concat_axis=1, tiled=True)
    right_two = lax.all_to_all(
        lax.all_to_all(right_one, "row", split_axis=1, concat_axis=0, tiled=True),
        "col",
        split_axis=0,
        concat_axis=0,
        tiled=True,
    )
    right_block = regroup(right_two, row_count, col_count)
    triangle = jnp.einsum(
        "ikc,jkc->ijc",
        left_full,
        lax.all_gather(right_block, "row", axis=1, tiled=True),
        preferred_element_type=jnp.float32,
    )
    mid = normalize(triangle, mid_gain, mid_shift).astype(jnp.bfloat16)
    update = (
        jnp.dot(
            mid.reshape(row_total * column_total, hidden),
            out_weight,
            preferred_element_type=jnp.float32,
        )
        + out_bias
    )
    updated = (pair_wide + (out_gate * update).reshape(row_total, column_total, width)).astype(
        jnp.bfloat16
    )
    moved_one = lax.all_to_all(updated, "col", split_axis=0, concat_axis=1, tiled=True)
    moved_two = lax.all_to_all(
        lax.all_to_all(moved_one, "row", split_axis=1, concat_axis=0, tiled=True),
        "col",
        split_axis=0,
        concat_axis=0,
        tiled=True,
    )
    mirrored = regroup(moved_two, row_count, col_count)
    symmetric = (
        (updated.astype(jnp.float32) + jnp.transpose(mirrored, (1, 0, 2)).astype(jnp.float32)) * 0.5
    ).astype(jnp.bfloat16)
    symmetric_wide = symmetric.astype(jnp.float32)
    first_input = jax.nn.relu(normalize(symmetric_wide, conv_gain[0], conv_shift[0])).astype(
        jnp.bfloat16
    )
    first_padded = padded(first_input, (("row", 0), ("col", 1)), FIRST_DILATION)
    first_result = (
        symmetric_wide
        + convolution_bias[0]
        + dilated_output(
            first_padded, convolution_weight[0], FIRST_DILATION, row_total, column_total
        )
    )
    second_input = jax.nn.relu(normalize(first_result, conv_gain[1], conv_shift[1])).astype(
        jnp.bfloat16
    )
    second_padded = padded(second_input, (("row", 0), ("col", 1)), SECOND_DILATION)
    refined = (
        first_result
        + convolution_bias[1]
        + dilated_output(
            second_padded, convolution_weight[1], SECOND_DILATION, row_total, column_total
        )
    ).astype(jnp.bfloat16)
    return refined


def solution(mesh):
    return jax.shard_map(
        local,
        mesh=mesh,
        in_specs=(
            P("row", "col", None),
            P(),
            P(),
            P(),
            P(),
            P(),
            P(),
            P(),
            P(),
            P(),
            P(),
            P(),
            P(),
        ),
        out_specs=P("row", "col", None),
        check_vma=False,
    )
```

profile of v0, /device:TPU:25, one launch (start us, length us, event | category | flops | bytes accessed | tf_op | source)
XLA Modules:
  0.0 487.2 jit_solution(7749120533275714769)
XLA Ops:
  6.6 2.4 convert_reduce_fusion.1
  9.0 3.6 fusion.12
  12.6 2.5 fusion.15
  15.1 1.8 convolution_add_fusion
  17.0 4.5 copy-done.2
  21.5 1.1 fusion.34
  22.6 1.3 copy.65
  24.3 26.4 %all_to_all.82 = bf16[64,128,64]{1,2,0:T(8,128)(2,1)S(1)} all-to-all(bf16[64,128,64]{1,2,0:T(8,128)(2,1)S(1)} %bitcast.206), channel_id=1, replica_groups=mesh['row'=16,'col'=8] {'col'}, dimensions={0} | all-to-all | bytes 2097152 | tf_op jit(solution)/shard_map/all_to_all | solution.py:100
  50.7 2.0 copy.60
  52.7 3.9 reshape.212
  56.6 25.0 %all_to_all.83 = bf16[16,2,16384]{2,1,0:T(2,128)(2,1)} all-to-all(bf16[16,2,16384]{2,1,0:T(2,128)(2,1)S(1)} %reshape.212), channel_id=1, replica_groups=mesh['row'=16,'col'=8] {'row'}, dimensions={0} | all-to-all | bytes 2097152 | tf_op jit(solution)/shard_map/all_to_all | solution.py:102
  81.6 4.7 reshape.213
  86.3 3.5 copy.48
  89.8 3.4 reshape.214
  93.2 41.3 %all_to_all.84 = bf16[8,2,32768]{2,1,0:T(2,128)(2,1)} all-to-all(bf16[8,2,32768]{2,1,0:T(2,128)(2,1)S(1)} %reshape.214), channel_id=1, replica_groups=mesh['row'=16,'col'=8] {'col'}, dimensions={0} | all-to-all | bytes 2097152 | tf_op jit(solution)/shard_map/all_to_all | solution.py:101
  134.5 4.3 reshape.215
  138.7 3.2 copy.49
  141.9 5.2 %copy.50 = bf16[128,64,64]{0,1,2:T(8,128)(2,1)} copy(bf16[128,64,64]{2,1,0:T(8,128)(2,1)} %bitcast.200) | data formatting | bytes 2097152 | tf_op jit(solution)/shard_map/reshape | solution.py:38
  147.2 3.8 all-gather.5.cloned.1.call-done
  151.0 115.4 %all-gather.3.cloned.1.call-done = bf16[128,1024,64]{0,1,2:T(8,128)(2,1)} async-done(((bf16[128,64,64]{0,1,2:T(8,128)(2,1)}), bf16[128,1024,64]{0,1,2:T(8,128)(2,1)}) %all-gather.3.cloned.1.call-update) | async-done | bytes 16777232 | tf_op jit(solution)/shard_map/all_gather | solution.py:112
  266.4 11.2 %bitcast_reduce_fusion = (f32[64,128]{1,0:T(8,128)S(1)}, f32[64,128,64]{1,2,0:T(8,128)S(1)}) fusion(bf16[64,1024,64]{1,0,2:T(8,128)(2,1)} %all-gather.5.cloned.1.call-done, bf16[128,1024,64]{0,1,2:T(8,128)(2,1)} %all-gather.3.cloned.1.call-done), kind=kOutput, calls=%fused_computation.72 | convolution fusion | flops 1074257920 | bytes 27295744 | tf_op jit(solution)/shard_map/ikc,jkc->ijc/dot_general | solution.py:109
  278.4 5.8 %fusion.2 = f32[8192,128]{0,1:T(8,128)} fusion(bf16[64,128]{1,0:T(8,128)(2,1)S(1)} %copy-done.16, f32[8192,384]{0,1:T(8,128)} %copy-done.2, f32[128]{0:T(128)S(1)} %copy-done.17, bf16[8,8,64,128]{3,2,1,0:T(8,128)(2,1)S(1)} %bitcast.207), kind=kOutput, calls=%fused_computation.18 | convolution fusion | flops 139460608 | bytes 9454080 | tf_op jit(solution)/shard_map/dot_general | solution.py:117
  284.2 5.7 %copy.61 = f32[8192,128]{1,0:T(8,128)} copy(f32[8192,128]{0,1:T(8,128)} %fusion.2) | data formatting | bytes 8388608 | tf_op jit(solution)/shard_map/reshape | solution.py:124
  289.9 2.8 fusion.16
  292.8 30.0 %all_to_all.85 = bf16[64,128,128]{2,1,0:T(8,128)(2,1)S(1)} all-to-all(bf16[64,128,128]{2,1,0:T(8,128)(2,1)S(1)} %fusion.16), channel_id=1, replica_groups=mesh['row'=16,'col'=8] {'col'}, dimensions={0} | all-to-all | bytes 4194304 | tf_op jit(solution)/shard_map/all_to_all | solution.py:127
  322.9 1.4 copy.54
  324.3 33.2 %all_to_all.86 = bf16[8,1024,128]{2,0,1:T(8,128)(2,1)S(1)} all-to-all(bf16[8,1024,128]{2,0,1:T(8,128)(2,1)S(1)} %copy.54), channel_id=1, replica_groups=mesh['row'=16,'col'=8] {'row'}, dimensions={1} | all-to-all | bytes 4194304 | tf_op jit(solution)/shard_map/all_to_all | solution.py:129
  357.5 1.9 copy.56
  359.4 4.6 all-to-all-start.5
  364.0 26.0 %all-to-all-done.5 = bf16[128,64,128]{2,1,0:T(8,128)(2,1)S(1)} async-done(((bf16[128,64,128]{2,1,0:T(8,128)(2,1)}), bf16[128,64,128]{2,1,0:T(8,128)(2,1)S(1)}, u32[]{:S(2)}, u32[]{:S(2)}) %all-to-all-start.5) | async-done | bytes 2097184 | tf_op jit(solution)/shard_map/all_to_all | solution.py:128
  390.8 1.3 copy-done.5
  392.1 2.8 convert_reduce_fusion
  394.9 2.4 fusion.7
  397.3 2.5 fusion.11
  399.8 4.8 collective-permute-start
  404.6 1.9 collective-permute-start.1
  406.6 6.0 %collective-permute-done.1 = bf16[2,128,128]{2,1,0:T(8,128)(2,1)S(1)} collective-permute-done((bf16[2,128,128]{2,1,0:T(8,128)(2,1)S(1)}, bf16[2,128,128]{2,1,0:T(8,128)(2,1)S(1)}, u32[]{:S(2)}, u32[]{:S(2)}) %collective-permute-start.1) | collective-permute-done | bytes 65568 | tf_op jit(solution)/shard_map/ppermute | solution.py:21
  412.7 2.5 collective-permute-start.2
  415.1 5.3 %collective-permute-start.3 = (bf16[68,2,128]{2,1,0:T(2,128)(2,1)S(1)}, bf16[68,2,128]{2,1,0:T(2,128)(2,1)S(1)}, u32[]{:S(2)}, u32[]{:S(2)}) collective-permute-start(bf16[68,2,128]{2,1,0:T(2,128)(2,1)S(1)} %get-tuple-element.28), channel_id=1, source_target_pairs={{1,0},{2,1},{3,2},{4,3},{5,4},{6,5},{7,6},{9,8},{10,9},{11,10},{12... | collective-permute-start | bytes 104456 | tf_op jit(solution)/shard_map/ppermute | solution.py:21
  421.5 3.2 maximum_maximum_fusion.1
  424.7 1.6 fusion.79
  426.3 1.2 fusion.80
  428.2 0.7 convolution_add_fusion.14
  428.9 0.7 convolution_add_fusion.13
  432.4 0.8 fusion.1
  433.2 1.2 fusion.75
  434.5 2.6 multiply_reduce_fusion
  437.1 2.5 maximum_convert_fusion
  439.7 2.6 collective-permute-start.4
  442.3 2.1 collective-permute-start.5
  444.4 6.6 %collective-permute-done.5 = bf16[4,128,128]{2,1,0:T(8,128)(2,1)S(1)} collective-permute-done((bf16[4,128,128]{2,1,0:T(8,128)(2,1)S(1)}, bf16[4,128,128]{2,1,0:T(8,128)(2,1)S(1)}, u32[]{:S(2)}, u32[]{:S(2)}) %collective-permute-start.5) | collective-permute-done | bytes 131104 | tf_op jit(solution)/shard_map/ppermute | solution.py:21
  451.1 1.9 collective-permute-start.6
  453.0 5.5 %collective-permute-start.7 = (bf16[72,4,128]{2,1,0:T(4,128)(2,1)S(1)}, bf16[72,4,128]{2,1,0:T(4,128)(2,1)S(1)}, u32[]{:S(2)}, u32[]{:S(2)}) collective-permute-start(bf16[72,4,128]{2,1,0:T(4,128)(2,1)S(1)} %get-tuple-element.24), channel_id=1, source_target_pairs={{1,0},{2,1},{3,2},{4,3},{5,4},{6,5},{7,6},{9,8},{10,9},{11,10},{12... | collective-permute-start | bytes 221192 | tf_op jit(solution)/shard_map/ppermute | solution.py:21
  458.5 1.7 pad_maximum_fusion.2
  461.0 3.8 maximum_maximum_fusion
  464.7 1.6 fusion.77
  466.4 3.1 fusion.78
  469.4 2.3 fusion.35
  472.4 0.7 convolution_add_fusion.6
  473.8 0.7 convolution_add_fusion.4
  474.5 0.7 convolution_add_fusion.3
  475.9 0.9 copy-done.6
  476.8 0.8 fusion
  477.6 2.5 add_convert_fusion
  (74 shorter events, 9.4 us)
Async XLA Ops:
  6.5 8.6 %copy-start = (bf16[128,384]{1,0:T(8,128)(2,1)S(1)}, bf16[128,384]{1,0:T(8,128)(2,1)}, u32[]{:S(2)}) copy-start(bf16[128,384]{1,0:T(8,128)(2,1)} %param.16) | copy-start | bytes 294916
  6.5 6.0 %copy-start.3 = (bf16[64,128,128]{2,1,0:T(8,128)(2,1)S(1)}, bf16[64,128,128]{2,1,0:T(8,128)(2,1)}, u32[]{:S(2)}) copy-start(bf16[64,128,128]{2,1,0:T(8,128)(2,1)} %param.13) | copy-start | bytes 6291460
  6.5 6.1 %copy-start.13 = (f32[128]{0:T(128)S(1)}, f32[128]{0:T(128)}, u32[]{:S(2)}) copy-start(f32[128]{0:T(128)} %param.14) | copy-start | bytes 1540
  6.5 6.1 %copy-start.12 = (f32[128]{0:T(128)S(1)}, f32[128]{0:T(128)}, u32[]{:S(2)}) copy-start(f32[128]{0:T(128)} %param.15) | copy-start | bytes 1540
  6.5 8.6 %copy-start.8 = (f32[384]{0:T(512)S(1)}, f32[384]{0:T(512)}, u32[]{:S(2)}) copy-start(f32[384]{0:T(512)} %param.17) | copy-start | bytes 4612
  6.5 144.5 %all-gather.5.cloned.1.call-start = ((), (), s32[]{:S(2)}) async-start(), calls=%async_computation.7 | async-start | bytes 9437184 | tf_op jit(solution)/shard_map/all_gather | solution.py:99
  17.0 4.5 copy-start.2
  23.9 242.5 %all-gather.3.cloned.1.call-start = ((), (), s32[]{:S(2)}) async-start(), calls=%async_computation.6 | async-start | bytes 17825792 | tf_op jit(solution)/shard_map/all_gather | solution.py:112
  147.2 130.8 %copy-start.14 = (f32[64]{0:T(128)S(1)}, f32[64]{0:T(128)}, u32[]{:S(2)}) copy-start(f32[64]{0:T(128)} %param.19) | copy-start | bytes 772
  147.2 130.8 %copy-start.15 = (f32[64]{0:T(128)S(1)}, f32[64]{0:T(128)}, u32[]{:S(2)}) copy-start(f32[64]{0:T(128)} %param.18) | copy-start | bytes 772
  277.7 0.8 copy-start.16
  277.7 0.8 copy-start.17
  292.8 30.1 %copy-start.4 = (bf16[64,128,128]{2,1,0:T(8,128)(2,1)}, bf16[64,128,128]{2,1,0:T(8,128)(2,1)S(1)}, u32[]{:S(2)}) copy-start(bf16[64,128,128]{2,1,0:T(8,128)(2,1)S(1)} %fusion.16) | copy-start | bytes 6291460
  357.5 6.6 %copy-start.10 = (f32[2,128]{1,0:T(2,128)S(1)}, f32[2,128]{1,0:T(2,128)}, u32[]{:S(2)}) copy-start(f32[2,128]{1,0:T(2,128)} %param.23) | copy-start | bytes 3076
  357.5 6.6 %copy-start.11 = (f32[2,128]{1,0:T(2,128)S(1)}, f32[2,128]{1,0:T(2,128)}, u32[]{:S(2)}) copy-start(f32[2,128]{1,0:T(2,128)} %param.22) | copy-start | bytes 3076
  359.4 30.6 %all-to-all-start.5 = ((bf16[128,64,128]{2,1,0:T(8,128)(2,1)}), bf16[128,64,128]{2,1,0:T(8,128)(2,1)S(1)}, u32[]{:S(2)}, u32[]{:S(2)}) async-start(bf16[128,64,128]{2,1,0:T(8,128)(2,1)} %bitcast.196), calls=%async_computation.5 | async-start | bytes 4194304 | tf_op jit(solution)/shard_map/all_to_all | solution.py:128
  390.5 1.6 copy-start.5
  394.8 11.7 %copy-start.9 = (f32[2,128]{1,0:T(2,128)S(1)}, f32[2,128]{1,0:T(2,128)}, u32[]{:S(2)}) copy-start(f32[2,128]{1,0:T(2,128)} %param.25) | copy-start | bytes 3076
  399.8 6.8 %collective-permute-start = (bf16[2,128,128]{2,1,0:T(8,128)(2,1)S(1)}, bf16[2,128,128]{2,1,0:T(8,128)(2,1)S(1)}, u32[]{:S(2)}, u32[]{:S(2)}) collective-permute-start(bf16[2,128,128]{2,1,0:T(8,128)(2,1)S(1)} %get-tuple-element.35), channel_id=1, source_target_pairs={{0,8},{8,16},{16,24},{24,32},{32,40},{40,48},{48,56},{56,64},{64,7... | collective-permute-start | bytes 196616 | tf_op jit(solution)/shard_map/ppermute | solution.py:18
  404.6 8.0 %collective-permute-start.1 = (bf16[2,128,128]{2,1,0:T(8,128)(2,1)S(1)}, bf16[2,128,128]{2,1,0:T(8,128)(2,1)S(1)}, u32[]{:S(2)}, u32[]{:S(2)}) collective-permute-start(bf16[2,128,128]{2,1,0:T(8,128)(2,1)S(1)} %get-tuple-element.36), channel_id=1, source_target_pairs={{8,0},{16,8},{24,16},{32,24},{40,32},{48,40},{56,48},{64,56},{72,6... | collective-permute-start | bytes 196616 | tf_op jit(solution)/shard_map/ppermute | solution.py:21
  406.6 14.2 %copy-start.7 = (bf16[2,9,128,128]{3,2,1,0:T(8,128)(2,1)S(1)}, bf16[2,9,128,128]{3,2,1,0:T(8,128)(2,1)}, u32[]{:S(2)}) copy-start(bf16[2,9,128,128]{3,2,1,0:T(8,128)(2,1)} %param.24) | copy-start | bytes 1769476
  412.7 8.8 %collective-permute-start.2 = (bf16[68,2,128]{2,1,0:T(2,128)(2,1)S(1)}, bf16[68,2,128]{2,1,0:T(2,128)(2,1)S(1)}, u32[]{:S(2)}, u32[]{:S(2)}) collective-permute-start(bf16[68,2,128]{2,1,0:T(2,128)(2,1)S(1)} %get-tuple-element.27), channel_id=1, source_target_pairs={{0,1},{1,2},{2,3},{3,4},{4,5},{5,6},{6,7},{8,9},{9,10},{10,11},{11... | collective-permute-start | bytes 104456 | tf_op jit(solution)/shard_map/ppermute | solution.py:18
  415.1 6.3 %collective-permute-start.3 = (bf16[68,2,128]{2,1,0:T(2,128)(2,1)S(1)}, bf16[68,2,128]{2,1,0:T(2,128)(2,1)S(1)}, u32[]{:S(2)}, u32[]{:S(2)}) collective-permute-start(bf16[68,2,128]{2,1,0:T(2,128)(2,1)S(1)} %get-tuple-element.28), channel_id=1, source_target_pairs={{1,0},{2,1},{3,2},{4,3},{5,4},{6,5},{7,6},{9,8},{10,9},{11,10},{12... | collective-permute-start | bytes 104456 | tf_op jit(solution)/shard_map/ppermute | solution.py:21
  439.7 4.7 collective-permute-start.4
  442.3 8.7 %collective-permute-start.5 = (bf16[4,128,128]{2,1,0:T(8,128)(2,1)S(1)}, bf16[4,128,128]{2,1,0:T(8,128)(2,1)S(1)}, u32[]{:S(2)}, u32[]{:S(2)}) collective-permute-start(bf16[4,128,128]{2,1,0:T(8,128)(2,1)S(1)} %get-tuple-element.32), channel_id=1, source_target_pairs={{8,0},{16,8},{24,16},{32,24},{40,32},{48,40},{56,48},{64,56},{72,6... | collective-permute-start | bytes 393224 | tf_op jit(solution)/shard_map/ppermute | solution.py:21
  451.1 9.9 %collective-permute-start.6 = (bf16[72,4,128]{2,1,0:T(4,128)(2,1)S(1)}, bf16[72,4,128]{2,1,0:T(4,128)(2,1)S(1)}, u32[]{:S(2)}, u32[]{:S(2)}) collective-permute-start(bf16[72,4,128]{2,1,0:T(4,128)(2,1)S(1)} %get-tuple-element.23), channel_id=1, source_target_pairs={{0,1},{1,2},{2,3},{3,4},{4,5},{5,6},{6,7},{8,9},{9,10},{10,11},{11... | collective-permute-start | bytes 221192 | tf_op jit(solution)/shard_map/ppermute | solution.py:18
  453.0 8.0 %collective-permute-start.7 = (bf16[72,4,128]{2,1,0:T(4,128)(2,1)S(1)}, bf16[72,4,128]{2,1,0:T(4,128)(2,1)S(1)}, u32[]{:S(2)}, u32[]{:S(2)}) collective-permute-start(bf16[72,4,128]{2,1,0:T(4,128)(2,1)S(1)} %get-tuple-element.24), channel_id=1, source_target_pairs={{1,0},{2,1},{3,2},{4,3},{5,4},{6,5},{7,6},{9,8},{10,9},{11,10},{12... | collective-permute-start | bytes 221192 | tf_op jit(solution)/shard_map/ppermute | solution.py:21
  475.2 1.6 copy-start.6
  477.6 2.5 copy-start.1
Sparse Core Ops, SparseCore 0:
  24.0 126.9 all-gather.4
  153.5 112.9 all-gather.2
where the time goes:
time: 496 us; the launch traced here: 487 us
  waiting for transfers between devices  158 us (32%)
  blocking collectives  156 us (31%)
  local copies, waits for them, and re-layouts  55.4 us (11%)
  other arithmetic  39.1 us (8%)
  matrix products  33.1 us (7%)
  starting transfers between devices  31.4 us (6%)
  between operations  14.3 us (3%)
    all_gather x1, waiting for transfers between devices, local(): lax.all_gather(right_block, 'row', axis=1, tiled=True)  115 us
    all_to_all x1, blocking collectives, local(): lax.all_to_all(lax.all_to_all(right_one, 'row', split_axis=1, concat_axis...  41.3 us
    all_to_all x1, blocking collectives, local(): lax.all_to_all(moved_one, 'row', split_axis=1, concat_axis=0, tiled=True)  33.2 us
    all_to_all x1, blocking collectives, local(): lax.all_to_all(updated, 'col', split_axis=0, concat_axis=1, tiled=True)  30 us
    all_to_all x1, blocking collectives, local(): lax.all_to_all(right, 'col', split_axis=0, concat_axis=1, tiled=True)  26.4 us
    all_to_all x1, waiting for transfers between devices, local(): lax.all_to_all(lax.all_to_all(moved_one, 'row', split_axis=1, concat_axis...  26 us
    all_to_all x1, blocking collectives, local(): lax.all_to_all(right_one, 'row', split_axis=1, concat_axis=0, tiled=True)  25 us
    unnamed x41, local copies, waits for them, and re-layouts  24.2 us
  transfers between devices with their start and end apart: 11, of which 5 were waited for; matrix products, arithmetic and copies ran while one was open for 7% of the time, Pallas kernels for 0%

commit v1 on v0

v1 whole, which is shorter than its diff:
```python
import jax
import jax.numpy as jnp
from jax import lax
from jax.experimental import pallas as pl
from jax.experimental.pallas import tpu as pltpu
from jax.sharding import PartitionSpec as P

FIRST_DILATION = 2
SECOND_DILATION = 4
HALO = FIRST_DILATION + SECOND_DILATION
EPS = 1e-05
BF = jnp.bfloat16
F32 = jnp.float32
MIB = 1 << 20
ROWS, COLS, CH, HID = 64, 128, 128, 64
NR, NC = 16, 8


def sigmoid(x):
    return 0.5 * jnp.tanh(0.5 * x) + 0.5


def normalize(values, gain, shift):
    mean = jnp.mean(values, axis=-1, keepdims=True)
    centred = values - mean
    spread = jnp.mean(centred * centred, axis=-1, keepdims=True)
    return centred * lax.rsqrt(spread + EPS) * gain + shift


NT = (((1,), (1,)), ((), ()))
TN = (((0,), (0,)), ((), ()))

STEP = 16


def factor_kernel(pair_ref, gain_ref, shift_ref, weight_ref, bias_ref, out_ref, lay_ref):
    step = pl.program_id(0)
    block = pair_ref[...]
    cells = block.astype(F32).reshape(STEP * COLS, CH)
    normed = normalize(cells, gain_ref[...], shift_ref[...]).astype(BF)
    projected = (
        lax.dot_general(weight_ref[...], normed, NT, preferred_element_type=F32) + bias_ref[...]
    )
    start = pl.multiple_of(step * STEP, STEP)
    for side in range(2):
        base = 2 * HID * side
        factor = sigmoid(projected[base : base + HID]) * projected[base + HID : base + 2 * HID]
        for row in range(STEP):
            lay_ref[pl.ds(row, HID, stride=STEP), :] = factor[:, row * COLS : (row + 1) * COLS]
        out_ref[:, side, :, 0, pl.ds(start, STEP), :] = (
            lay_ref[...].astype(BF).reshape(8, 8, STEP, COLS)
        )
    for row in range(STEP):
        for q in range(2):
            local = 2 * row + q
            group = step * 2 + local // 16
            side = (local // 8) % 2
            column = local % 8
            for half in range(2):
                out_ref[group, side, column, 1, half * 32 : half * 32 + 32, :] = pair_ref[
                    row, half * 64 + q * 32 : half * 64 + q * 32 + 32, :
                ]


def factors(pair, gain, shift, weight_t, bias_t):
    whole = lambda *shape: pl.BlockSpec(shape, lambda s: (0,) * len(shape))
    return pl.pallas_call(
        factor_kernel,
        grid=(ROWS // STEP,),
        out_shape=jax.ShapeDtypeStruct((8, 2, 8, 2, ROWS, COLS), BF),
        in_specs=[
            pl.BlockSpec((STEP, COLS, CH), lambda s: (s, 0, 0)),
            whole(1, CH),
            whole(1, CH),
            whole(4 * HID, CH),
            whole(4 * HID, 1),
        ],
        out_specs=whole(8, 2, 8, 2, ROWS, COLS),
        scratch_shapes=[pltpu.VMEM((HID * STEP, COLS), F32)],
        compiler_params=pltpu.CompilerParams(vmem_limit_bytes=40 * MIB),
        name="factors",
    )(pair, gain, shift, weight_t, bias_t)


def product_kernel(own_ref, moved_ref, other_ref, out_ref, rhs_ref):
    for col in range(NC):
        rhs_ref[:, col * COLS : (col + 1) * COLS] = other_ref[:, col].reshape(NR * ROWS, COLS)
    half = NR // 2
    for part in range(2):
        lhs = jnp.concatenate(
            [
                own_ref[part * half : (part + 1) * half, col, 0].reshape(half * ROWS, COLS)
                for col in range(NC)
            ],
            axis=1,
        )
        for block in range(4):
            result = lax.dot_general(
                lhs,
                rhs_ref[block * 256 : (block + 1) * 256, :],
                NT,
                preferred_element_type=F32,
            ).astype(BF)
            for col in range(2):
                out_ref[part * half : (part + 1) * half, block * 2 + col, 0] = result[
                    :, col * COLS : (col + 1) * COLS
                ].reshape(half, ROWS, COLS)
    for row in range(NR):
        for col in range(NC):
            side = row % 2
            for e in range(2):
                out_ref[row, col, 1, e * 32 : e * 32 + 32, :] = moved_ref[
                    2 * col + e, row // 2, 0, side * 32 : side * 32 + 32, :
                ]


def product(received, other):
    whole = lambda *shape: pl.BlockSpec(shape, lambda s: (0,) * len(shape))
    slot = lambda k: pl.BlockSpec((NR, NC, 1, ROWS, COLS), lambda s: (0, 0, k, 0, 0))
    return pl.pallas_call(
        product_kernel,
        grid=(1,),
        out_shape=jax.ShapeDtypeStruct((NR, NC, 2, ROWS, COLS), BF),
        in_specs=[slot(0), slot(1), whole(NR, NC, ROWS, COLS)],
        out_specs=whole(NR, NC, 2, ROWS, COLS),
        scratch_shapes=[pltpu.VMEM((NR * ROWS, NC * COLS), BF)],
        compiler_params=pltpu.CompilerParams(vmem_limit_bytes=48 * MIB),
        name="product",
    )(received, received, other)


def channel_normalize(values, gain, shift):
    mean = jnp.mean(values, axis=0, keepdims=True)
    centred = values - mean
    spread = jnp.mean(centred * centred, axis=0, keepdims=True)
    return centred * lax.rsqrt(spread + EPS) * gain + shift


USTEP = 16


def update_kernel(
    pair_ref, tri_ref, mirror_ref, gain_ref, shift_ref, gate_ref, gate_bias_ref,
    mid_gain_ref, mid_shift_ref, out_weight_ref, out_bias_ref, sym_ref, cells_ref, lay_ref,
):
    step = pl.program_id(0)

    @pl.when(step == 0)
    def _():
        for d in range(128):
            for e in range(2):
                at = (e * 64 + d // 2) * 64 + (d % 2) * 32
                cells_ref[at : at + 32, :] = mirror_ref[d, 0, e * 32 : e * 32 + 32, :].astype(F32)

    def gated(cells, side, row):
        normed = normalize(cells, gain_ref[...], shift_ref[...]).astype(BF)
        gate = sigmoid(
            jnp.dot(normed, gate_ref[...], preferred_element_type=F32) + gate_bias_ref[...]
        )
        mid = lay_ref[side, pl.ds(row, HID, stride=USTEP), :].astype(BF)
        change = (
            lax.dot_general(mid, out_weight_ref[...], TN, preferred_element_type=F32)
            + out_bias_ref[...]
        )
        return (cells + gate * change).astype(BF).astype(F32)

    for side in range(2):
        tri = tri_ref[:, side, :, 0].astype(F32).reshape(HID, USTEP, COLS)
        mid = channel_normalize(tri, mid_gain_ref[...], mid_shift_ref[...])
        lay_ref[side] = mid.reshape(HID * USTEP, COLS)

    def body(row, carry):
        own = gated(pair_ref[row].astype(F32), 0, row)
        mirrored = gated(cells_ref[pl.ds(step * USTEP + row, COLS, stride=ROWS), :], 1, row)
        sym_ref[row] = ((own + mirrored) * 0.5).astype(BF)
        return carry

    lax.fori_loop(0, USTEP, body, 0, unroll=4)


def update(pair, received, gain, shift, gate, gate_bias, mid_gain, mid_shift, out_weight, out_bias):
    whole = lambda *shape: pl.BlockSpec(shape, lambda s: (0,) * len(shape))
    tri = received.reshape(8, 2, 8, 2, ROWS, COLS)
    cells = received.reshape(128, 2, ROWS, COLS)
    return pl.pallas_call(
        update_kernel,
        grid=(ROWS // USTEP,),
        out_shape=jax.ShapeDtypeStruct((ROWS, COLS, CH), BF),
        in_specs=[
            pl.BlockSpec((USTEP, COLS, CH), lambda s: (s, 0, 0)),
            pl.BlockSpec((8, 2, 8, 1, USTEP, COLS), lambda s: (0, 0, 0, 0, s, 0)),
            pl.BlockSpec((128, 1, ROWS, COLS), lambda s: (0, 1, 0, 0)),
            whole(1, CH),
            whole(1, CH),
            whole(CH, CH),
            whole(1, CH),
            whole(HID, 1, 1),
            whole(HID, 1, 1),
            whole(HID, CH),
            whole(1, CH),
        ],
        out_specs=pl.BlockSpec((USTEP, COLS, CH), lambda s: (s, 0, 0)),
        scratch_shapes=[
            pltpu.VMEM((COLS * ROWS, CH), F32),
            pltpu.VMEM((2, HID * USTEP, COLS), F32),
        ],
        compiler_params=pltpu.CompilerParams(vmem_limit_bytes=48 * MIB),
        name="update",
    )(pair, tri, cells, gain, shift, gate, gate_bias, mid_gain, mid_shift, out_weight, out_bias)


TALL = ROWS + 2 * HALO
WIDE = 160
FIRST_TALL = ROWS + 2 * SECOND_DILATION
FIRST_WIDE = 144


def convolution_kernel(
    place_ref, sym_ref, top_ref, bottom_ref, low_ref, high_ref, gain_ref, shift_ref, bias_ref,
    weight_ref, out_ref, wide_ref, act_ref, cols_ref, first_ref, second_ref, second_cols_ref,
):
    row_at, col_at = place_ref[0], place_ref[1]

    def fill(row, carry):
        def put(centre):
            wide_ref[row, 0:16, :] = jnp.zeros((16, CH), F32)
            wide_ref[row, 144:160, :] = jnp.zeros((16, CH), F32)
            wide_ref[row, 16:144, :] = centre.astype(F32)
            wide_ref[row, 10:16, :] = low_ref[row].astype(F32)
            wide_ref[row, 144:150, :] = high_ref[row].astype(F32)

        @pl.when(row < HALO)
        def _():
            put(top_ref[row])

        @pl.when((row >= HALO) & (row < HALO + ROWS))
        def _():
            put(sym_ref[row - HALO])

        @pl.when(row >= HALO + ROWS)
        def _():
            put(bottom_ref[row - HALO - ROWS])

        act = jnp.maximum(
            normalize(wide_ref[row], gain_ref[0:1], shift_ref[0:1]), 0.0
        )
        column = lax.broadcasted_iota(jnp.int32, (WIDE, CH), 0) + (col_at - 16)
        inside_row = (row + row_at >= HALO) & (row + row_at < HALO + NR * ROWS)
        inside = (column >= 0) & (column < NC * COLS) & inside_row
        act_ref[...] = jnp.where(inside, act, 0.0)
        for tap in range(3):
            cols_ref[row, :, tap * CH : (tap + 1) * CH] = act_ref[
                6 + 2 * tap : 6 + 2 * tap + FIRST_WIDE, :
            ].astype(BF)
        return carry

    lax.fori_loop(0, TALL, fill, 0)

    group = 8

    def convolve_first(step, carry):
        at = step * group
        total = jnp.zeros((group * FIRST_WIDE, CH), F32)
        for tap in range(3):
            total = total + jnp.dot(
                cols_ref[pl.ds(at + 2 * tap, group)].reshape(group * FIRST_WIDE, 3 * CH),
                weight_ref[0, tap],
                preferred_element_type=F32,
            )
        first = (
            total.reshape(group, FIRST_WIDE, CH)
            + wide_ref[pl.ds(at + 2, group), 8:152, :]
            + bias_ref[0:1].reshape(1, 1, CH)
        )
        first_ref[pl.ds(at, group)] = first[:, 8:136]
        act = jnp.maximum(
            normalize(
                first, gain_ref[1:2].reshape(1, 1, CH), shift_ref[1:2].reshape(1, 1, CH)
            ),
            0.0,
        )
        row = lax.broadcasted_iota(jnp.int32, (group, FIRST_WIDE, CH), 0) + (row_at + at - 4)
        column = lax.broadcasted_iota(jnp.int32, (group, FIRST_WIDE, CH), 1) + (col_at - 8)
        inside = (row >= 0) & (row < NR * ROWS) & (column >= 0) & (column < NC * COLS)
        second_ref[...] = jnp.where(inside, act, 0.0)
        for tap in range(3):
            second_cols_ref[pl.ds(at, group), :, tap * CH : (tap + 1) * CH] = second_ref[
                :, 4 + 4 * tap : 4 + 4 * tap + COLS, :
            ].astype(BF)
        return carry

    lax.fori_loop(0, FIRST_TALL // group, convolve_first, 0)

    def convolve_second(step, carry):
        at = step * group
        total = jnp.zeros((group * COLS, CH), F32)
        for tap in range(3):
            total = total + jnp.dot(
                second_cols_ref[pl.ds(at + 4 * tap, group)].reshape(group * COLS, 3 * CH),
                weight_ref[1, tap],
                preferred_element_type=F32,
            )
        out_ref[pl.ds(at, group)] = (
            total.reshape(group, COLS, CH)
            + first_ref[pl.ds(at + 4, group)]
            + bias_ref[1:2].reshape(1, 1, CH)
        ).astype(BF)
        return carry

    lax.fori_loop(0, ROWS // group, convolve_second, 0)


def convolutions(place, sym, top, bottom, low, high, gain, shift, bias, weight):
    vmem = pl.BlockSpec(memory_space=pltpu.VMEM)
    return pl.pallas_call(
        convolution_kernel,
        out_shape=jax.ShapeDtypeStruct((ROWS, COLS, CH), BF),
        in_specs=[pl.BlockSpec(memory_space=pltpu.SMEM)] + [vmem] * 9,
        out_specs=vmem,
        scratch_shapes=[
            pltpu.VMEM((TALL, WIDE, CH), F32),
            pltpu.VMEM((WIDE, CH), F32),
            pltpu.VMEM((TALL, FIRST_WIDE, 3 * CH), BF),
            pltpu.VMEM((FIRST_TALL, COLS, CH), F32),
            pltpu.VMEM((8, FIRST_WIDE, CH), F32),
            pltpu.VMEM((FIRST_TALL, COLS, 3 * CH), BF),
        ],
        compiler_params=pltpu.CompilerParams(vmem_limit_bytes=56 * MIB),
        name="convolutions",
    )(place, sym, top, bottom, low, high, gain, shift, bias, weight)


def neighbours(low_strip, high_strip, axis):
    count = lax.axis_size(axis)
    forward = [(i, i + 1) for i in range(count - 1)]
    backward = [(i + 1, i) for i in range(count - 1)]
    return lax.ppermute(high_strip, axis, forward), lax.ppermute(low_strip, axis, backward)


def local(
    pair, norm_gain, norm_shift, proj_weight, proj_bias, mid_gain, mid_shift, out_weight, out_bias,
    conv_gain, conv_shift, convolution_weight, convolution_bias,
):
    gain, shift = norm_gain[None], norm_shift[None]
    sent = factors(
        pair, gain, shift, proj_weight[:, : 4 * HID].T, proj_bias[: 4 * HID, None]
    )
    received = lax.all_to_all(
        sent.reshape(128, 2, ROWS, COLS), ("row", "col"), split_axis=0, concat_axis=0, tiled=True
    ).reshape(NR, NC, 2, ROWS, COLS)
    other = lax.ppermute(received[:, :, 0], "row", [(i, i ^ 1) for i in range(NR)])
    back = product(received, other)
    returned = lax.all_to_all(
        back.reshape(128, 2, ROWS, COLS), ("row", "col"), split_axis=0, concat_axis=0, tiled=True
    )
    sym = update(
        pair, returned, gain, shift, proj_weight[:, 4 * HID :], proj_bias[None, 4 * HID :],
        mid_gain[:, None, None], mid_shift[:, None, None], out_weight, out_bias[None],
    )
    top, bottom = neighbours(sym[:HALO], sym[ROWS - HALO :], "row")
    edge = lambda low, high: jnp.concatenate(
        [top[:, low:high], sym[:, low:high], bottom[:, low:high]], axis=0
    )
    low, high = neighbours(edge(0, HALO), edge(COLS - HALO, COLS), "col")
    place = jnp.stack([lax.axis_index("row") * ROWS, lax.axis_index("col") * COLS]).astype(jnp.int32)
    return convolutions(
        place, sym, top, bottom, low, high, conv_gain, conv_shift, convolution_bias,
        convolution_weight.reshape(2, 3, 3 * CH, CH),
    )


def solution(mesh):
    return jax.shard_map(
        local,
        mesh=mesh,
        in_specs=(P("row", "col", None),) + (P(),) * 12,
        out_specs=P("row", "col", None),
        check_vma=False,
    )
```

time: 496 us -> 229 us (0.46)
  the two profiles are of different devices: /device:TPU:25 before, /device:TPU:10 now
where the time goes in v1:
time: 229 us; the launch traced here: 228 us
  Pallas kernels  68.1 us (30%)
  waiting for transfers between devices  66.7 us (29%)
  blocking collectives  61.2 us (27%)
  starting transfers between devices  19.8 us (9%)
  local copies, waits for them, and re-layouts  11.4 us (5%)
    all_to_all x1, blocking collectives, local(): lax.all_to_all(sent.reshape(128, 2, ROWS, COLS), ('row', 'col'), split_ax...  61.2 us
    all_to_all x1, waiting for transfers between devices, local(): lax.all_to_all(back.reshape(128, 2, ROWS, COLS), ('row', 'col'), split_ax...  49 us
    pallas_call x1, Pallas kernels, convolutions(): pl.pallas_call(convolution_kernel, out_shape=jax.ShapeDtypeStruct((ROWS,...  38.4 us
    pallas_call x1, Pallas kernels, update(): pl.pallas_call(update_kernel, grid=(ROWS // USTEP,), out_shape=jax.ShapeD...  17.2 us
    ppermute x2, waiting for transfers between devices, neighbours(): lax.ppermute(high_strip, axis, forward)  11.7 us
    all_to_all x1, starting transfers between devices, local(): lax.all_to_all(back.reshape(128, 2, ROWS, COLS), ('row', 'col'), split_ax...  8 us
    ppermute x2, starting transfers between devices, neighbours(): lax.ppermute(low_strip, axis, backward)  7.25 us
    pallas_call x1, Pallas kernels, product(): pl.pallas_call(product_kernel, grid=(1,), out_shape=jax.ShapeDtypeStruct(...  6.75 us
  transfers between devices with their start and end apart: 6, of which 6 were waited for; matrix products, arithmetic and copies ran while one was open for 1% of the time, Pallas kernels for 0%

profile of v1, /device:TPU:10, one launch (start us, length us, event | category | flops | bytes accessed | tf_op | source)
XLA Modules:
  0.0 228.0 jit_solution(1091572233677714842)
XLA Ops:
  0.0 0.7 slice.40
  0.7 0.1 copy.28.bias_ref
  0.8 0.9 slice.39
  1.7 0.1 copy.35
  1.8 0.0 copy-start.1
  1.8 1.6 copy-done.1
  3.4 0.0 copy-start.4
  3.4 0.7 copy-done.4
  4.0 0.0 copy-start.6
  4.0 0.7 copy-done.6
  4.7 5.7 %factors.1 = bf16[8,2,8,2,64,128]{5,4,3,2,1,0:T(8,128)(2,1)S(1)} custom-call(bf16[64,128,128]{2,1,0:T(8,128)(2,1)S(1)} %copy-done.1, f32[1,128]{1,0:T(1,128)S(1)} %bitcast.21, f32[1,128]{1,0:T(1,128)S(1)} %bitcast.23, bf16[256,128]{1,0:T(8,128)(2,1)S(1)} %bitcast.20, f32[256,1]{1,0:T(8,128)S(1)} %copy.28.bias_ref), custom_call_target="tpu_custom_call" | custom-call | tf_op jit(solution)/shard_map/factors/pallas_call | solution.py:67
  10.4 61.2 %all_to_all.10 = bf16[128,2,64,128]{3,2,1,0:T(8,128)(2,1)S(1)} all-to-all(bf16[128,2,64,128]{3,2,1,0:T(8,128)(2,1)S(1)} %bitcast.19), channel_id=1, replica_groups=mesh['row'=16,'col'=8] {'row','col'}, dimensions={0} | all-to-all | bytes 8388608 | tf_op jit(solution)/shard_map/all_to_all | solution.py:348
  71.6 0.0 copy-start.9
  71.6 1.2 copy.29
  72.8 1.3 copy-done.9
  74.1 0.2 slice_bitcast_fusion
  74.3 0.1 collective-permute-start
  74.4 4.1 %collective-permute-done.other_ref = bf16[16,8,64,128]{3,2,1,0:T(8,128)(2,1)S(1)} collective-permute-done((bf16[16,8,64,128]{3,2,1,0:T(8,128)(2,1)S(1)}, bf16[16,8,64,128]{3,2,1,0:T(8,128)(2,1)S(1)}, u32[]{:S(2)}, u32[]{:S(2)}) %collective-permute-start) | collective-permute-done | bytes 2097184 | tf_op jit(solution)/shard_map/ppermute | solution.py:351
  78.6 6.7 %product.1 = bf16[16,8,2,64,128]{4,3,2,1,0:T(8,128)(2,1)} custom-call(bf16[16,8,2,64,128]{4,3,2,1,0:T(8,128)(2,1)} %bitcast.26, bf16[16,8,2,64,128]{4,3,2,1,0:T(8,128)(2,1)} %bitcast.27, bf16[16,8,64,128]{3,2,1,0:T(8,128)(2,1)S(1)} %collective-permute-done.other_ref), custom_call_target="tpu_custom_call" | custom-call | tf_op jit(solution)/shard_map/product/pallas_call | solution.py:120
  85.3 0.0 copy-start.14
  85.3 0.0 copy-start.15
  85.3 0.0 copy-start.3
  85.3 0.0 copy-start.5
  85.3 0.0 copy-start.7
  85.3 0.0 copy-start.8
  85.4 8.0 %all-to-all-start.1 = ((bf16[128,2,64,128]{3,2,1,0:T(8,128)(2,1)}), bf16[128,2,64,128]{3,2,1,0:T(8,128)(2,1)}, u32[]{:S(2)}, u32[]{:S(2)}) async-start(bf16[128,2,64,128]{3,2,1,0:T(8,128)(2,1)} %bitcast.28), calls=%async_computation.1 | async-start | bytes 8388608 | tf_op jit(solution)/shard_map/all_to_all | solution.py:353
  93.4 0.8 slice.42.gate_ref
  94.1 0.0 copy-done.14
  94.1 0.1 copy.32.mid_gain_ref
  94.2 0.0 copy-done.15
  94.2 0.1 copy.33.mid_shift_ref
  94.3 0.7 slice_bitcast_fusion.1.gate_bias_ref
  95.0 49.0 %all-to-all-done.1.mirror_ref = bf16[128,2,64,128]{3,2,1,0:T(8,128)(2,1)} async-done(((bf16[128,2,64,128]{3,2,1,0:T(8,128)(2,1)}), bf16[128,2,64,128]{3,2,1,0:T(8,128)(2,1)}, u32[]{:S(2)}, u32[]{:S(2)}) %all-to-all-start.1) | async-done | bytes 4194336 | tf_op jit(solution)/shard_map/all_to_all | solution.py:353
  144.0 0.0 copy-done.3
  144.0 0.0 copy-done.5
  144.0 0.0 copy-done.7
  144.1 0.0 copy-done.8
  144.1 0.0 copy-start.2
  144.1 1.6 copy-done.2
  145.7 17.2 %update.1.sym_ref = bf16[64,128,128]{2,1,0:T(8,128)(2,1)S(1)} custom-call(bf16[64,128,128]{2,1,0:T(8,128)(2,1)S(1)} %copy-done.2, bf16[8,2,8,2,64,128]{5,4,3,2,1,0:T(8,128)(2,1)} %bitcast.11.tri_ref, bf16[128,2,64,128]{3,2,1,0:T(8,128)(2,1)} %all-to-all-done.1.mirror_ref, f32[1,128]{1,0:T(1,128)S(1)} %bitcast.22, f32[1,128]{1,0:T(1,128)S(1)} %bitcast.24, ...), custom_call_target="tpu_custom_call" | custom-call | tf_op jit(solution)/shard_map/update/pallas_call | solution.py:185
  162.8 0.0 copy-start
  162.9 3.9 %collective-permute-start.2 = (bf16[6,128,128]{2,1,0:T(8,128)(2,1)S(1)}, bf16[6,128,128]{2,1,0:T(8,128)(2,1)S(1)}, u32[]{:S(2)}, u32[]{:S(2)}) collective-permute-start(bf16[6,128,128]{2,1,0:T(8,128)(2,1)S(1)} %get-tuple-element.7), channel_id=1, source_target_pairs={{8,0},{16,8},{24,16},{32,24},{40,32},{48,40},{56,48},{64,56},{72,6... | collective-permute-start | bytes 589832 | tf_op jit(solution)/shard_map/ppermute | solution.py:337
  166.8 1.9 collective-permute-start.1
  168.8 0.1 fusion
  168.8 1.2 collective-permute-done.2.bottom_ref
  170.0 0.0 copy-start.10
  170.0 6.2 %collective-permute-done.1.top_ref = bf16[6,128,128]{2,1,0:T(8,128)(2,1)S(1)} collective-permute-done((bf16[6,128,128]{2,1,0:T(8,128)(2,1)S(1)}, bf16[6,128,128]{2,1,0:T(8,128)(2,1)S(1)}, u32[]{:S(2)}, u32[]{:S(2)}) %collective-permute-start.1) | collective-permute-done | bytes 196640 | tf_op jit(solution)/shard_map/ppermute | solution.py:337
  176.2 0.0 copy-start.11
  176.3 3.3 %collective-permute-start.4 = (bf16[76,6,128]{2,1,0:T(8,128)(2,1)S(1)}, bf16[76,6,128]{2,1,0:T(8,128)(2,1)S(1)}, u32[]{:S(2)}, u32[]{:S(2)}) collective-permute-start(bf16[76,6,128]{2,1,0:T(8,128)(2,1)S(1)} %pad_maximum_fusion.1), channel_id=1, source_target_pairs={{1,0},{2,1},{3,2},{4,3},{5,4},{6,5},{7,6},{9,8},{10,9},{11,10},{12... | collective-permute-start | bytes 350216 | tf_op jit(solution)/shard_map/ppermute | solution.py:337
  179.7 2.5 %collective-permute-start.3 = (bf16[76,6,128]{2,1,0:T(8,128)(2,1)S(1)}, bf16[76,6,128]{2,1,0:T(8,128)(2,1)S(1)}, u32[]{:S(2)}, u32[]{:S(2)}) collective-permute-start(bf16[76,6,128]{2,1,0:T(8,128)(2,1)S(1)} %pad_maximum_fusion), channel_id=1, source_target_pairs={{0,1},{1,2},{2,3},{3,4},{4,5},{5,6},{6,7},{8,9},{9,10},{10,11},{11... | collective-permute-start | bytes 350216 | tf_op jit(solution)/shard_map/ppermute | solution.py:337
  182.2 0.6 pad_add_fusion.place_ref
  182.8 0.6 collective-permute-done.4.high_ref
  183.4 0.0 copy-start.12
  183.4 5.5 %collective-permute-done.3.low_ref = bf16[76,6,128]{2,1,0:T(8,128)(2,1)S(1)} collective-permute-done((bf16[76,6,128]{2,1,0:T(8,128)(2,1)S(1)}, bf16[76,6,128]{2,1,0:T(8,128)(2,1)S(1)}, u32[]{:S(2)}, u32[]{:S(2)}) %collective-permute-start.3) | collective-permute-done | bytes 116768 | tf_op jit(solution)/shard_map/ppermute | solution.py:337
  188.9 0.0 copy-start.13
  188.9 0.0 copy-done
  188.9 0.0 copy-done.10
  188.9 0.0 copy-done.11
  188.9 0.0 copy-done.12
  188.9 0.6 copy-done.13
  189.6 38.4 %convolutions.1 = bf16[64,128,128]{2,1,0:T(8,128)(2,1)} custom-call(s32[2]{0:T(128)} %pad_add_fusion.place_ref, bf16[64,128,128]{2,1,0:T(8,128)(2,1)} %copy-done, bf16[6,128,128]{2,1,0:T(8,128)(2,1)} %copy-done.11, bf16[6,128,128]{2,1,0:T(8,128)(2,1)} %copy-done.10, bf16[76,6,128]{2,1,0:T(8,128)(2,1)} %copy-done.13, bf16[76,6,128]{2,1,0:T(8,128)(2,1)} %copy-done.12, ...), custom_call_target="tpu_custom_call" | custom-call | tf_op jit(solution)/shard_map/convolutions/pallas_call | solution.py:315
  (5 shorter events, 0.1 us)
Async XLA Ops:
  1.8 1.6 copy-start.1
  3.4 0.7 copy-start.4
  4.0 0.7 copy-start.6
  71.6 2.5 %copy-start.9 = (bf16[128,2,64,128]{3,2,1,0:T(8,128)(2,1)}, bf16[128,2,64,128]{3,2,1,0:T(8,128)(2,1)S(1)}, u32[]{:S(2)}) copy-start(bf16[128,2,64,128]{3,2,1,0:T(8,128)(2,1)S(1)} %all_to_all.10) | copy-start | bytes 12582916
  74.3 4.2 %collective-permute-start = (bf16[16,8,64,128]{3,2,1,0:T(8,128)(2,1)S(1)}, bf16[16,8,64,128]{3,2,1,0:T(8,128)(2,1)S(1)}, u32[]{:S(2)}, u32[]{:S(2)}) collective-permute-start(bf16[16,8,64,128]{3,2,1,0:T(8,128)(2,1)S(1)} %slice_bitcast_fusion), channel_id=1, source_target_pairs={{0,8},{8,0},{16,24},{24,16},{32,40},{40,32},{48,56},{56,48},{64,72... | collective-permute-start | bytes 6291464 | tf_op jit(solution)/shard_map/ppermute | solution.py:351
  85.3 8.8 %copy-start.14 = (f32[64]{0:T(128)S(1)}, f32[64]{0:T(128)}, u32[]{:S(2)}) copy-start(f32[64]{0:T(128)} %param.18) | copy-start | bytes 772
  85.3 8.9 %copy-start.15 = (f32[64]{0:T(128)S(1)}, f32[64]{0:T(128)}, u32[]{:S(2)}) copy-start(f32[64]{0:T(128)} %param.19) | copy-start | bytes 772
  85.3 58.7 %copy-start.3 = (bf16[64,128]{1,0:T(8,128)(2,1)S(1)}, bf16[64,128]{1,0:T(8,128)(2,1)}, u32[]{:S(2)}) copy-start(bf16[64,128]{1,0:T(8,128)(2,1)} %out_weight_ref.1) | copy-start | bytes 49156
  85.3 58.7 %copy-start.5 = (f32[128]{0:T(128)S(1)}, f32[128]{0:T(128)}, u32[]{:S(2)}) copy-start(f32[128]{0:T(128)} %param.14) | copy-start | bytes 1540
  85.3 58.7 %copy-start.7 = (f32[128]{0:T(128)S(1)}, f32[128]{0:T(128)}, u32[]{:S(2)}) copy-start(f32[128]{0:T(128)} %param.15) | copy-start | bytes 1540
  85.3 58.7 %copy-start.8 = (f32[128]{0:T(128)S(1)}, f32[128]{0:T(128)}, u32[]{:S(2)}) copy-start(f32[128]{0:T(128)} %param.21) | copy-start | bytes 1540
  85.4 58.7 %all-to-all-start.1 = ((bf16[128,2,64,128]{3,2,1,0:T(8,128)(2,1)}), bf16[128,2,64,128]{3,2,1,0:T(8,128)(2,1)}, u32[]{:S(2)}, u32[]{:S(2)}) async-start(bf16[128,2,64,128]{3,2,1,0:T(8,128)(2,1)} %bitcast.28), calls=%async_computation.1 | async-start | bytes 8388608 | tf_op jit(solution)/shard_map/all_to_all | solution.py:353
  144.1 1.6 copy-start.2
  162.8 26.1 %copy-start = (bf16[64,128,128]{2,1,0:T(8,128)(2,1)}, bf16[64,128,128]{2,1,0:T(8,128)(2,1)S(1)}, u32[]{:S(2)}) copy-start(bf16[64,128,128]{2,1,0:T(8,128)(2,1)S(1)} %update.1.sym_ref) | copy-start | bytes 6291460
  162.9 7.1 %collective-permute-start.2 = (bf16[6,128,128]{2,1,0:T(8,128)(2,1)S(1)}, bf16[6,128,128]{2,1,0:T(8,128)(2,1)S(1)}, u32[]{:S(2)}, u32[]{:S(2)}) collective-permute-start(bf16[6,128,128]{2,1,0:T(8,128)(2,1)S(1)} %get-tuple-element.7), channel_id=1, source_target_pairs={{8,0},{16,8},{24,16},{32,24},{40,32},{48,40},{56,48},{64,56},{72,6... | collective-permute-start | bytes 589832 | tf_op jit(solution)/shard_map/ppermute | solution.py:337
  166.8 9.4 %collective-permute-start.1 = (bf16[6,128,128]{2,1,0:T(8,128)(2,1)S(1)}, bf16[6,128,128]{2,1,0:T(8,128)(2,1)S(1)}, u32[]{:S(2)}, u32[]{:S(2)}) collective-permute-start(bf16[6,128,128]{2,1,0:T(8,128)(2,1)S(1)} %get-tuple-element.8), channel_id=1, source_target_pairs={{0,8},{8,16},{16,24},{24,32},{32,40},{40,48},{48,56},{56,64},{64,7... | collective-permute-start | bytes 589832 | tf_op jit(solution)/shard_map/ppermute | solution.py:337
  170.0 18.9 %copy-start.10 = (bf16[6,128,128]{2,1,0:T(8,128)(2,1)}, bf16[6,128,128]{2,1,0:T(8,128)(2,1)S(1)}, u32[]{:S(2)}) copy-start(bf16[6,128,128]{2,1,0:T(8,128)(2,1)S(1)} %collective-permute-done.2.bottom_ref) | copy-start | bytes 589828
  176.2 12.7 %copy-start.11 = (bf16[6,128,128]{2,1,0:T(8,128)(2,1)}, bf16[6,128,128]{2,1,0:T(8,128)(2,1)S(1)}, u32[]{:S(2)}) copy-start(bf16[6,128,128]{2,1,0:T(8,128)(2,1)S(1)} %collective-permute-done.1.top_ref) | copy-start | bytes 589828
  176.3 7.1 %collective-permute-start.4 = (bf16[76,6,128]{2,1,0:T(8,128)(2,1)S(1)}, bf16[76,6,128]{2,1,0:T(8,128)(2,1)S(1)}, u32[]{:S(2)}, u32[]{:S(2)}) collective-permute-start(bf16[76,6,128]{2,1,0:T(8,128)(2,1)S(1)} %pad_maximum_fusion.1), channel_id=1, source_target_pairs={{1,0},{2,1},{3,2},{4,3},{5,4},{6,5},{7,6},{9,8},{10,9},{11,10},{12... | collective-permute-start | bytes 350216 | tf_op jit(solution)/shard_map/ppermute | solution.py:337
  179.7 9.2 %collective-permute-start.3 = (bf16[76,6,128]{2,1,0:T(8,128)(2,1)S(1)}, bf16[76,6,128]{2,1,0:T(8,128)(2,1)S(1)}, u32[]{:S(2)}, u32[]{:S(2)}) collective-permute-start(bf16[76,6,128]{2,1,0:T(8,128)(2,1)S(1)} %pad_maximum_fusion), channel_id=1, source_target_pairs={{0,1},{1,2},{2,3},{3,4},{4,5},{5,6},{6,7},{8,9},{9,10},{10,11},{11... | collective-permute-start | bytes 350216 | tf_op jit(solution)/shard_map/ppermute | solution.py:337
  183.4 5.5 %copy-start.12 = (bf16[76,6,128]{2,1,0:T(8,128)(2,1)}, bf16[76,6,128]{2,1,0:T(8,128)(2,1)S(1)}, u32[]{:S(2)}) copy-start(bf16[76,6,128]{2,1,0:T(8,128)(2,1)S(1)} %collective-permute-done.4.high_ref) | copy-start | bytes 350212
  188.9 0.7 copy-start.13

commit v2 on v1

v2 whole, which is shorter than its diff:
```python
import jax
import jax.numpy as jnp
from jax import lax
from jax.experimental import pallas as pl
from jax.experimental.pallas import tpu as pltpu
from jax.sharding import PartitionSpec as P

FIRST_DILATION = 2
SECOND_DILATION = 4
HALO = FIRST_DILATION + SECOND_DILATION
EPS = 1e-05
BF = jnp.bfloat16
F32 = jnp.float32
MIB = 1 << 20
ROWS, COLS, CH, HID = 64, 128, 128, 64
NR, NC = 16, 8


def sigmoid(x):
    return 0.5 * jnp.tanh(0.5 * x) + 0.5


def normalize(values, gain, shift):
    mean = jnp.mean(values, axis=-1, keepdims=True)
    centred = values - mean
    spread = jnp.mean(centred * centred, axis=-1, keepdims=True)
    return centred * lax.rsqrt(spread + EPS) * gain + shift


NT = (((1,), (1,)), ((), ()))
TN = (((0,), (0,)), ((), ()))

STEP = 16


def factor_kernel(pair_ref, gain_ref, shift_ref, weight_ref, bias_ref, out_ref, lay_ref):
    step = pl.program_id(0)
    block = pair_ref[...]
    cells = block.astype(F32).reshape(STEP * COLS, CH)
    normed = normalize(cells, gain_ref[...], shift_ref[...]).astype(BF)
    bias = jnp.transpose(jnp.broadcast_to(bias_ref[:, : 4 * HID], (COLS, 4 * HID)))
    projected = lax.dot_general(
        weight_ref[:, : 4 * HID], normed, (((0,), (1,)), ((), ())), preferred_element_type=F32
    )
    start = pl.multiple_of(step * STEP, STEP)
    for side in range(2):
        base = 2 * HID * side
        for row in range(STEP):
            part = slice(row * COLS, (row + 1) * COLS)
            gate = projected[base : base + HID, part] + bias[base : base + HID]
            value = projected[base + HID : base + 2 * HID, part] + bias[base + HID : base + 2 * HID]
            lay_ref[pl.ds(row, HID, stride=STEP), :] = sigmoid(gate) * value
        out_ref[:, side, :, 0, pl.ds(start, STEP), :] = (
            lay_ref[...].astype(BF).reshape(8, 8, STEP, COLS)
        )
    for row in range(STEP):
        for q in range(2):
            local = 2 * row + q
            group = step * 2 + local // 16
            side = (local // 8) % 2
            column = local % 8
            for half in range(2):
                out_ref[group, side, column, 1, half * 32 : half * 32 + 32, :] = pair_ref[
                    row, half * 64 + q * 32 : half * 64 + q * 32 + 32, :
                ]


FACTORS_VMEM = 60


def factors(pair, gain, shift, weight, bias):
    whole = lambda *shape: pl.BlockSpec(shape, lambda s: (0,) * len(shape))
    return pl.pallas_call(
        factor_kernel,
        grid=(ROWS // STEP,),
        out_shape=jax.ShapeDtypeStruct((8, 2, 8, 2, ROWS, COLS), BF),
        in_specs=[
            pl.BlockSpec((STEP, COLS, CH), lambda s: (s, 0, 0)),
            whole(1, CH),
            whole(1, CH),
            whole(CH, 4 * HID + CH),
            whole(1, 4 * HID + CH),
        ],
        out_specs=whole(8, 2, 8, 2, ROWS, COLS),
        scratch_shapes=[pltpu.VMEM((HID * STEP, COLS), F32)],
        compiler_params=pltpu.CompilerParams(vmem_limit_bytes=FACTORS_VMEM * MIB),
        name="factors",
    )(pair, gain, shift, weight, bias)


def product_kernel(own_ref, moved_ref, other_ref, out_ref, rhs_ref):
    for col in range(NC):
        rhs_ref[:, col * COLS : (col + 1) * COLS] = other_ref[:, col].reshape(NR * ROWS, COLS)
    half = NR // 2
    for part in range(2):
        lhs = jnp.concatenate(
            [
                own_ref[part * half : (part + 1) * half, col, 0].reshape(half * ROWS, COLS)
                for col in range(NC)
            ],
            axis=1,
        )
        for block in range(4):
            result = lax.dot_general(
                lhs,
                rhs_ref[block * 256 : (block + 1) * 256, :],
                NT,
                preferred_element_type=F32,
            ).astype(BF)
            for col in range(2):
                out_ref[part * half : (part + 1) * half, block * 2 + col, 0] = result[
                    :, col * COLS : (col + 1) * COLS
                ].reshape(half, ROWS, COLS)
    for row in range(NR):
        for col in range(NC):
            side = row % 2
            for e in range(2):
                out_ref[row, col, 1, e * 32 : e * 32 + 32, :] = moved_ref[
                    2 * col + e, row // 2, 0, side * 32 : side * 32 + 32, :
                ]


def product(received, other):
    whole = lambda *shape: pl.BlockSpec(shape, lambda s: (0,) * len(shape))
    slot = lambda k: pl.BlockSpec((NR, NC, 1, ROWS, COLS), lambda s: (0, 0, k, 0, 0))
    return pl.pallas_call(
        product_kernel,
        grid=(1,),
        out_shape=jax.ShapeDtypeStruct((NR, NC, 2, ROWS, COLS), BF),
        in_specs=[slot(0), slot(1), whole(NR, NC, ROWS, COLS)],
        out_specs=whole(NR, NC, 2, ROWS, COLS),
        scratch_shapes=[pltpu.VMEM((NR * ROWS, NC * COLS), BF)],
        compiler_params=pltpu.CompilerParams(vmem_limit_bytes=48 * MIB),
        name="product",
    )(received, received, other)


def gate_kernel(pair_ref, gain_ref, shift_ref, weight_ref, bias_ref, out_ref):
    cells = pair_ref[...].astype(F32).reshape(STEP * COLS, CH)
    normed = normalize(cells, gain_ref[...], shift_ref[...]).astype(BF)
    gate = jnp.dot(normed, weight_ref[...], preferred_element_type=F32) + bias_ref[...]
    out_ref[...] = sigmoid(gate).reshape(STEP, COLS, CH)


def gates(pair, gain, shift, weight, bias):
    whole = lambda *shape: pl.BlockSpec(shape, lambda s: (0,) * len(shape))
    block = pl.BlockSpec((STEP, COLS, CH), lambda s: (s, 0, 0))
    return pl.pallas_call(
        gate_kernel,
        grid=(ROWS // STEP,),
        out_shape=jax.ShapeDtypeStruct((ROWS, COLS, CH), F32),
        in_specs=[block, whole(1, CH), whole(1, CH), whole(CH, CH), whole(1, CH)],
        out_specs=block,
        compiler_params=pltpu.CompilerParams(vmem_limit_bytes=24 * MIB),
        cost_estimate=pl.CostEstimate(
            flops=2 * ROWS * COLS * CH * CH, bytes_accessed=6 * ROWS * COLS * CH, transcendentals=ROWS * COLS * CH
        ),
        name="gates",
    )(pair, gain, shift, weight, bias)


USTEP = 16
UNROLL_U = 1
UGROUP = 8
PITCH = 72


def update_kernel(
    pair_ref, own_gate_ref, tri_ref, mirror_ref, gain_ref, shift_ref, gate_ref, gate_bias_ref,
    out_weight_ref, out_bias_ref, sym_ref, cells_ref, lay_ref,
):
    step = pl.program_id(0)

    @pl.when(step == 0)
    def _():
        for d in range(128):
            for e in range(2):
                at = (e * 64 + d // 2) * PITCH + (d % 2) * 32
                cells_ref[at : at + 32, :] = mirror_ref[d, 0, e * 32 : e * 32 + 32, :].astype(F32)

    tri = tri_ref[:, :, :, 0].astype(F32)
    mean = jnp.mean(tri, axis=(0, 2), keepdims=True)
    centred = tri - mean
    spread = jnp.mean(centred * centred, axis=(0, 2), keepdims=True)
    lay_ref[...] = (centred * lax.rsqrt(spread + EPS)).reshape(2 * HID * USTEP, COLS)

    def body(part, carry):
        first = part * UGROUP
        change, cells = [], []
        for k in range(UGROUP):
            mid = lay_ref[pl.ds(first + k, 2 * HID, stride=USTEP), :].astype(BF)
            change.append(
                lax.dot_general(mid, out_weight_ref[...], TN, preferred_element_type=F32)
            )
            cells.append(
                cells_ref[pl.ds(step * USTEP + first + k, COLS, stride=PITCH), :]
            )
        change = jnp.concatenate(change, axis=0) + out_bias_ref[...]
        cells = jnp.concatenate(cells, axis=0)
        size = UGROUP * COLS
        own = (
            pair_ref[pl.ds(first, UGROUP)].astype(F32).reshape(size, CH)
            + own_gate_ref[pl.ds(first, UGROUP)].reshape(size, CH) * change[:, :CH]
        )
        normed = normalize(cells, gain_ref[...], shift_ref[...]).astype(BF)
        gate = sigmoid(
            jnp.dot(normed, gate_ref[...], preferred_element_type=F32) + gate_bias_ref[...]
        )
        mirrored = cells + gate * change[:, CH:]
        total = own.astype(BF).astype(F32) + mirrored.astype(BF).astype(F32)
        sym_ref[pl.ds(first, UGROUP)] = (total * 0.5).astype(BF).reshape(UGROUP, COLS, CH)
        return carry

    lax.fori_loop(0, USTEP // UGROUP, body, 0, unroll=UNROLL_U)


def update(pair, own_gate, received, gain, shift, gate, gate_bias, out_weight, out_bias):
    whole = lambda *shape: pl.BlockSpec(shape, lambda s: (0,) * len(shape))
    tri = received.reshape(8, 2, 8, 2, ROWS, COLS)
    cells = received.reshape(128, 2, ROWS, COLS)
    block = pl.BlockSpec((USTEP, COLS, CH), lambda s: (s, 0, 0))
    return pl.pallas_call(
        update_kernel,
        grid=(ROWS // USTEP,),
        out_shape=jax.ShapeDtypeStruct((ROWS, COLS, CH), BF),
        in_specs=[
            block,
            block,
            pl.BlockSpec((8, 2, 8, 1, USTEP, COLS), lambda s: (0, 0, 0, 0, s, 0)),
            pl.BlockSpec((128, 1, ROWS, COLS), lambda s: (0, 1, 0, 0)),
            whole(1, CH),
            whole(1, CH),
            whole(CH, CH),
            whole(1, CH),
            whole(2 * HID, 2 * CH),
            whole(1, 2 * CH),
        ],
        out_specs=block,
        scratch_shapes=[
            pltpu.VMEM((COLS * PITCH, CH), F32),
            pltpu.VMEM((2 * HID * USTEP, COLS), F32),
        ],
        compiler_params=pltpu.CompilerParams(vmem_limit_bytes=48 * MIB),
        name="update",
    )(pair, own_gate, tri, cells, gain, shift, gate, gate_bias, out_weight, out_bias)


def output_weight(weight, bias, gain, shift):
    scaled = (gain[:, None] * weight.astype(F32)).astype(BF).reshape(8, 1, 8, CH)
    nothing = jnp.zeros_like(scaled)
    own = jnp.concatenate([scaled, nothing], axis=1)
    mirrored = jnp.concatenate([nothing, scaled], axis=1)
    full = jnp.concatenate([own, mirrored], axis=3).reshape(2 * HID, 2 * CH)
    offset = bias + jnp.sum(shift[:, None] * weight.astype(F32), axis=0)
    return full, jnp.concatenate([offset, offset])[None]


TALL = ROWS + 2 * HALO
SIDE = 8
WIDE = COLS + 2 * SIDE
FIRST_TALL = ROWS + 2 * SECOND_DILATION
GROUP_A, GROUP_B, GROUP_C = 4, 4, 8
UNROLL_A, UNROLL_B = 2, 6


def convolution_kernel(
    place_ref, sym_ref, top_ref, bottom_ref, low_ref, high_ref, gain_ref, shift_ref, bias_ref,
    weight_hbm, out_hbm, tall_ref, act_ref, cols_ref, first_ref, second_ref, second_cols_ref,
    weight_ref, out_ref, sems, out_sems,
):
    def rows_copy(k):
        return pltpu.make_async_copy(
            sym_ref.at[16 * k : 16 * k + 16],
            tall_ref.at[HALO + 16 * k : HALO + 16 * k + 16],
            sems.at[k],
        )

    top_copy = pltpu.make_async_copy(top_ref, tall_ref.at[0:HALO], sems.at[4])
    bottom_copy = pltpu.make_async_copy(bottom_ref, tall_ref.at[HALO + ROWS : TALL], sems.at[5])
    weight_copy = pltpu.make_async_copy(weight_hbm, weight_ref, sems.at[6])
    top_copy.start()
    for k in range(4):
        rows_copy(k).start()
    bottom_copy.start()
    weight_copy.start()
    above = place_ref[0] > 0
    below = place_ref[0] < (NR - 1) * ROWS
    low_ok = (place_ref[1] > 0).astype(F32)
    high_ok = (place_ref[1] < (NC - 1) * COLS).astype(F32)
    act_ref[...] = jnp.zeros((GROUP_A, WIDE + 16, CH), F32)

    def values(at, count):
        return jnp.concatenate(
            [
                low_ref[pl.ds(at, count)].astype(F32),
                tall_ref[pl.ds(at, count)].astype(F32),
                high_ref[pl.ds(at, count)].astype(F32),
            ],
            axis=1,
        )

    def activate(cells, which):
        return jnp.maximum(
            normalize(
                cells,
                gain_ref[which : which + 1].reshape(1, 1, CH),
                shift_ref[which : which + 1].reshape(1, 1, CH),
            ),
            0.0,
        )

    def prepare(step, carry):
        at = step * GROUP_A
        act = activate(values(at, GROUP_A), 0)
        act_ref[:, 8:16, :] = act[:, :SIDE] * low_ok
        act_ref[:, 16 : 16 + COLS, :] = act[:, SIDE : SIDE + COLS]
        act_ref[:, 16 + COLS : 24 + COLS, :] = act[:, SIDE + COLS :] * high_ok
        for tap in range(3):
            cols_ref[pl.ds(at, GROUP_A), :, tap * CH : (tap + 1) * CH] = act_ref[
                :, 6 + 2 * tap : 6 + 2 * tap + WIDE, :
            ].astype(BF)
        return carry

    top_copy.wait()
    begin = 0
    for k, end in enumerate((20, 36, 52, TALL)):
        rows_copy(k).wait()
        if k == 3:
            bottom_copy.wait()
        lax.fori_loop(begin // GROUP_A, end // GROUP_A, prepare, 0, unroll=UNROLL_A)
        begin = end
    weight_copy.wait()

    @pl.when(jnp.logical_not(above))
    def _():
        cols_ref[0:HALO] = jnp.zeros((HALO, WIDE, 3 * CH), BF)

    @pl.when(jnp.logical_not(below))
    def _():
        cols_ref[HALO + ROWS :] = jnp.zeros((HALO, WIDE, 3 * CH), BF)

    def paired(source_ref, at, spacing, group, width, which):
        sets = group // (2 * spacing)
        lhs = jnp.concatenate(
            [
                jnp.concatenate(
                    [
                        source_ref[pl.ds(at + 2 * spacing * k + spacing * slot, spacing)]
                        for k in range(sets)
                    ],
                    axis=0,
                ).reshape(group // 2 * width, 3 * CH)
                for slot in range(4)
            ],
            axis=1,
        )
        total = jnp.dot(lhs, weight_ref[which], preferred_element_type=F32)
        near = total[:, :CH].reshape(sets, spacing, width, CH)
        far = total[:, CH:].reshape(sets, spacing, width, CH)
        return jnp.concatenate([near, far], axis=1).reshape(group, width, CH)

    def convolve_first(step, carry):
        at = step * GROUP_B
        first = (
            paired(cols_ref, at, FIRST_DILATION, GROUP_B, WIDE, 0)
            + values(at + 2, GROUP_B)
            + bias_ref[0:1].reshape(1, 1, CH)
        )
        first_ref[pl.ds(at, GROUP_B)] = first[:, SIDE : SIDE + COLS]
        act = activate(first, 1)
        second_ref[:, :SIDE, :] = act[:, :SIDE] * low_ok
        second_ref[:, SIDE : SIDE + COLS, :] = act[:, SIDE : SIDE + COLS]
        second_ref[:, SIDE + COLS :, :] = act[:, SIDE + COLS :] * high_ok
        for tap in range(3):
            second_cols_ref[pl.ds(at, GROUP_B), :, tap * CH : (tap + 1) * CH] = second_ref[
                :, 4 + 4 * tap : 4 + 4 * tap + COLS, :
            ].astype(BF)
        return carry

    lax.fori_loop(0, FIRST_TALL // GROUP_B, convolve_first, 0, unroll=UNROLL_B)

    @pl.when(jnp.logical_not(above))
    def _():
        second_cols_ref[0:SECOND_DILATION] = jnp.zeros((SECOND_DILATION, COLS, 3 * CH), BF)

    @pl.when(jnp.logical_not(below))
    def _():
        second_cols_ref[SECOND_DILATION + ROWS :] = jnp.zeros(
            (SECOND_DILATION, COLS, 3 * CH), BF
        )

    def out_copy(k):
        return pltpu.make_async_copy(
            out_ref.at[16 * k : 16 * k + 16], out_hbm.at[16 * k : 16 * k + 16], out_sems.at[k]
        )

    for k in range(4):
        for part in range(16 // GROUP_C):
            at = 16 * k + part * GROUP_C
            out_ref[at : at + GROUP_C] = (
                paired(second_cols_ref, at, SECOND_DILATION, GROUP_C, COLS, 1)
                + first_ref[at + 4 : at + 4 + GROUP_C]
                + bias_ref[1:2].reshape(1, 1, CH)
            ).astype(BF)
        out_copy(k).start()
    for k in range(4):
        out_copy(k).wait()


def convolutions(place, sym, top, bottom, low, high, gain, shift, bias, weight):
    vmem = pl.BlockSpec(memory_space=pltpu.VMEM)
    anywhere = pl.BlockSpec(memory_space=pl.ANY)
    return pl.pallas_call(
        convolution_kernel,
        out_shape=jax.ShapeDtypeStruct((ROWS, COLS, CH), BF),
        in_specs=[pl.BlockSpec(memory_space=pltpu.SMEM)] + [anywhere] * 3 + [vmem] * 5 + [anywhere],
        out_specs=anywhere,
        scratch_shapes=[
            pltpu.VMEM((TALL, COLS, CH), BF),
            pltpu.VMEM((GROUP_A, WIDE + 16, CH), F32),
            pltpu.VMEM((TALL, WIDE, 3 * CH), BF),
            pltpu.VMEM((FIRST_TALL, COLS, CH), F32),
            pltpu.VMEM((GROUP_B, WIDE, CH), F32),
            pltpu.VMEM((FIRST_TALL, COLS, 3 * CH), BF),
            pltpu.VMEM((2, 12 * CH, 2 * CH), BF),
            pltpu.VMEM((ROWS, COLS, CH), BF),
            pltpu.SemaphoreType.DMA((7,)),
            pltpu.SemaphoreType.DMA((4,)),
        ],
        compiler_params=pltpu.CompilerParams(vmem_limit_bytes=44 * MIB),
        name="convolutions",
    )(place, sym, top, bottom, low, high, gain, shift, bias, weight)


def paired_weight(weight):
    taps = weight.reshape(3, 3 * CH, CH)
    near = jnp.concatenate([taps, jnp.zeros_like(taps[:1])], axis=0)
    far = jnp.concatenate([jnp.zeros_like(taps[:1]), taps], axis=0)
    return jnp.concatenate([near, far], axis=2).reshape(12 * CH, 2 * CH)


def neighbours(low_strip, high_strip, axis):
    count = lax.axis_size(axis)
    forward = [(i, i + 1) for i in range(count - 1)]
    backward = [(i + 1, i) for i in range(count - 1)]
    return lax.ppermute(high_strip, axis, forward), lax.ppermute(low_strip, axis, backward)


def local(
    pair, norm_gain, norm_shift, proj_weight, proj_bias, mid_gain, mid_shift, out_weight, out_bias,
    conv_gain, conv_shift, convolution_weight, convolution_bias,
):
    gain, shift = norm_gain[None], norm_shift[None]
    sent = factors(pair, gain, shift, proj_weight, proj_bias[None])
    received = lax.all_to_all(
        sent.reshape(128, 2, ROWS, COLS), ("row", "col"), split_axis=0, concat_axis=0, tiled=True
    ).reshape(NR, NC, 2, ROWS, COLS)
    other = lax.ppermute(received[:, :, 0], "row", [(i, i ^ 1) for i in range(NR)])
    back = product(received, other)
    returned = lax.all_to_all(
        back.reshape(128, 2, ROWS, COLS), ("row", "col"), split_axis=0, concat_axis=0, tiled=True
    )
    gate, gate_bias = proj_weight[:, 4 * HID :], proj_bias[None, 4 * HID :]
    sym = update(
        pair, gates(pair, gain, shift, gate, gate_bias), returned, gain, shift, gate, gate_bias,
        *output_weight(out_weight, out_bias, mid_gain, mid_shift),
    )
    top, bottom = neighbours(sym[:HALO], sym[ROWS - HALO :], "row")
    edge = lambda low, high: jnp.concatenate(
        [top[:, low:high], sym[:, low:high], bottom[:, low:high]], axis=0
    )
    low, high = neighbours(edge(0, SIDE), edge(COLS - SIDE, COLS), "col")
    place = jnp.stack([lax.axis_index("row") * ROWS, lax.axis_index("col") * COLS]).astype(jnp.int32)
    return convolutions(
        place, sym, top, bottom, low, high, conv_gain, conv_shift, convolution_bias,
        jnp.stack([paired_weight(convolution_weight[0]), paired_weight(convolution_weight[1])]),
    )


def solution(mesh):
    return jax.shard_map(
        local,
        mesh=mesh,
        in_specs=(P("row", "col", None),) + (P(),) * 12,
        out_specs=P("row", "col", None),
        check_vma=False,
    )
```

time: 229 us -> 200 us (0.87)
  Pallas kernels: 68.1 us -> 46.4 us
  waiting for transfers between devices: 66.7 us -> 57.7 us
  starting transfers between devices: 19.8 us -> 22.2 us
    pallas_call x1, Pallas kernels: 38.4 us -> 17.4 us  [convolutions(): pl.pallas_call(convolution_kernel, out_shape=jax.ShapeDtypeStruct((ROWS,...]
    pallas_call x1, Pallas kernels: 17.2 us -> 9.94 us  [update(): pl.pallas_call(update_kernel, grid=(ROWS // USTEP,), out_shape=jax.ShapeD...]
    all_to_all x1, waiting for transfers between devices: 49 us -> 42.5 us  [local(): lax.all_to_all(back.reshape(128, 2, ROWS, COLS), ('row', 'col'), split_ax...]
    ppermute x2, waiting for transfers between devices: 11.7 us -> 7.62 us  [neighbours(): lax.ppermute(high_strip, axis, forward)]
    pallas_call x0 -> x1, Pallas kernels: none -> 3.42 us  [gates(): pl.pallas_call(gate_kernel, grid=(ROWS // STEP,), out_shape=jax.ShapeDtyp...]
    pallas_call x1, Pallas kernels: 5.69 us -> 8.93 us  [factors(): pl.pallas_call(factor_kernel, grid=(ROWS // STEP,), out_shape=jax.ShapeDt...]
    ppermute x2, starting transfers between devices: 7.25 us -> 10.1 us  [neighbours(): lax.ppermute(low_strip, axis, backward)]
    unnamed x33 -> x32, local copies, waits for them, and re-layouts: 6.6 us -> 4.95 us
  transfers between devices with their start and end apart: 6 -> 6, of which waited for: 6 -> 6; matrix products, arithmetic and copies ran while one was open for 1% -> 1% of each run, Pallas kernels for 0% -> 2%
where the time goes in v2:
time: 200 us; the launch traced here: 199 us
  blocking collectives  61.4 us (31%)
  waiting for transfers between devices  57.7 us (29%)
  Pallas kernels  46.4 us (23%)
  starting transfers between devices  22.2 us (11%)
  local copies, waits for them, and re-layouts  9.17 us (5%)
    all_to_all x1, blocking collectives, local(): lax.all_to_all(sent.reshape(128, 2, ROWS, COLS), ('row', 'col'), split_ax...  61.4 us
    all_to_all x1, waiting for transfers between devices, local(): lax.all_to_all(back.reshape(128, 2, ROWS, COLS), ('row', 'col'), split_ax...  42.5 us
    pallas_call x1, Pallas kernels, convolutions(): pl.pallas_call(convolution_kernel, out_shape=jax.ShapeDtypeStruct((ROWS,...  17.4 us
    ppermute x2, starting transfers between devices, neighbours(): lax.ppermute(low_strip, axis, backward)  10.1 us
    pallas_call x1, Pallas kernels, update(): pl.pallas_call(update_kernel, grid=(ROWS // USTEP,), out_shape=jax.ShapeD...  9.94 us
    pallas_call x1, Pallas kernels, factors(): pl.pallas_call(factor_kernel, grid=(ROWS // STEP,), out_shape=jax.ShapeDt...  8.93 us
    all_to_all x1, starting transfers between devices, local(): lax.all_to_all(back.reshape(128, 2, ROWS, COLS), ('row', 'col'), split_ax...  8.01 us
    ppermute x2, waiting for transfers between devices, neighbours(): lax.ppermute(high_strip, axis, forward)  7.62 us
  transfers between devices with their start and end apart: 6, of which 6 were waited for; matrix products, arithmetic and copies ran while one was open for 1% of the time, Pallas kernels for 2%

profile of v2, /device:TPU:10, one launch (start us, length us, event | category | flops | bytes accessed | tf_op | source)
XLA Modules:
  0.0 198.9 jit_solution(14806964181030863804)
XLA Ops:
  0.0 1.2 broadcast_in_dim.21.bias_ref
  1.2 8.9 %factors.1 = bf16[8,2,8,2,64,128]{5,4,3,2,1,0:T(8,128)(2,1)} custom-call(bf16[64,128,128]{2,1,0:T(8,128)(2,1)} %pair_ref.5, f32[1,128]{1,0:T(1,128)} %bitcast.24, f32[1,128]{1,0:T(1,128)} %bitcast.27, bf16[128,384]{1,0:T(8,128)(2,1)} %weight_ref.1, f32[1,384]{1,0:T(1,128)} %broadcast_in_dim.21.bias_ref), custom_call_target="tpu_custom_call" | custom-call | tf_op jit(solution)/shard_map/factors/pallas_call | solution.py:73
  10.2 61.4 %all_to_all.10 = bf16[128,2,64,128]{3,2,1,0:T(8,128)(2,1)S(1)} all-to-all(bf16[128,2,64,128]{3,2,1,0:T(8,128)(2,1)} %bitcast.34), channel_id=1, replica_groups=mesh['row'=16,'col'=8] {'row','col'}, dimensions={0} | all-to-all | bytes 8388608 | tf_op jit(solution)/shard_map/all_to_all | solution.py:455
  71.6 0.0 copy-start.9
  71.6 1.2 copy.19
  72.8 1.3 copy-done.9
  74.1 0.2 slice_bitcast_fusion
  74.3 0.1 collective-permute-start
  74.4 4.1 %collective-permute-done.other_ref = bf16[16,8,64,128]{3,2,1,0:T(8,128)(2,1)S(1)} collective-permute-done((bf16[16,8,64,128]{3,2,1,0:T(8,128)(2,1)S(1)}, bf16[16,8,64,128]{3,2,1,0:T(8,128)(2,1)S(1)}, u32[]{:S(2)}, u32[]{:S(2)}) %collective-permute-start) | collective-permute-done | bytes 2097184 | tf_op jit(solution)/shard_map/ppermute | solution.py:458
  78.5 6.7 %product.1 = bf16[16,8,2,64,128]{4,3,2,1,0:T(8,128)(2,1)} custom-call(bf16[16,8,2,64,128]{4,3,2,1,0:T(8,128)(2,1)} %bitcast.31, bf16[16,8,2,64,128]{4,3,2,1,0:T(8,128)(2,1)} %bitcast.32, bf16[16,8,64,128]{3,2,1,0:T(8,128)(2,1)S(1)} %collective-permute-done.other_ref), custom_call_target="tpu_custom_call" | custom-call | tf_op jit(solution)/shard_map/product/pallas_call | solution.py:126
  85.3 0.0 copy-start.12
  85.3 0.0 copy-start.13
  85.3 0.0 copy-start.14
  85.3 0.0 copy-start.15
  85.3 0.0 copy-start
  85.3 0.0 copy-start.4
  85.3 0.0 copy-start.5
  85.3 8.0 %all-to-all-start.1 = ((bf16[128,2,64,128]{3,2,1,0:T(8,128)(2,1)}), bf16[128,2,64,128]{3,2,1,0:T(8,128)(2,1)}, u32[]{:S(2)}, u32[]{:S(2)}) async-start(bf16[128,2,64,128]{3,2,1,0:T(8,128)(2,1)} %bitcast.33), calls=%async_computation.1 | async-start | bytes 8388608 | tf_op jit(solution)/shard_map/all_to_all | solution.py:460
  93.4 0.8 slice.39.weight_ref.gate_ref
  94.1 0.0 copy-done.12
  94.1 0.0 copy-done.13
  94.1 0.0 copy-done.14
  94.1 0.1 fusion.10
  94.2 0.0 copy-done.15
  94.2 0.7 slice_bitcast_fusion.1.bias_ref.gate_bias_ref
  94.9 0.0 copy-done
  94.9 0.0 copy-done.4
  94.9 0.0 copy-done.5
  94.9 0.0 copy-start.11
  95.0 3.4 %gates.1.own_gate_ref = f32[64,128,128]{2,1,0:T(8,128)S(1)} custom-call(bf16[64,128,128]{2,1,0:T(8,128)(2,1)S(1)} %copy-done, f32[1,128]{1,0:T(1,128)S(1)} %bitcast.25, f32[1,128]{1,0:T(1,128)S(1)} %bitcast.28, bf16[128,128]{1,0:T(8,128)(2,1)S(1)} %slice.39.weight_ref.gate_ref, f32[1,128]{1,0:T(1,128)S(1)} %slice_bitcast_fusion.1.bias_ref.gate_bias_ref), custom_call_target="tpu_custom_call" | custom-call | flops 268435456 | bytes 6291456 | tf_op jit(solution)/shard_map/gates/pallas_call | solution.py:148
  98.4 0.0 copy-start.1
  98.4 2.0 copy-done.1
  100.4 0.0 copy-done.11
  100.5 0.1 fusion.4
  100.5 1.0 fusion.5
  101.5 42.5 %all-to-all-done.1.mirror_ref = bf16[128,2,64,128]{3,2,1,0:T(8,128)(2,1)} async-done(((bf16[128,2,64,128]{3,2,1,0:T(8,128)(2,1)}), bf16[128,2,64,128]{3,2,1,0:T(8,128)(2,1)}, u32[]{:S(2)}, u32[]{:S(2)}) %all-to-all-start.1) | async-done | bytes 4194336 | tf_op jit(solution)/shard_map/all_to_all | solution.py:460
  144.0 9.9 %update.1.sym_ref = bf16[64,128,128]{2,1,0:T(8,128)(2,1)S(1)} custom-call(bf16[64,128,128]{2,1,0:T(8,128)(2,1)S(1)} %copy-done, f32[64,128,128]{2,1,0:T(8,128)} %copy-done.1, bf16[8,2,8,2,64,128]{5,4,3,2,1,0:T(8,128)(2,1)} %bitcast.10.tri_ref, bf16[128,2,64,128]{3,2,1,0:T(8,128)(2,1)} %all-to-all-done.1.mirror_ref, f32[1,128]{1,0:T(1,128)S(1)} %bitcast.26, ...), custom_call_target="tpu_custom_call" | custom-call | tf_op jit(solution)/shard_map/update/pallas_call | solution.py:222
  154.0 0.0 copy-start.2
  154.0 0.0 copy-start.10
  154.0 2.1 %collective-permute-start.1 = (bf16[6,128,128]{2,1,0:T(8,128)(2,1)S(1)}, bf16[6,128,128]{2,1,0:T(8,128)(2,1)S(1)}, u32[]{:S(2)}, u32[]{:S(2)}) collective-permute-start(bf16[6,128,128]{2,1,0:T(8,128)(2,1)S(1)} %get-tuple-element.8), channel_id=1, source_target_pairs={{0,8},{8,16},{16,24},{24,32},{32,40},{40,48},{48,56},{56,64},{64,7... | collective-permute-start | bytes 589832 | tf_op jit(solution)/shard_map/ppermute | solution.py:446
  156.1 6.0 %collective-permute-start.2 = (bf16[6,128,128]{2,1,0:T(8,128)(2,1)S(1)}, bf16[6,128,128]{2,1,0:T(8,128)(2,1)S(1)}, u32[]{:S(2)}, u32[]{:S(2)}) collective-permute-start(bf16[6,128,128]{2,1,0:T(8,128)(2,1)S(1)} %get-tuple-element.7), channel_id=1, source_target_pairs={{8,0},{16,8},{24,16},{32,24},{40,32},{48,40},{56,48},{64,56},{72,6... | collective-permute-start | bytes 589832 | tf_op jit(solution)/shard_map/ppermute | solution.py:446
  162.2 1.4 collective-permute-done.1.top_ref
  163.6 1.7 collective-permute-done.2.bottom_ref
  165.4 4.1 %collective-permute-start.4 = (bf16[76,8,128]{2,1,0:T(8,128)(2,1)S(1)}, bf16[76,8,128]{2,1,0:T(8,128)(2,1)S(1)}, u32[]{:S(2)}, u32[]{:S(2)}) collective-permute-start(bf16[76,8,128]{2,1,0:T(8,128)(2,1)S(1)} %pad_maximum_fusion.2), channel_id=1, source_target_pairs={{1,0},{2,1},{3,2},{4,3},{5,4},{6,5},{7,6},{9,8},{10,9},{11,10},{12... | collective-permute-start | bytes 466952 | tf_op jit(solution)/shard_map/ppermute | solution.py:446
  169.5 1.9 collective-permute-start.3
  171.4 0.0 copy-done.10
  171.4 0.0 copy-start.6
  171.4 0.0 copy-start.7
  171.5 0.0 copy-start.8
  171.5 0.1 pad_maximum_fusion.weight_hbm
  171.6 0.0 copy-done.2
  171.6 0.1 pad_add_fusion.place_ref
  171.7 1.7 collective-permute-done.4.high_ref
  173.4 6.3 %collective-permute-done.3.low_ref = bf16[76,8,128]{2,1,0:T(8,128)(2,1)S(1)} collective-permute-done((bf16[76,8,128]{2,1,0:T(8,128)(2,1)S(1)}, bf16[76,8,128]{2,1,0:T(8,128)(2,1)S(1)}, u32[]{:S(2)}, u32[]{:S(2)}) %collective-permute-start.3) | collective-permute-done | bytes 155680 | tf_op jit(solution)/shard_map/ppermute | solution.py:446
  179.7 0.0 copy-done.6
  179.7 0.0 copy-done.7
  179.7 0.0 copy-done.8
  179.7 0.0 copy-start.3
  179.7 1.6 copy-done.3
  181.3 17.4 %convolutions.1 = bf16[64,128,128]{2,1,0:T(8,128)(2,1)} custom-call(s32[2]{0:T(128)S(1)} %pad_add_fusion.place_ref, bf16[64,128,128]{2,1,0:T(8,128)(2,1)S(1)} %copy-done.3, bf16[6,128,128]{2,1,0:T(8,128)(2,1)S(1)} %collective-permute-done.1.top_ref, bf16[6,128,128]{2,1,0:T(8,128)(2,1)S(1)} %collective-permute-done.2.bottom_ref, ...), custom_call_target="tpu_custom_call" | custom-call | tf_op jit(solution)/shard_map/convolutions/pallas_call | solution.py:413
  (10 shorter events, 0.2 us)
Async XLA Ops:
  71.6 2.5 %copy-start.9 = (bf16[128,2,64,128]{3,2,1,0:T(8,128)(2,1)}, bf16[128,2,64,128]{3,2,1,0:T(8,128)(2,1)S(1)}, u32[]{:S(2)}) copy-start(bf16[128,2,64,128]{3,2,1,0:T(8,128)(2,1)S(1)} %all_to_all.10) | copy-start | bytes 12582916
  74.3 4.2 %collective-permute-start = (bf16[16,8,64,128]{3,2,1,0:T(8,128)(2,1)S(1)}, bf16[16,8,64,128]{3,2,1,0:T(8,128)(2,1)S(1)}, u32[]{:S(2)}, u32[]{:S(2)}) collective-permute-start(bf16[16,8,64,128]{3,2,1,0:T(8,128)(2,1)S(1)} %slice_bitcast_fusion), channel_id=1, source_target_pairs={{0,8},{8,0},{16,24},{24,16},{32,40},{40,32},{48,56},{56,48},{64,72... | collective-permute-start | bytes 6291464 | tf_op jit(solution)/shard_map/ppermute | solution.py:458
  85.3 8.8 %copy-start.12 = (bf16[64,128]{1,0:T(8,128)(2,1)S(1)}, bf16[64,128]{1,0:T(8,128)(2,1)}, u32[]{:S(2)}) copy-start(bf16[64,128]{1,0:T(8,128)(2,1)} %param.20) | copy-start | bytes 49156
  85.3 8.8 %copy-start.13 = (f32[64]{0:T(128)S(1)}, f32[64]{0:T(128)}, u32[]{:S(2)}) copy-start(f32[64]{0:T(128)} %param.19) | copy-start | bytes 772
  85.3 8.8 %copy-start.14 = (f32[64]{0:T(128)S(1)}, f32[64]{0:T(128)}, u32[]{:S(2)}) copy-start(f32[64]{0:T(128)} %param.18) | copy-start | bytes 772
  85.3 8.9 %copy-start.15 = (f32[128]{0:T(128)S(1)}, f32[128]{0:T(128)}, u32[]{:S(2)}) copy-start(f32[128]{0:T(128)} %param.21) | copy-start | bytes 1540
  85.3 9.6 %copy-start = (bf16[64,128,128]{2,1,0:T(8,128)(2,1)S(1)}, bf16[64,128,128]{2,1,0:T(8,128)(2,1)}, u32[]{:S(2)}) copy-start(bf16[64,128,128]{2,1,0:T(8,128)(2,1)} %pair_ref.5) | copy-start | bytes 6291460
  85.3 9.6 %copy-start.4 = (f32[128]{0:T(128)S(1)}, f32[128]{0:T(128)}, u32[]{:S(2)}) copy-start(f32[128]{0:T(128)} %param.14) | copy-start | bytes 1540
  85.3 9.6 %copy-start.5 = (f32[128]{0:T(128)S(1)}, f32[128]{0:T(128)}, u32[]{:S(2)}) copy-start(f32[128]{0:T(128)} %param.15) | copy-start | bytes 1540
  85.3 58.7 %all-to-all-start.1 = ((bf16[128,2,64,128]{3,2,1,0:T(8,128)(2,1)}), bf16[128,2,64,128]{3,2,1,0:T(8,128)(2,1)}, u32[]{:S(2)}, u32[]{:S(2)}) async-start(bf16[128,2,64,128]{3,2,1,0:T(8,128)(2,1)} %bitcast.33), calls=%async_computation.1 | async-start | bytes 8388608 | tf_op jit(solution)/shard_map/all_to_all | solution.py:460
  94.9 5.4 %copy-start.11 = (bf16[2,9,128,128]{3,2,1,0:T(8,128)(2,1)S(1)}, bf16[2,9,128,128]{3,2,1,0:T(8,128)(2,1)}, u32[]{:S(2)}) copy-start(bf16[2,9,128,128]{3,2,1,0:T(8,128)(2,1)} %param.24) | copy-start | bytes 1769476
  98.4 2.0 copy-start.1
  154.0 17.6 %copy-start.2 = (bf16[64,128,128]{2,1,0:T(8,128)(2,1)}, bf16[64,128,128]{2,1,0:T(8,128)(2,1)S(1)}, u32[]{:S(2)}) copy-start(bf16[64,128,128]{2,1,0:T(8,128)(2,1)S(1)} %update.1.sym_ref) | copy-start | bytes 6291460
  154.0 17.4 %copy-start.10 = (bf16[4,384,256]{2,1,0:T(8,128)(2,1)S(1)}, bf16[4,384,256]{2,1,0:T(8,128)(2,1)}, u32[]{:S(2)}) copy-start(bf16[4,384,256]{2,1,0:T(8,128)(2,1)} %fusion.5) | copy-start | bytes 2359300
  154.0 9.5 %collective-permute-start.1 = (bf16[6,128,128]{2,1,0:T(8,128)(2,1)S(1)}, bf16[6,128,128]{2,1,0:T(8,128)(2,1)S(1)}, u32[]{:S(2)}, u32[]{:S(2)}) collective-permute-start(bf16[6,128,128]{2,1,0:T(8,128)(2,1)S(1)} %get-tuple-element.8), channel_id=1, source_target_pairs={{0,8},{8,16},{16,24},{24,32},{32,40},{40,48},{48,56},{56,64},{64,7... | collective-permute-start | bytes 589832 | tf_op jit(solution)/shard_map/ppermute | solution.py:446
  156.1 9.2 %collective-permute-start.2 = (bf16[6,128,128]{2,1,0:T(8,128)(2,1)S(1)}, bf16[6,128,128]{2,1,0:T(8,128)(2,1)S(1)}, u32[]{:S(2)}, u32[]{:S(2)}) collective-permute-start(bf16[6,128,128]{2,1,0:T(8,128)(2,1)S(1)} %get-tuple-element.7), channel_id=1, source_target_pairs={{8,0},{16,8},{24,16},{32,24},{40,32},{48,40},{56,48},{64,56},{72,6... | collective-permute-start | bytes 589832 | tf_op jit(solution)/shard_map/ppermute | solution.py:446
  165.4 8.1 %collective-permute-start.4 = (bf16[76,8,128]{2,1,0:T(8,128)(2,1)S(1)}, bf16[76,8,128]{2,1,0:T(8,128)(2,1)S(1)}, u32[]{:S(2)}, u32[]{:S(2)}) collective-permute-start(bf16[76,8,128]{2,1,0:T(8,128)(2,1)S(1)} %pad_maximum_fusion.2), channel_id=1, source_target_pairs={{1,0},{2,1},{3,2},{4,3},{5,4},{6,5},{7,6},{9,8},{10,9},{11,10},{12... | collective-permute-start | bytes 466952 | tf_op jit(solution)/shard_map/ppermute | solution.py:446
  169.5 10.2 %collective-permute-start.3 = (bf16[76,8,128]{2,1,0:T(8,128)(2,1)S(1)}, bf16[76,8,128]{2,1,0:T(8,128)(2,1)S(1)}, u32[]{:S(2)}, u32[]{:S(2)}) collective-permute-start(bf16[76,8,128]{2,1,0:T(8,128)(2,1)S(1)} %pad_maximum_fusion.1), channel_id=1, source_target_pairs={{0,1},{1,2},{2,3},{3,4},{4,5},{5,6},{6,7},{8,9},{9,10},{10,11},{11... | collective-permute-start | bytes 466952 | tf_op jit(solution)/shard_map/ppermute | solution.py:446
  171.4 8.3 %copy-start.6 = (f32[2,128]{1,0:T(2,128)S(1)}, f32[2,128]{1,0:T(2,128)}, u32[]{:S(2)}) copy-start(f32[2,128]{1,0:T(2,128)} %gain_ref.1) | copy-start | bytes 3076
  171.4 8.3 %copy-start.7 = (f32[2,128]{1,0:T(2,128)S(1)}, f32[2,128]{1,0:T(2,128)}, u32[]{:S(2)}) copy-start(f32[2,128]{1,0:T(2,128)} %shift_ref.1) | copy-start | bytes 3076
  171.5 8.3 %copy-start.8 = (f32[2,128]{1,0:T(2,128)S(1)}, f32[2,128]{1,0:T(2,128)}, u32[]{:S(2)}) copy-start(f32[2,128]{1,0:T(2,128)} %bias_ref.1) | copy-start | bytes 3076
  179.7 1.6 copy-start.3

commit v3 on v2

--- a/solution.py
+++ b/solution.py
@@ -33,16 +33,37 @@
 STEP = 16
 
 
-def factor_kernel(pair_ref, gain_ref, shift_ref, weight_ref, bias_ref, out_ref, lay_ref):
+def factor_kernel(
+    pair_ref, gain_ref, shift_ref, weight_ref, bias_ref, out_ref, lay_ref, stage_ref, cells_ref,
+    cell_sems, stage_sems,
+):
     step = pl.program_id(0)
-    block = pair_ref[...]
-    cells = block.astype(F32).reshape(STEP * COLS, CH)
+
+    def cell_copy(k):
+        return pltpu.make_async_copy(
+            cells_ref.at[k], out_ref.at[pl.ds(2 * k, 2), :, :, :, 1], cell_sems.at[k]
+        )
+
+    def stage_copy(k):
+        start = pl.multiple_of(k * STEP, STEP)
+        return pltpu.make_async_copy(
+            stage_ref.at[k], out_ref.at[:, :, :, :, 0, pl.ds(start, STEP), :], stage_sems.at[k]
+        )
+
+    for row in range(STEP):
+        for q in range(2):
+            for half in range(2):
+                start = half * 64 + q * 32
+                cells_ref[
+                    step, row // 8, (row // 4) % 2, row % 4, q, half * 32 : half * 32 + 32, :
+                ] = pair_ref[row, start : start + 32, :]
+    cell_copy(step).start()
+    cells = pair_ref[...].astype(F32).reshape(STEP * COLS, CH)
     normed = normalize(cells, gain_ref[...], shift_ref[...]).astype(BF)
     bias = jnp.transpose(jnp.broadcast_to(bias_ref[:, : 4 * HID], (COLS, 4 * HID)))
     projected = lax.dot_general(
         weight_ref[:, : 4 * HID], normed, (((0,), (1,)), ((), ())), preferred_element_type=F32
     )
-    start = pl.multiple_of(step * STEP, STEP)
     for side in range(2):
         base = 2 * HID * side
         for row in range(STEP):
@@ -50,19 +71,14 @@
             gate = projected[base : base + HID, part] + bias[base : base + HID]
             value = projected[base + HID : base + 2 * HID, part] + bias[base + HID : base + 2 * HID]
             lay_ref[pl.ds(row, HID, stride=STEP), :] = sigmoid(gate) * value
-        out_ref[:, side, :, 0, pl.ds(start, STEP), :] = (
-            lay_ref[...].astype(BF).reshape(8, 8, STEP, COLS)
-        )
-    for row in range(STEP):
-        for q in range(2):
-            local = 2 * row + q
-            group = step * 2 + local // 16
-            side = (local // 8) % 2
-            column = local % 8
-            for half in range(2):
-                out_ref[group, side, column, 1, half * 32 : half * 32 + 32, :] = pair_ref[
-                    row, half * 64 + q * 32 : half * 64 + q * 32 + 32, :
-                ]
+        stage_ref[step, :, side] = lay_ref[...].astype(BF).reshape(8, 4, 2, STEP, COLS)
+    stage_copy(step).start()
+
+    @pl.when(step == ROWS // STEP - 1)
+    def _():
+        for k in range(ROWS // STEP):
+            cell_copy(k).wait()
+            stage_copy(k).wait()
 
 
 FACTORS_VMEM = 60
@@ -70,10 +86,11 @@
 
 def factors(pair, gain, shift, weight, bias):
     whole = lambda *shape: pl.BlockSpec(shape, lambda s: (0,) * len(shape))
+    steps = ROWS // STEP
     return pl.pallas_call(
         factor_kernel,
-        grid=(ROWS // STEP,),
-        out_shape=jax.ShapeDtypeStruct((8, 2, 8, 2, ROWS, COLS), BF),
+        grid=(steps,),
+        out_shape=jax.ShapeDtypeStruct((8, 2, 4, 2, 2, ROWS, COLS), BF),
         in_specs=[
             pl.BlockSpec((STEP, COLS, CH), lambda s: (s, 0, 0)),
             whole(1, CH),
@@ -81,58 +98,149 @@
             whole(CH, 4 * HID + CH),
             whole(1, 4 * HID + CH),
         ],
-        out_specs=whole(8, 2, 8, 2, ROWS, COLS),
-        scratch_shapes=[pltpu.VMEM((HID * STEP, COLS), F32)],
+        out_specs=pl.BlockSpec(memory_space=pl.ANY),
+        scratch_shapes=[
+            pltpu.VMEM((HID * STEP, COLS), F32),
+            pltpu.VMEM((steps, 8, 2, 4, 2, STEP, COLS), BF),
+            pltpu.VMEM((steps, 2, 2, 4, 2, ROWS, COLS), BF),
+            pltpu.SemaphoreType.DMA((steps,)),
+            pltpu.SemaphoreType.DMA((steps,)),
+        ],
         compiler_params=pltpu.CompilerParams(vmem_limit_bytes=FACTORS_VMEM * MIB),
         name="factors",
     )(pair, gain, shift, weight, bias)
 
 
-def product_kernel(own_ref, moved_ref, other_ref, out_ref, rhs_ref):
-    for col in range(NC):
-        rhs_ref[:, col * COLS : (col + 1) * COLS] = other_ref[:, col].reshape(NR * ROWS, COLS)
+def plane_kernel(received_ref, out_ref, hold_ref, in_sems, out_sems):
+    parts = [slice(k * NR // 4, (k + 1) * NR // 4) for k in range(4)]
+    inward = [
+        pltpu.make_async_copy(received_ref.at[part, :, 0], hold_ref.at[part], in_sems.at[k])
+        for k, part in enumerate(parts)
+    ]
+    outward = [
+        pltpu.make_async_copy(hold_ref.at[part], out_ref.at[part], out_sems.at[k])
+        for k, part in enumerate(parts)
+    ]
+    for copy in inward:
+        copy.start()
+    for k in range(4):
+        inward[k].wait()
+        outward[k].start()
+    for copy in outward:
+        copy.wait()
+
+
+def plane(received):
+    return pl.pallas_call(
+        plane_kernel,
+        out_shape=jax.ShapeDtypeStruct((NR, NC, ROWS, COLS), BF),
+        in_specs=[pl.BlockSpec(memory_space=pl.ANY)],
+        out_specs=pl.BlockSpec(memory_space=pl.ANY),
+        scratch_shapes=[
+            pltpu.VMEM((NR, NC, ROWS, COLS), BF),
+            pltpu.SemaphoreType.DMA((4,)),
+            pltpu.SemaphoreType.DMA((4,)),
+        ],
+        compiler_params=pltpu.CompilerParams(vmem_limit_bytes=PLANE_VMEM * MIB),
+        name="plane",
+    )(received)
+
+
+PLANE_VMEM = 60
+PRODUCT_VMEM = 60
+
+
+def product_kernel(
+    received_ref, other_ref, out_ref, lhs_ref, rhs_ref, result_ref, cells_ref,
+    lhs_sems, rhs_sems, cell_sems, out_sems, cell_out_sem,
+):
     half = NR // 2
-    for part in range(2):
-        lhs = jnp.concatenate(
-            [
-                own_ref[part * half : (part + 1) * half, col, 0].reshape(half * ROWS, COLS)
-                for col in range(NC)
-            ],
-            axis=1,
-        )
+
+    def columns(col):
+        return slice(col * COLS, (col + 1) * COLS)
+
+    lhs = [
+        pltpu.make_async_copy(
+            received_ref.at[:, side, col, 0],
+            lhs_ref.at[side, :, :, columns(col)],
+            lhs_sems.at[side, col],
+        )
+        for side in range(2)
+        for col in range(NC)
+    ]
+    rhs = [
+        pltpu.make_async_copy(
+            other_ref.at[:, col], rhs_ref.at[:, :, columns(col)], rhs_sems.at[col]
+        )
+        for col in range(NC)
+    ]
+    cells = [
+        pltpu.make_async_copy(
+            received_ref.at[col, e, :, 1, side * 32 : side * 32 + 32, :],
+            cells_ref.at[:, side, col, e * 32 : e * 32 + 32, :],
+            cell_sems.at[col, e, side],
+        )
+        for col in range(NC)
+        for e in range(2)
+        for side in range(2)
+    ]
+    for copy in rhs + lhs + cells:
+        copy.start()
+    for copy in rhs:
+        copy.wait()
+    outs = []
+    for side in range(2):
+        for copy in lhs[side * NC : side * NC + NC]:
+            copy.wait()
+        own = lhs_ref[side].reshape(half * ROWS, NC * COLS)
         for block in range(4):
             result = lax.dot_general(
-                lhs,
-                rhs_ref[block * 256 : (block + 1) * 256, :],
+                own,
+                rhs_ref[4 * block : 4 * block + 4].reshape(256, NC * COLS),
                 NT,
                 preferred_element_type=F32,
             ).astype(BF)
             for col in range(2):
-                out_ref[part * half : (part + 1) * half, block * 2 + col, 0] = result[
-                    :, col * COLS : (col + 1) * COLS
-                ].reshape(half, ROWS, COLS)
-    for row in range(NR):
-        for col in range(NC):
-            side = row % 2
-            for e in range(2):
-                out_ref[row, col, 1, e * 32 : e * 32 + 32, :] = moved_ref[
-                    2 * col + e, row // 2, 0, side * 32 : side * 32 + 32, :
-                ]
+                result_ref[side, :, block * 2 + col] = result[:, columns(col)].reshape(
+                    half, ROWS, COLS
+                )
+        copy = pltpu.make_async_copy(
+            result_ref.at[side], out_ref.at[:, side, :, 0], out_sems.at[side]
+        )
+        copy.start()
+        outs.append(copy)
+        if side == 0:
+            for moved in cells:
+                moved.wait()
+            copy = pltpu.make_async_copy(cells_ref, out_ref.at[:, :, :, 1], cell_out_sem)
+            copy.start()
+            outs.append(copy)
+    for copy in outs:
+        copy.wait()
 
 
 def product(received, other):
-    whole = lambda *shape: pl.BlockSpec(shape, lambda s: (0,) * len(shape))
-    slot = lambda k: pl.BlockSpec((NR, NC, 1, ROWS, COLS), lambda s: (0, 0, k, 0, 0))
+    anywhere = pl.BlockSpec(memory_space=pl.ANY)
+    half = NR // 2
     return pl.pallas_call(
         product_kernel,
-        grid=(1,),
-        out_shape=jax.ShapeDtypeStruct((NR, NC, 2, ROWS, COLS), BF),
-        in_specs=[slot(0), slot(1), whole(NR, NC, ROWS, COLS)],
-        out_specs=whole(NR, NC, 2, ROWS, COLS),
-        scratch_shapes=[pltpu.VMEM((NR * ROWS, NC * COLS), BF)],
-        compiler_params=pltpu.CompilerParams(vmem_limit_bytes=48 * MIB),
+        out_shape=jax.ShapeDtypeStruct((half, 2, NC, 2, ROWS, COLS), BF),
+        in_specs=[anywhere, anywhere],
+        out_specs=anywhere,
+        scratch_shapes=[
+            pltpu.VMEM((2, half, ROWS, NC * COLS), BF),
+            pltpu.VMEM((NR, ROWS, NC * COLS), BF),
+            pltpu.VMEM((2, half, NC, ROWS, COLS), BF),
+            pltpu.VMEM((half, 2, NC, ROWS, COLS), BF),
+            pltpu.SemaphoreType.DMA((2, NC)),
+            pltpu.SemaphoreType.DMA((NC,)),
+            pltpu.SemaphoreType.DMA((NC, 2, 2)),
+            pltpu.SemaphoreType.DMA((2,)),
+            pltpu.SemaphoreType.DMA(()),
+        ],
+        compiler_params=pltpu.CompilerParams(vmem_limit_bytes=PRODUCT_VMEM * MIB),
         name="product",
-    )(received, received, other)
+    )(received.reshape(half, 2, NC, 2, ROWS, COLS), other)
 
 
 def gate_kernel(pair_ref, gain_ref, shift_ref, weight_ref, bias_ref, out_ref):
@@ -261,6 +369,7 @@
 FIRST_TALL = ROWS + 2 * SECOND_DILATION
 GROUP_A, GROUP_B, GROUP_C = 4, 4, 8
 UNROLL_A, UNROLL_B = 2, 6
+CONV_VMEM = 62
 
 
 def convolution_kernel(
@@ -427,7 +536,7 @@
             pltpu.SemaphoreType.DMA((7,)),
             pltpu.SemaphoreType.DMA((4,)),
         ],
-        compiler_params=pltpu.CompilerParams(vmem_limit_bytes=44 * MIB),
+        compiler_params=pltpu.CompilerParams(vmem_limit_bytes=CONV_VMEM * MIB),
         name="convolutions",
     )(place, sym, top, bottom, low, high, gain, shift, bias, weight)
 
@@ -451,11 +560,11 @@
     conv_gain, conv_shift, convolution_weight, convolution_bias,
 ):
     gain, shift = norm_gain[None], norm_shift[None]
-    sent = factors(pair, gain, shift, proj_weight, proj_bias[None])
+    sent = factors(pair, gain, shift, proj_weight, proj_bias.reshape(1, 4 * HID + CH))
     received = lax.all_to_all(
         sent.reshape(128, 2, ROWS, COLS), ("row", "col"), split_axis=0, concat_axis=0, tiled=True
     ).reshape(NR, NC, 2, ROWS, COLS)
-    other = lax.ppermute(received[:, :, 0], "row", [(i, i ^ 1) for i in range(NR)])
+    other = lax.ppermute(plane(received), "row", [(i, i ^ 1) for i in range(NR)])
     back = product(received, other)
     returned = lax.all_to_all(
         back.reshape(128, 2, ROWS, COLS), ("row", "col"), split_axis=0, concat_axis=0, tiled=True

time: 200 us -> 199 us (level)
  local copies, waits for them, and re-layouts: 9.17 us -> 6.84 us
    pallas_call x2 -> x3, Pallas kernels: 15.7 us -> 16.2 us  [the longest x1 7.74 us: factors(): pl.pallas_call(factor_kernel, grid=(steps,), out_shape=jax.ShapeDtypeStru...]
  transfers between devices with their start and end apart: 6 -> 6, of which waited for: 6 -> 6; matrix products, arithmetic and copies ran while one was open for 1% -> 2% of each run, Pallas kernels for 2% -> 2%
where the time goes in v3:
time: 199 us; the launch traced here: 198 us
  blocking collectives  61.5 us (31%)
  waiting for transfers between devices  56.4 us (28%)
  Pallas kernels  47.7 us (24%)
  starting transfers between devices  22.2 us (11%)
  local copies, waits for them, and re-layouts  6.84 us (3%)
  other arithmetic  3.08 us (2%)
    all_to_all x1, blocking collectives, local(): lax.all_to_all(sent.reshape(128, 2, ROWS, COLS), ('row', 'col'), split_ax...  61.5 us
    all_to_all x1, waiting for transfers between devices, local(): lax.all_to_all(back.reshape(128, 2, ROWS, COLS), ('row', 'col'), split_ax...  42.6 us
    pallas_call x1, Pallas kernels, convolutions(): pl.pallas_call(convolution_kernel, out_shape=jax.ShapeDtypeStruct((ROWS,...  18.2 us
    ppermute x2, starting transfers between devices, neighbours(): lax.ppermute(low_strip, axis, backward)  10.1 us
    pallas_call x1, Pallas kernels, update(): pl.pallas_call(update_kernel, grid=(ROWS // USTEP,), out_shape=jax.ShapeD...  9.95 us
    all_to_all x1, starting transfers between devices, local(): lax.all_to_all(back.reshape(128, 2, ROWS, COLS), ('row', 'col'), split_ax...  7.98 us
    pallas_call x1, Pallas kernels, factors(): pl.pallas_call(factor_kernel, grid=(steps,), out_shape=jax.ShapeDtypeStru...  7.74 us
    ppermute x2, waiting for transfers between devices, neighbours(): lax.ppermute(high_strip, axis, forward)  7.62 us
  transfers between devices with their start and end apart: 6, of which 6 were waited for; matrix products, arithmetic and copies ran while one was open for 2% of the time, Pallas kernels for 2%

profile of v3, /device:TPU:10, one launch (start us, length us, event | category | flops | bytes accessed | tf_op | source)
XLA Modules:
  0.0 198.2 jit_solution(15468821062251032837)
XLA Ops:
  0.0 1.2 reshape.23.bias_ref
  1.2 7.7 %factors.1 = bf16[8,2,4,2,2,64,128]{6,5,4,3,2,1,0:T(8,128)(2,1)} custom-call(bf16[64,128,128]{2,1,0:T(8,128)(2,1)} %pair_ref.5, f32[1,128]{1,0:T(1,128)} %bitcast.22, f32[1,128]{1,0:T(1,128)} %bitcast.25, bf16[128,384]{1,0:T(8,128)(2,1)} %weight_ref.1, f32[1,384]{1,0:T(1,128)} %reshape.23.bias_ref), custom_call_target="tpu_custom_call" | custom-call | tf_op jit(solution)/shard_map/factors/pallas_call | solution.py:90
  9.0 61.5 %all_to_all.10 = bf16[128,2,64,128]{3,2,1,0:T(8,128)(2,1)} all-to-all(bf16[128,2,64,128]{3,2,1,0:T(8,128)(2,1)} %bitcast.32), channel_id=1, replica_groups=mesh['row'=16,'col'=8] {'row','col'}, dimensions={0} | all-to-all | bytes 8388608 | tf_op jit(solution)/shard_map/all_to_all | solution.py:564
  70.5 2.4 %plane.1 = bf16[16,8,64,128]{3,2,1,0:T(8,128)(2,1)} custom-call(bf16[16,8,2,64,128]{4,3,2,1,0:T(8,128)(2,1)} %bitcast.29), custom_call_target="tpu_custom_call" | custom-call | tf_op jit(solution)/shard_map/plane/pallas_call | solution.py:134
  72.9 0.1 collective-permute-start
  73.0 4.4 %collective-permute-done.other_ref = bf16[16,8,64,128]{3,2,1,0:T(8,128)(2,1)S(1)} collective-permute-done((bf16[16,8,64,128]{3,2,1,0:T(8,128)(2,1)}, bf16[16,8,64,128]{3,2,1,0:T(8,128)(2,1)S(1)}, u32[]{:S(2)}, u32[]{:S(2)}) %collective-permute-start) | collective-permute-done | bytes 2097184 | tf_op jit(solution)/shard_map/ppermute | solution.py:567
  77.4 0.0 copy-start.6
  77.4 1.3 copy-done.6
  78.7 6.0 %product.1 = bf16[8,2,8,2,64,128]{5,4,3,2,1,0:T(8,128)(2,1)} custom-call(bf16[8,2,8,2,64,128]{5,4,3,2,1,0:T(8,128)(2,1)} %bitcast.30, bf16[16,8,64,128]{3,2,1,0:T(8,128)(2,1)} %copy-done.6), custom_call_target="tpu_custom_call" | custom-call | tf_op jit(solution)/shard_map/product/pallas_call | solution.py:225
  84.7 0.0 copy-start.12
  84.7 0.0 copy-start.13
  84.7 0.0 copy-start.14
  84.7 0.0 copy-start.15
  84.7 0.0 copy-start
  84.8 0.0 copy-start.3
  84.8 0.0 copy-start.4
  84.8 8.0 %all-to-all-start.1 = ((bf16[128,2,64,128]{3,2,1,0:T(8,128)(2,1)}), bf16[128,2,64,128]{3,2,1,0:T(8,128)(2,1)}, u32[]{:S(2)}, u32[]{:S(2)}) async-start(bf16[128,2,64,128]{3,2,1,0:T(8,128)(2,1)} %bitcast.31), calls=%async_computation.1 | async-start | bytes 8388608 | tf_op jit(solution)/shard_map/all_to_all | solution.py:569
  92.8 0.8 slice.36.weight_ref.gate_ref
  93.5 0.0 copy-done.12
  93.5 0.0 copy-done.13
  93.5 0.0 copy-done.14
  93.5 0.1 fusion.10
  93.6 0.0 copy-done.15
  93.7 0.7 slice_bitcast_fusion.bias_ref.gate_bias_ref
  94.3 0.0 copy-done
  94.3 0.0 copy-done.3
  94.4 0.0 copy-done.4
  94.4 0.0 copy-start.7
  94.4 3.4 %gates.1.own_gate_ref = f32[64,128,128]{2,1,0:T(8,128)S(1)} custom-call(bf16[64,128,128]{2,1,0:T(8,128)(2,1)S(1)} %copy-done, f32[1,128]{1,0:T(1,128)S(1)} %bitcast.23, f32[1,128]{1,0:T(1,128)S(1)} %bitcast.26, bf16[128,128]{1,0:T(8,128)(2,1)S(1)} %slice.36.weight_ref.gate_ref, f32[1,128]{1,0:T(1,128)S(1)} %slice_bitcast_fusion.bias_ref.gate_bias_ref), custom_call_target="tpu_custom_call" | custom-call | flops 268435456 | bytes 6291456 | tf_op jit(solution)/shard_map/gates/pallas_call | solution.py:256
  97.8 0.0 copy-start.1
  97.8 2.0 copy-done.1
  99.8 0.0 copy-done.7
  99.9 0.1 fusion.4
  99.9 0.9 fusion.5
  100.9 42.6 %all-to-all-done.1.mirror_ref = bf16[128,2,64,128]{3,2,1,0:T(8,128)(2,1)} async-done(((bf16[128,2,64,128]{3,2,1,0:T(8,128)(2,1)}), bf16[128,2,64,128]{3,2,1,0:T(8,128)(2,1)}, u32[]{:S(2)}, u32[]{:S(2)}) %all-to-all-start.1) | async-done | bytes 4194336 | tf_op jit(solution)/shard_map/all_to_all | solution.py:569
  143.5 9.9 %update.1.sym_ref = bf16[64,128,128]{2,1,0:T(8,128)(2,1)S(1)} custom-call(bf16[64,128,128]{2,1,0:T(8,128)(2,1)S(1)} %copy-done, f32[64,128,128]{2,1,0:T(8,128)} %copy-done.1, bf16[8,2,8,2,64,128]{5,4,3,2,1,0:T(8,128)(2,1)} %bitcast.9.tri_ref, bf16[128,2,64,128]{3,2,1,0:T(8,128)(2,1)} %all-to-all-done.1.mirror_ref, f32[1,128]{1,0:T(1,128)S(1)} %bitcast.24, ...), custom_call_target="tpu_custom_call" | custom-call | tf_op jit(solution)/shard_map/update/pallas_call | solution.py:330
  153.4 0.0 copy-start.2
  153.4 0.0 copy-start.5
  153.5 2.1 %collective-permute-start.1 = (bf16[6,128,128]{2,1,0:T(8,128)(2,1)S(1)}, bf16[6,128,128]{2,1,0:T(8,128)(2,1)S(1)}, u32[]{:S(2)}, u32[]{:S(2)}) collective-permute-start(bf16[6,128,128]{2,1,0:T(8,128)(2,1)S(1)} %get-tuple-element.8), channel_id=1, source_target_pairs={{0,8},{8,16},{16,24},{24,32},{32,40},{40,48},{48,56},{56,64},{64,7... | collective-permute-start | bytes 589832 | tf_op jit(solution)/shard_map/ppermute | solution.py:555
  155.5 6.0 %collective-permute-start.2 = (bf16[6,128,128]{2,1,0:T(8,128)(2,1)S(1)}, bf16[6,128,128]{2,1,0:T(8,128)(2,1)S(1)}, u32[]{:S(2)}, u32[]{:S(2)}) collective-permute-start(bf16[6,128,128]{2,1,0:T(8,128)(2,1)S(1)} %get-tuple-element.7), channel_id=1, source_target_pairs={{8,0},{16,8},{24,16},{32,24},{40,32},{48,40},{56,48},{64,56},{72,6... | collective-permute-start | bytes 589832 | tf_op jit(solution)/shard_map/ppermute | solution.py:555
  161.6 1.4 collective-permute-done.1.top_ref
  163.0 0.0 copy-start.8
  163.0 1.7 collective-permute-done.2.bottom_ref
  164.7 0.0 copy-start.9
  164.8 4.1 %collective-permute-start.4 = (bf16[76,8,128]{2,1,0:T(8,128)(2,1)S(1)}, bf16[76,8,128]{2,1,0:T(8,128)(2,1)S(1)}, u32[]{:S(2)}, u32[]{:S(2)}) collective-permute-start(bf16[76,8,128]{2,1,0:T(8,128)(2,1)S(1)} %pad_maximum_fusion.2), channel_id=1, source_target_pairs={{1,0},{2,1},{3,2},{4,3},{5,4},{6,5},{7,6},{9,8},{10,9},{11,10},{12... | collective-permute-start | bytes 466952 | tf_op jit(solution)/shard_map/ppermute | solution.py:555
  168.9 1.9 collective-permute-start.3
  170.8 0.0 copy-done.5
  170.8 1.3 pad_maximum_fusion.weight_hbm
  172.1 0.0 copy-done.2
  172.1 0.0 copy-done.8
  172.1 0.0 copy-done.9
  172.1 0.6 pad_add_fusion.place_ref
  172.8 0.1 collective-permute-done.4.high_ref
  172.9 0.0 copy-start.10
  172.9 6.3 %collective-permute-done.3.low_ref = bf16[76,8,128]{2,1,0:T(8,128)(2,1)S(1)} collective-permute-done((bf16[76,8,128]{2,1,0:T(8,128)(2,1)S(1)}, bf16[76,8,128]{2,1,0:T(8,128)(2,1)S(1)}, u32[]{:S(2)}, u32[]{:S(2)}) %collective-permute-start.3) | collective-permute-done | bytes 155680 | tf_op jit(solution)/shard_map/ppermute | solution.py:555
  179.1 0.0 copy-done.10
  179.1 0.0 copy-start.11
  179.1 0.7 copy-done.11
  179.8 18.2 %convolutions.1 = bf16[64,128,128]{2,1,0:T(8,128)(2,1)} custom-call(s32[2]{0:T(128)} %pad_add_fusion.place_ref, bf16[64,128,128]{2,1,0:T(8,128)(2,1)} %copy-done.2, bf16[6,128,128]{2,1,0:T(8,128)(2,1)} %copy-done.8, bf16[6,128,128]{2,1,0:T(8,128)(2,1)} %copy-done.9, bf16[76,8,128]{2,1,0:T(8,128)(2,1)} %copy-done.11, bf16[76,8,128]{2,1,0:T(8,128)(2,1)} %copy-done.10, ...), custom_call_target="tpu_custom_call" | custom-call | tf_op jit(solution)/shard_map/convolutions/pallas_call | solution.py:522
  (10 shorter events, 0.2 us)
Async XLA Ops:
  72.9 4.5 %collective-permute-start = (bf16[16,8,64,128]{3,2,1,0:T(8,128)(2,1)}, bf16[16,8,64,128]{3,2,1,0:T(8,128)(2,1)S(1)}, u32[]{:S(2)}, u32[]{:S(2)}) collective-permute-start(bf16[16,8,64,128]{3,2,1,0:T(8,128)(2,1)} %plane.1), channel_id=1, source_target_pairs={{0,8},{8,0},{16,24},{24,16},{32,40},{40,32},{48,56},{56,48},{64,72... | collective-permute-start | bytes 6291464 | tf_op jit(solution)/shard_map/ppermute | solution.py:567
  77.4 1.3 copy-start.6
  84.7 8.8 %copy-start.12 = (bf16[64,128]{1,0:T(8,128)(2,1)S(1)}, bf16[64,128]{1,0:T(8,128)(2,1)}, u32[]{:S(2)}) copy-start(bf16[64,128]{1,0:T(8,128)(2,1)} %param.20) | copy-start | bytes 49156
  84.7 8.8 %copy-start.13 = (f32[64]{0:T(128)S(1)}, f32[64]{0:T(128)}, u32[]{:S(2)}) copy-start(f32[64]{0:T(128)} %param.19) | copy-start | bytes 772
  84.7 8.8 %copy-start.14 = (f32[64]{0:T(128)S(1)}, f32[64]{0:T(128)}, u32[]{:S(2)}) copy-start(f32[64]{0:T(128)} %param.18) | copy-start | bytes 772
  84.7 8.9 %copy-start.15 = (f32[128]{0:T(128)S(1)}, f32[128]{0:T(128)}, u32[]{:S(2)}) copy-start(f32[128]{0:T(128)} %param.21) | copy-start | bytes 1540
  84.7 9.6 %copy-start = (bf16[64,128,128]{2,1,0:T(8,128)(2,1)S(1)}, bf16[64,128,128]{2,1,0:T(8,128)(2,1)}, u32[]{:S(2)}) copy-start(bf16[64,128,128]{2,1,0:T(8,128)(2,1)} %pair_ref.5) | copy-start | bytes 6291460
  84.8 9.6 %copy-start.3 = (f32[128]{0:T(128)S(1)}, f32[128]{0:T(128)}, u32[]{:S(2)}) copy-start(f32[128]{0:T(128)} %param.14) | copy-start | bytes 1540
  84.8 9.6 %copy-start.4 = (f32[128]{0:T(128)S(1)}, f32[128]{0:T(128)}, u32[]{:S(2)}) copy-start(f32[128]{0:T(128)} %param.15) | copy-start | bytes 1540
  84.8 58.7 %all-to-all-start.1 = ((bf16[128,2,64,128]{3,2,1,0:T(8,128)(2,1)}), bf16[128,2,64,128]{3,2,1,0:T(8,128)(2,1)}, u32[]{:S(2)}, u32[]{:S(2)}) async-start(bf16[128,2,64,128]{3,2,1,0:T(8,128)(2,1)} %bitcast.31), calls=%async_computation.1 | async-start | bytes 8388608 | tf_op jit(solution)/shard_map/all_to_all | solution.py:569
  94.4 5.4 %copy-start.7 = (bf16[2,9,128,128]{3,2,1,0:T(8,128)(2,1)S(1)}, bf16[2,9,128,128]{3,2,1,0:T(8,128)(2,1)}, u32[]{:S(2)}) copy-start(bf16[2,9,128,128]{3,2,1,0:T(8,128)(2,1)} %param.24) | copy-start | bytes 1769476
  97.8 2.0 copy-start.1
  153.4 18.7 %copy-start.2 = (bf16[64,128,128]{2,1,0:T(8,128)(2,1)}, bf16[64,128,128]{2,1,0:T(8,128)(2,1)S(1)}, u32[]{:S(2)}) copy-start(bf16[64,128,128]{2,1,0:T(8,128)(2,1)S(1)} %update.1.sym_ref) | copy-start | bytes 6291460
  153.4 17.4 %copy-start.5 = (bf16[4,384,256]{2,1,0:T(8,128)(2,1)S(1)}, bf16[4,384,256]{2,1,0:T(8,128)(2,1)}, u32[]{:S(2)}) copy-start(bf16[4,384,256]{2,1,0:T(8,128)(2,1)} %fusion.5) | copy-start | bytes 2359300
  153.5 9.5 %collective-permute-start.1 = (bf16[6,128,128]{2,1,0:T(8,128)(2,1)S(1)}, bf16[6,128,128]{2,1,0:T(8,128)(2,1)S(1)}, u32[]{:S(2)}, u32[]{:S(2)}) collective-permute-start(bf16[6,128,128]{2,1,0:T(8,128)(2,1)S(1)} %get-tuple-element.8), channel_id=1, source_target_pairs={{0,8},{8,16},{16,24},{24,32},{32,40},{40,48},{48,56},{56,64},{64,7... | collective-permute-start | bytes 589832 | tf_op jit(solution)/shard_map/ppermute | solution.py:555
  155.5 9.2 %collective-permute-start.2 = (bf16[6,128,128]{2,1,0:T(8,128)(2,1)S(1)}, bf16[6,128,128]{2,1,0:T(8,128)(2,1)S(1)}, u32[]{:S(2)}, u32[]{:S(2)}) collective-permute-start(bf16[6,128,128]{2,1,0:T(8,128)(2,1)S(1)} %get-tuple-element.7), channel_id=1, source_target_pairs={{8,0},{16,8},{24,16},{32,24},{40,32},{48,40},{56,48},{64,56},{72,6... | collective-permute-start | bytes 589832 | tf_op jit(solution)/shard_map/ppermute | solution.py:555
  163.0 9.1 %copy-start.8 = (bf16[6,128,128]{2,1,0:T(8,128)(2,1)}, bf16[6,128,128]{2,1,0:T(8,128)(2,1)S(1)}, u32[]{:S(2)}) copy-start(bf16[6,128,128]{2,1,0:T(8,128)(2,1)S(1)} %collective-permute-done.1.top_ref) | copy-start | bytes 589828
  164.7 7.4 %copy-start.9 = (bf16[6,128,128]{2,1,0:T(8,128)(2,1)}, bf16[6,128,128]{2,1,0:T(8,128)(2,1)S(1)}, u32[]{:S(2)}) copy-start(bf16[6,128,128]{2,1,0:T(8,128)(2,1)S(1)} %collective-permute-done.2.bottom_ref) | copy-start | bytes 589828
  164.8 8.1 %collective-permute-start.4 = (bf16[76,8,128]{2,1,0:T(8,128)(2,1)S(1)}, bf16[76,8,128]{2,1,0:T(8,128)(2,1)S(1)}, u32[]{:S(2)}, u32[]{:S(2)}) collective-permute-start(bf16[76,8,128]{2,1,0:T(8,128)(2,1)S(1)} %pad_maximum_fusion.2), channel_id=1, source_target_pairs={{1,0},{2,1},{3,2},{4,3},{5,4},{6,5},{7,6},{9,8},{10,9},{11,10},{12... | collective-permute-start | bytes 466952 | tf_op jit(solution)/shard_map/ppermute | solution.py:555
  168.9 10.2 %collective-permute-start.3 = (bf16[76,8,128]{2,1,0:T(8,128)(2,1)S(1)}, bf16[76,8,128]{2,1,0:T(8,128)(2,1)S(1)}, u32[]{:S(2)}, u32[]{:S(2)}) collective-permute-start(bf16[76,8,128]{2,1,0:T(8,128)(2,1)S(1)} %pad_maximum_fusion.1), channel_id=1, source_target_pairs={{0,1},{1,2},{2,3},{3,4},{4,5},{5,6},{6,7},{8,9},{9,10},{10,11},{11... | collective-permute-start | bytes 466952 | tf_op jit(solution)/shard_map/ppermute | solution.py:555
  172.9 6.3 %copy-start.10 = (bf16[76,8,128]{2,1,0:T(8,128)(2,1)}, bf16[76,8,128]{2,1,0:T(8,128)(2,1)S(1)}, u32[]{:S(2)}) copy-start(bf16[76,8,128]{2,1,0:T(8,128)(2,1)S(1)} %collective-permute-done.4.high_ref) | copy-start | bytes 466948
  179.1 0.7 copy-start.11

commit v4 on v3

--- a/solution.py
+++ b/solution.py
@@ -363,50 +363,57 @@
     return full, jnp.concatenate([offset, offset])[None]
 
 
+def activation_kernel(sym_ref, gain_ref, shift_ref, out_ref):
+    cells = sym_ref[...].astype(F32).reshape(STEP * COLS, CH)
+    act = jnp.maximum(normalize(cells, gain_ref[0:1], shift_ref[0:1]), 0.0)
+    out_ref[...] = act.astype(BF).reshape(STEP, COLS, CH)
+
+
+def activations(sym, gain, shift):
+    whole = lambda *shape: pl.BlockSpec(shape, lambda s: (0,) * len(shape))
+    block = pl.BlockSpec((STEP, COLS, CH), lambda s: (s, 0, 0))
+    return pl.pallas_call(
+        activation_kernel,
+        grid=(ROWS // STEP,),
+        out_shape=jax.ShapeDtypeStruct((ROWS, COLS, CH), BF),
+        in_specs=[block, whole(2, CH), whole(2, CH)],
+        out_specs=block,
+        compiler_params=pltpu.CompilerParams(vmem_limit_bytes=60 * MIB),
+        cost_estimate=pl.CostEstimate(
+            flops=16 * ROWS * COLS * CH, bytes_accessed=4 * ROWS * COLS * CH, transcendentals=ROWS * COLS
+        ),
+        name="activations",
+    )(sym, gain, shift)
+
+
 TALL = ROWS + 2 * HALO
 SIDE = 8
-WIDE = COLS + 2 * SIDE
+WIDE = COLS + 4 * SIDE
 FIRST_TALL = ROWS + 2 * SECOND_DILATION
-GROUP_A, GROUP_B, GROUP_C = 4, 4, 8
-UNROLL_A, UNROLL_B = 2, 6
+FIRST_WIDE = COLS + 2 * SIDE
+GROUP_B, GROUP_C = 4, 8
+INNER_B, SLOTS_C = 9, 2
 CONV_VMEM = 62
 
 
 def convolution_kernel(
-    place_ref, sym_ref, top_ref, bottom_ref, low_ref, high_ref, gain_ref, shift_ref, bias_ref,
-    weight_hbm, out_hbm, tall_ref, act_ref, cols_ref, first_ref, second_ref, second_cols_ref,
-    weight_ref, out_ref, sems, out_sems,
+    place_ref, sym_ref, act_ref, top_ref, bottom_ref, low_ref, high_ref, gain_ref, shift_ref,
+    bias_ref, weight_hbm, out_hbm, tall_ref, wide_ref, first_ref, second_ref, shifted_ref,
+    late_ref, weight_ref, out_ref, sems, out_sems,
 ):
-    def rows_copy(k):
-        return pltpu.make_async_copy(
-            sym_ref.at[16 * k : 16 * k + 16],
-            tall_ref.at[HALO + 16 * k : HALO + 16 * k + 16],
-            sems.at[k],
-        )
-
-    top_copy = pltpu.make_async_copy(top_ref, tall_ref.at[0:HALO], sems.at[4])
-    bottom_copy = pltpu.make_async_copy(bottom_ref, tall_ref.at[HALO + ROWS : TALL], sems.at[5])
-    weight_copy = pltpu.make_async_copy(weight_hbm, weight_ref, sems.at[6])
-    top_copy.start()
-    for k in range(4):
-        rows_copy(k).start()
-    bottom_copy.start()
-    weight_copy.start()
+    top_copy = pltpu.make_async_copy(top_ref, tall_ref.at[0:HALO], sems.at[0])
+    bottom_copy = pltpu.make_async_copy(bottom_ref, tall_ref.at[HALO + ROWS : TALL], sems.at[1])
+    act_copy = pltpu.make_async_copy(
+        act_ref, wide_ref.at[HALO : HALO + ROWS, 16 : 16 + COLS], sems.at[2]
+    )
+    weight_copy = pltpu.make_async_copy(weight_hbm, weight_ref, sems.at[3])
+    sym_copy = pltpu.make_async_copy(sym_ref, tall_ref.at[HALO : HALO + ROWS], sems.at[4])
+    for copy in (top_copy, bottom_copy, act_copy, weight_copy, sym_copy):
+        copy.start()
     above = place_ref[0] > 0
     below = place_ref[0] < (NR - 1) * ROWS
     low_ok = (place_ref[1] > 0).astype(F32)
     high_ok = (place_ref[1] < (NC - 1) * COLS).astype(F32)
-    act_ref[...] = jnp.zeros((GROUP_A, WIDE + 16, CH), F32)
-
-    def values(at, count):
-        return jnp.concatenate(
-            [
-                low_ref[pl.ds(at, count)].astype(F32),
-                tall_ref[pl.ds(at, count)].astype(F32),
-                high_ref[pl.ds(at, count)].astype(F32),
-            ],
-            axis=1,
-        )
 
     def activate(cells, which):
         return jnp.maximum(
@@ -418,35 +425,25 @@
             0.0,
         )
 
-    def prepare(step, carry):
-        at = step * GROUP_A
-        act = activate(values(at, GROUP_A), 0)
-        act_ref[:, 8:16, :] = act[:, :SIDE] * low_ok
-        act_ref[:, 16 : 16 + COLS, :] = act[:, SIDE : SIDE + COLS]
-        act_ref[:, 16 + COLS : 24 + COLS, :] = act[:, SIDE + COLS :] * high_ok
-        for tap in range(3):
-            cols_ref[pl.ds(at, GROUP_A), :, tap * CH : (tap + 1) * CH] = act_ref[
-                :, 6 + 2 * tap : 6 + 2 * tap + WIDE, :
-            ].astype(BF)
-        return carry
-
+    nothing = jnp.zeros((TALL, SIDE, CH), F32)
+    low = activate(low_ref[...].astype(F32), 0) * low_ok
+    wide_ref[:, 0:16, :] = jnp.concatenate([nothing, low], axis=1).astype(BF)
+    high = activate(high_ref[...].astype(F32), 0) * high_ok
+    wide_ref[:, 16 + COLS :, :] = jnp.concatenate([high, nothing], axis=1).astype(BF)
     top_copy.wait()
-    begin = 0
-    for k, end in enumerate((20, 36, 52, TALL)):
-        rows_copy(k).wait()
-        if k == 3:
-            bottom_copy.wait()
-        lax.fori_loop(begin // GROUP_A, end // GROUP_A, prepare, 0, unroll=UNROLL_A)
-        begin = end
-    weight_copy.wait()
+    bottom_copy.wait()
+    wide_ref[0:HALO, 16 : 16 + COLS, :] = activate(tall_ref[0:HALO].astype(F32), 0).astype(BF)
+    wide_ref[HALO + ROWS :, 16 : 16 + COLS, :] = activate(
+        tall_ref[HALO + ROWS :].astype(F32), 0
+    ).astype(BF)
 
     @pl.when(jnp.logical_not(above))
     def _():
-        cols_ref[0:HALO] = jnp.zeros((HALO, WIDE, 3 * CH), BF)
+        wide_ref[0:HALO] = jnp.zeros((HALO, WIDE, CH), BF)
 
     @pl.when(jnp.logical_not(below))
     def _():
-        cols_ref[HALO + ROWS :] = jnp.zeros((HALO, WIDE, 3 * CH), BF)
+        wide_ref[HALO + ROWS :] = jnp.zeros((HALO, WIDE, CH), BF)
 
     def paired(source_ref, at, spacing, group, width, which):
         sets = group // (2 * spacing)
@@ -458,45 +455,66 @@
                         for k in range(sets)
                     ],
                     axis=0,
-                ).reshape(group // 2 * width, 3 * CH)
+                ).reshape(group // 2 * width, CH)
                 for slot in range(4)
             ],
             axis=1,
         )
         total = jnp.dot(lhs, weight_ref[which], preferred_element_type=F32)
-        near = total[:, :CH].reshape(sets, spacing, width, CH)
-        far = total[:, CH:].reshape(sets, spacing, width, CH)
-        return jnp.concatenate([near, far], axis=1).reshape(group, width, CH)
-
-    def convolve_first(step, carry):
-        at = step * GROUP_B
+        taps = []
+        for tap in range(3):
+            near = total[:, tap * CH : (tap + 1) * CH].reshape(sets, spacing, width, CH)
+            far = total[:, (3 + tap) * CH : (4 + tap) * CH].reshape(sets, spacing, width, CH)
+            taps.append(jnp.concatenate([near, far], axis=1).reshape(group, width, CH))
+        return taps
+
+    def first_rows(at, slot):
+        before, centre, after = paired(wide_ref, at, FIRST_DILATION, GROUP_B, WIDE, 0)
+        shifted_ref[slot, 0] = before
+        shifted_ref[slot, 1] = after
+        residual = jnp.concatenate(
+            [
+                low_ref[pl.ds(at + 2, GROUP_B)].astype(F32),
+                tall_ref[pl.ds(at + 2, GROUP_B)].astype(F32),
+                high_ref[pl.ds(at + 2, GROUP_B)].astype(F32),
+            ],
+            axis=1,
+        )
         first = (
-            paired(cols_ref, at, FIRST_DILATION, GROUP_B, WIDE, 0)
-            + values(at + 2, GROUP_B)
+            centre[:, 8 : 8 + FIRST_WIDE]
+            + shifted_ref[slot, 0, :, 6 : 6 + FIRST_WIDE, :]
+            + shifted_ref[slot, 1, :, 10 : 10 + FIRST_WIDE, :]
+            + residual
             + bias_ref[0:1].reshape(1, 1, CH)
         )
         first_ref[pl.ds(at, GROUP_B)] = first[:, SIDE : SIDE + COLS]
         act = activate(first, 1)
-        second_ref[:, :SIDE, :] = act[:, :SIDE] * low_ok
-        second_ref[:, SIDE : SIDE + COLS, :] = act[:, SIDE : SIDE + COLS]
-        second_ref[:, SIDE + COLS :, :] = act[:, SIDE + COLS :] * high_ok
-        for tap in range(3):
-            second_cols_ref[pl.ds(at, GROUP_B), :, tap * CH : (tap + 1) * CH] = second_ref[
-                :, 4 + 4 * tap : 4 + 4 * tap + COLS, :
-            ].astype(BF)
+        second_ref[pl.ds(at, GROUP_B)] = jnp.concatenate(
+            [
+                act[:, :SIDE] * low_ok,
+                act[:, SIDE : SIDE + COLS],
+                act[:, SIDE + COLS :] * high_ok,
+            ],
+            axis=1,
+        ).astype(BF)
+
+    def convolve_first(step, carry):
+        for k in range(INNER_B):
+            first_rows(step * (GROUP_B * INNER_B) + k * GROUP_B, k)
         return carry
 
-    lax.fori_loop(0, FIRST_TALL // GROUP_B, convolve_first, 0, unroll=UNROLL_B)
+    act_copy.wait()
+    weight_copy.wait()
+    sym_copy.wait()
+    lax.fori_loop(0, FIRST_TALL // (GROUP_B * INNER_B), convolve_first, 0)
 
     @pl.when(jnp.logical_not(above))
     def _():
-        second_cols_ref[0:SECOND_DILATION] = jnp.zeros((SECOND_DILATION, COLS, 3 * CH), BF)
+        second_ref[0:SECOND_DILATION] = jnp.zeros((SECOND_DILATION, FIRST_WIDE, CH), BF)
 
     @pl.when(jnp.logical_not(below))
     def _():
-        second_cols_ref[SECOND_DILATION + ROWS :] = jnp.zeros(
-            (SECOND_DILATION, COLS, 3 * CH), BF
-        )
+        second_ref[SECOND_DILATION + ROWS :] = jnp.zeros((SECOND_DILATION, FIRST_WIDE, CH), BF)
 
     def out_copy(k):
         return pltpu.make_async_copy(
@@ -506,8 +524,16 @@
     for k in range(4):
         for part in range(16 // GROUP_C):
             at = 16 * k + part * GROUP_C
+            slot = at // GROUP_C % SLOTS_C
+            before, centre, after = paired(
+                second_ref, at, SECOND_DILATION, GROUP_C, FIRST_WIDE, 1
+            )
+            late_ref[slot, 0] = before
+            late_ref[slot, 1] = after
             out_ref[at : at + GROUP_C] = (
-                paired(second_cols_ref, at, SECOND_DILATION, GROUP_C, COLS, 1)
+                centre[:, SIDE : SIDE + COLS]
+                + late_ref[slot, 0, :, 4 : 4 + COLS, :]
+                + late_ref[slot, 1, :, 12 : 12 + COLS, :]
                 + first_ref[at + 4 : at + 4 + GROUP_C]
                 + bias_ref[1:2].reshape(1, 1, CH)
             ).astype(BF)
@@ -516,36 +542,39 @@
         out_copy(k).wait()
 
 
-def convolutions(place, sym, top, bottom, low, high, gain, shift, bias, weight):
+def convolutions(place, sym, act, top, bottom, low, high, gain, shift, bias, weight):
     vmem = pl.BlockSpec(memory_space=pltpu.VMEM)
     anywhere = pl.BlockSpec(memory_space=pl.ANY)
     return pl.pallas_call(
         convolution_kernel,
         out_shape=jax.ShapeDtypeStruct((ROWS, COLS, CH), BF),
-        in_specs=[pl.BlockSpec(memory_space=pltpu.SMEM)] + [anywhere] * 3 + [vmem] * 5 + [anywhere],
+        in_specs=[pl.BlockSpec(memory_space=pltpu.SMEM)]
+        + [anywhere] * 4
+        + [vmem] * 5
+        + [anywhere],
         out_specs=anywhere,
         scratch_shapes=[
             pltpu.VMEM((TALL, COLS, CH), BF),
-            pltpu.VMEM((GROUP_A, WIDE + 16, CH), F32),
-            pltpu.VMEM((TALL, WIDE, 3 * CH), BF),
+            pltpu.VMEM((TALL, WIDE, CH), BF),
             pltpu.VMEM((FIRST_TALL, COLS, CH), F32),
-            pltpu.VMEM((GROUP_B, WIDE, CH), F32),
-            pltpu.VMEM((FIRST_TALL, COLS, 3 * CH), BF),
-            pltpu.VMEM((2, 12 * CH, 2 * CH), BF),
+            pltpu.VMEM((FIRST_TALL, FIRST_WIDE, CH), BF),
+            pltpu.VMEM((INNER_B, 2, GROUP_B, WIDE, CH), F32),
+            pltpu.VMEM((SLOTS_C, 2, GROUP_C, FIRST_WIDE, CH), F32),
+            pltpu.VMEM((2, 4 * CH, 6 * CH), BF),
             pltpu.VMEM((ROWS, COLS, CH), BF),
-            pltpu.SemaphoreType.DMA((7,)),
+            pltpu.SemaphoreType.DMA((5,)),
             pltpu.SemaphoreType.DMA((4,)),
         ],
         compiler_params=pltpu.CompilerParams(vmem_limit_bytes=CONV_VMEM * MIB),
         name="convolutions",
-    )(place, sym, top, bottom, low, high, gain, shift, bias, weight)
+    )(place, sym, act, top, bottom, low, high, gain, shift, bias, weight)
 
 
 def paired_weight(weight):
-    taps = weight.reshape(3, 3 * CH, CH)
+    taps = jnp.transpose(weight.reshape(3, 3, CH, CH), (0, 2, 1, 3)).reshape(3, CH, 3 * CH)
     near = jnp.concatenate([taps, jnp.zeros_like(taps[:1])], axis=0)
     far = jnp.concatenate([jnp.zeros_like(taps[:1]), taps], axis=0)
-    return jnp.concatenate([near, far], axis=2).reshape(12 * CH, 2 * CH)
+    return jnp.concatenate([near, far], axis=2).reshape(4 * CH, 6 * CH)
 
 
 def neighbours(low_strip, high_strip, axis):
@@ -581,7 +610,7 @@
     low, high = neighbours(edge(0, SIDE), edge(COLS - SIDE, COLS), "col")
     place = jnp.stack([lax.axis_index("row") * ROWS, lax.axis_index("col") * COLS]).astype(jnp.int32)
     return convolutions(
-        place, sym, top, bottom, low, high, conv_gain, conv_shift, convolution_bias,
+        place, sym, activations(sym, conv_gain, conv_shift), top, bottom, low, high, conv_gain, conv_shift, convolution_bias,
         jnp.stack([paired_weight(convolution_weight[0]), paired_weight(convolution_weight[1])]),
     )
 

time: 199 us -> 206 us (1.035); the launches traced: 198 us -> 202 us
  waiting for transfers between devices: 56.4 us -> 48.6 us
  local copies, waits for them, and re-layouts: 6.84 us -> 13.2 us
  other arithmetic: 3.08 us -> 5.66 us
  Pallas kernels: 47.7 us -> 50.2 us
    ppermute x2, waiting for transfers between devices: 7.62 us -> 1.37 us  [neighbours(): lax.ppermute(high_strip, axis, forward)]
    pallas_call x0 -> x1, Pallas kernels: none -> 5.13 us  [activations(): pl.pallas_call(activation_kernel, grid=(ROWS // STEP,), out_shape=jax.Sha...]
    concatenate x0 -> x2, local copies, waits for them, and re-layouts: none -> 3.54 us  [paired_weight(): return jnp.concatenate([near, far], axis=2).reshape(4 * CH, 6 * CH)]
    pallas_call x1, Pallas kernels: 18.2 us -> 15.6 us  [convolutions(): pl.pallas_call(convolution_kernel, out_shape=jax.ShapeDtypeStruct((ROWS,...]
    unnamed x32 -> x34, local copies, waits for them, and re-layouts: 4.02 us -> 5.61 us
  transfers between devices with their start and end apart: 6 -> 6, of which waited for: 6 -> 4; matrix products, arithmetic and copies ran while one was open for 2% -> 6% of each run, Pallas kernels for 2% -> 4%
where the time goes in v4:
time: 206 us; the launch traced here: 202 us
  blocking collectives  61.5 us (30%)
  Pallas kernels  50.2 us (24%)
  waiting for transfers between devices  48.6 us (24%)
  starting transfers between devices  22 us (11%)
  local copies, waits for them, and re-layouts  13.2 us (6%)
  other arithmetic  5.66 us (3%)
    all_to_all x1, blocking collectives, local(): lax.all_to_all(sent.reshape(128, 2, ROWS, COLS), ('row', 'col'), split_ax...  61.5 us
    all_to_all x1, waiting for transfers between devices, local(): lax.all_to_all(back.reshape(128, 2, ROWS, COLS), ('row', 'col'), split_ax...  41.2 us
    pallas_call x1, Pallas kernels, convolutions(): pl.pallas_call(convolution_kernel, out_shape=jax.ShapeDtypeStruct((ROWS,...  15.6 us
    ppermute x2, starting transfers between devices, neighbours(): lax.ppermute(low_strip, axis, backward)  10.1 us
    pallas_call x1, Pallas kernels, update(): pl.pallas_call(update_kernel, grid=(ROWS // USTEP,), out_shape=jax.ShapeD...  9.92 us
    all_to_all x1, starting transfers between devices, local(): lax.all_to_all(back.reshape(128, 2, ROWS, COLS), ('row', 'col'), split_ax...  7.95 us
    pallas_call x1, Pallas kernels, factors(): pl.pallas_call(factor_kernel, grid=(steps,), out_shape=jax.ShapeDtypeStru...  7.75 us
    pallas_call x1, Pallas kernels, product(): pl.pallas_call(product_kernel, out_shape=jax.ShapeDtypeStruct((half, 2, N...  5.99 us
  transfers between devices with their start and end apart: 6, of which 4 were waited for; matrix products, arithmetic and copies ran while one was open for 6% of the time, Pallas kernels for 4%

profile of v4, /device:TPU:10, one launch (start us, length us, event | category | flops | bytes accessed | tf_op | source)
XLA Modules:
  0.0 201.7 jit_solution(8193372054551217890)
XLA Ops:
  0.0 1.2 reshape.29.bias_ref
  1.2 7.7 %factors.1 = bf16[8,2,4,2,2,64,128]{6,5,4,3,2,1,0:T(8,128)(2,1)} custom-call(bf16[64,128,128]{2,1,0:T(8,128)(2,1)} %pair_ref.5, f32[1,128]{1,0:T(1,128)} %bitcast.30, f32[1,128]{1,0:T(1,128)} %bitcast.33, bf16[128,384]{1,0:T(8,128)(2,1)} %weight_ref.1, f32[1,384]{1,0:T(1,128)} %reshape.29.bias_ref), custom_call_target="tpu_custom_call" | custom-call | tf_op jit(solution)/shard_map/factors/pallas_call | solution.py:90
  9.0 61.5 %all_to_all.10 = bf16[128,2,64,128]{3,2,1,0:T(8,128)(2,1)} all-to-all(bf16[128,2,64,128]{3,2,1,0:T(8,128)(2,1)} %bitcast.40), channel_id=1, replica_groups=mesh['row'=16,'col'=8] {'row','col'}, dimensions={0} | all-to-all | bytes 8388608 | tf_op jit(solution)/shard_map/all_to_all | solution.py:593
  70.5 2.4 %plane.1 = bf16[16,8,64,128]{3,2,1,0:T(8,128)(2,1)} custom-call(bf16[16,8,2,64,128]{4,3,2,1,0:T(8,128)(2,1)} %bitcast.37), custom_call_target="tpu_custom_call" | custom-call | tf_op jit(solution)/shard_map/plane/pallas_call | solution.py:134
  72.9 0.1 collective-permute-start
  73.0 4.4 %collective-permute-done.other_ref = bf16[16,8,64,128]{3,2,1,0:T(8,128)(2,1)S(1)} collective-permute-done((bf16[16,8,64,128]{3,2,1,0:T(8,128)(2,1)}, bf16[16,8,64,128]{3,2,1,0:T(8,128)(2,1)S(1)}, u32[]{:S(2)}, u32[]{:S(2)}) %collective-permute-start) | collective-permute-done | bytes 2097184 | tf_op jit(solution)/shard_map/ppermute | solution.py:596
  77.4 0.0 copy-start.7
  77.4 1.3 copy-done.7
  78.7 6.0 %product.1 = bf16[8,2,8,2,64,128]{5,4,3,2,1,0:T(8,128)(2,1)} custom-call(bf16[8,2,8,2,64,128]{5,4,3,2,1,0:T(8,128)(2,1)} %bitcast.38, bf16[16,8,64,128]{3,2,1,0:T(8,128)(2,1)} %copy-done.7), custom_call_target="tpu_custom_call" | custom-call | tf_op jit(solution)/shard_map/product/pallas_call | solution.py:225
  84.7 0.0 copy-start.9
  84.7 8.0 %all-to-all-start.1 = ((bf16[128,2,64,128]{3,2,1,0:T(8,128)(2,1)}), bf16[128,2,64,128]{3,2,1,0:T(8,128)(2,1)}, u32[]{:S(2)}, u32[]{:S(2)}) async-start(bf16[128,2,64,128]{3,2,1,0:T(8,128)(2,1)} %bitcast.39), calls=%async_computation.1 | async-start | bytes 8388608 | tf_op jit(solution)/shard_map/all_to_all | solution.py:598
  92.7 0.0 copy-start.13
  92.7 0.0 copy-start.14
  92.7 0.0 copy-start.15
  92.7 0.0 copy-start.16
  92.7 0.0 copy-start.1
  92.7 0.0 copy-start.4
  92.7 0.0 copy-start.5
  92.8 0.9 slice.36.weight_ref.gate_ref
  93.7 0.0 copy-done.9
  93.7 0.2 copy.20
  93.9 0.9 copy.22
  94.8 0.0 copy-done.13
  94.8 0.0 copy-done.14
  94.8 0.0 copy-done.15
  94.8 0.1 fusion.10
  94.9 0.0 copy-done.16
  95.0 0.7 slice_bitcast_fusion.bias_ref.gate_bias_ref
  95.7 0.0 copy-done.1
  95.7 0.0 copy-done.4
  95.7 0.0 copy-done.5
  95.7 0.0 copy-start.8
  95.7 3.4 %gates.1.own_gate_ref = f32[64,128,128]{2,1,0:T(8,128)S(1)} custom-call(bf16[64,128,128]{2,1,0:T(8,128)(2,1)S(1)} %copy-done.1, f32[1,128]{1,0:T(1,128)S(1)} %bitcast.31, f32[1,128]{1,0:T(1,128)S(1)} %bitcast.34, bf16[128,128]{1,0:T(8,128)(2,1)S(1)} %slice.36.weight_ref.gate_ref, f32[1,128]{1,0:T(1,128)S(1)} %slice_bitcast_fusion.bias_ref.gate_bias_ref), custom_call_target="tpu_custom_call" | custom-call | flops 268435456 | bytes 6291456 | tf_op jit(solution)/shard_map/gates/pallas_call | solution.py:256
  99.1 0.0 copy-start.3
  99.1 2.0 copy-done.3
  101.1 0.1 fusion.4
  101.2 0.0 copy-done.8
  101.2 1.0 fusion.5
  102.2 41.2 %all-to-all-done.1.mirror_ref = bf16[128,2,64,128]{3,2,1,0:T(8,128)(2,1)} async-done(((bf16[128,2,64,128]{3,2,1,0:T(8,128)(2,1)}), bf16[128,2,64,128]{3,2,1,0:T(8,128)(2,1)}, u32[]{:S(2)}, u32[]{:S(2)}) %all-to-all-start.1) | async-done | bytes 4194336 | tf_op jit(solution)/shard_map/all_to_all | solution.py:598
  143.4 0.0 copy-start.2
  143.4 1.6 copy-done.2
  144.9 9.9 %update.1.sym_ref = bf16[64,128,128]{2,1,0:T(8,128)(2,1)S(1)} custom-call(bf16[64,128,128]{2,1,0:T(8,128)(2,1)S(1)} %copy-done.2, f32[64,128,128]{2,1,0:T(8,128)} %copy-done.3, bf16[8,2,8,2,64,128]{5,4,3,2,1,0:T(8,128)(2,1)} %bitcast.9.tri_ref, bf16[128,2,64,128]{3,2,1,0:T(8,128)(2,1)} %all-to-all-done.1.mirror_ref, f32[1,128]{1,0:T(1,128)S(1)} %bitcast.32, ...), custom_call_target="tpu_custom_call" | custom-call | tf_op jit(solution)/shard_map/update/pallas_call | solution.py:330
  154.9 0.0 copy-start
  154.9 1.9 collective-permute-start.1
  156.8 6.0 %collective-permute-start.2 = (bf16[6,128,128]{2,1,0:T(8,128)(2,1)S(1)}, bf16[6,128,128]{2,1,0:T(8,128)(2,1)S(1)}, u32[]{:S(2)}, u32[]{:S(2)}) collective-permute-start(bf16[6,128,128]{2,1,0:T(8,128)(2,1)S(1)} %get-tuple-element.7), channel_id=1, source_target_pairs={{8,0},{16,8},{24,16},{32,24},{40,32},{48,40},{56,48},{64,56},{72,6... | collective-permute-start | bytes 589832 | tf_op jit(solution)/shard_map/ppermute | solution.py:584
  162.9 1.4 collective-permute-done.1.top_ref
  164.3 1.7 collective-permute-done.2.bottom_ref
  166.1 0.7 pad_maximum_fusion.2
  166.8 4.1 %collective-permute-start.4 = (bf16[76,8,128]{2,1,0:T(8,128)(2,1)}, bf16[76,8,128]{2,1,0:T(8,128)(2,1)S(1)}, u32[]{:S(2)}, u32[]{:S(2)}) collective-permute-start(bf16[76,8,128]{2,1,0:T(8,128)(2,1)} %pad_maximum_fusion.2), channel_id=1, source_target_pairs={{1,0},{2,1},{3,2},{4,3},{5,4},{6,5},{7,6},{9,8},{10,9},{11,10},{12... | collective-permute-start | bytes 466952 | tf_op jit(solution)/shard_map/ppermute | solution.py:584
  170.9 0.7 pad_maximum_fusion.1
  171.6 1.9 collective-permute-start.3
  173.5 0.6 pad_add_fusion.place_ref
  174.1 1.2 copy.21
  175.3 0.0 copy-done
  175.3 2.4 %copy.23 = bf16[4,128,768]{2,1,0:T(8,128)(2,1)} copy(bf16[4,128,768]{1,2,0:T(8,128)(2,1)} %fusion.5) | data formatting | bytes 1572864 | tf_op jit(solution)/shard_map/concatenate | solution.py:577
  177.6 0.0 copy-done.10
  177.6 0.0 copy-done.11
  177.6 0.0 copy-done.6
  177.6 2.5 %pad_maximum_fusion.weight_hbm = bf16[2,512,768]{2,1,0:T(8,128)(2,1)} fusion(bf16[1,512,768]{2,1,0:T(8,128)(2,1)} %bitcast.42, bf16[1,512,768]{2,1,0:T(8,128)(2,1)S(1)} %bitcast.41), kind=kLoop, calls=%fused_computation.6 | loop fusion | flops 786432 | bytes 3145728 | tf_op jit(solution)/shard_map/stack | solution.py:614
  180.1 5.1 %activations.1.act_ref = bf16[64,128,128]{2,1,0:T(8,128)(2,1)} custom-call(bf16[64,128,128]{2,1,0:T(8,128)(2,1)} %copy-done, f32[2,128]{1,0:T(2,128)} %gain_ref.3, f32[2,128]{1,0:T(2,128)} %shift_ref.3), custom_call_target="tpu_custom_call" | custom-call | flops 16777216 | bytes 4194304 | tf_op jit(solution)/shard_map/activations/pallas_call | solution.py:375
  185.2 0.0 collective-permute-done.4.high_ref
  185.2 0.0 collective-permute-done.3.low_ref
  185.3 0.7 copy-done.12
  185.9 15.6 %convolutions.1 = bf16[64,128,128]{2,1,0:T(8,128)(2,1)} custom-call(s32[2]{0:T(128)} %pad_add_fusion.place_ref, bf16[64,128,128]{2,1,0:T(8,128)(2,1)} %copy-done, bf16[64,128,128]{2,1,0:T(8,128)(2,1)} %activations.1.act_ref, bf16[6,128,128]{2,1,0:T(8,128)(2,1)} %copy-done.10, bf16[6,128,128]{2,1,0:T(8,128)(2,1)} %copy-done.11, ...), custom_call_target="tpu_custom_call" | custom-call | tf_op jit(solution)/shard_map/convolutions/pallas_call | solution.py:548
  (12 shorter events, 0.1 us)
Async XLA Ops:
  72.9 4.5 %collective-permute-start = (bf16[16,8,64,128]{3,2,1,0:T(8,128)(2,1)}, bf16[16,8,64,128]{3,2,1,0:T(8,128)(2,1)S(1)}, u32[]{:S(2)}, u32[]{:S(2)}) collective-permute-start(bf16[16,8,64,128]{3,2,1,0:T(8,128)(2,1)} %plane.1), channel_id=1, source_target_pairs={{0,8},{8,0},{16,24},{24,16},{32,40},{40,32},{48,56},{56,48},{64,72... | collective-permute-start | bytes 6291464 | tf_op jit(solution)/shard_map/ppermute | solution.py:596
  77.4 1.3 copy-start.7
  84.7 9.0 %copy-start.9 = (bf16[2,9,128,128]{3,2,1,0:T(8,128)(2,1)S(1)}, bf16[2,9,128,128]{3,2,1,0:T(8,128)(2,1)}, u32[]{:S(2)}) copy-start(bf16[2,9,128,128]{3,2,1,0:T(8,128)(2,1)} %param.24) | copy-start | bytes 1769476
  84.7 58.6 %all-to-all-start.1 = ((bf16[128,2,64,128]{3,2,1,0:T(8,128)(2,1)}), bf16[128,2,64,128]{3,2,1,0:T(8,128)(2,1)}, u32[]{:S(2)}, u32[]{:S(2)}) async-start(bf16[128,2,64,128]{3,2,1,0:T(8,128)(2,1)} %bitcast.39), calls=%async_computation.1 | async-start | bytes 8388608 | tf_op jit(solution)/shard_map/all_to_all | solution.py:598
  92.7 2.2 %copy-start.13 = (bf16[64,128]{1,0:T(8,128)(2,1)S(1)}, bf16[64,128]{1,0:T(8,128)(2,1)}, u32[]{:S(2)}) copy-start(bf16[64,128]{1,0:T(8,128)(2,1)} %param.20) | copy-start | bytes 49156
  92.7 2.2 %copy-start.14 = (f32[64]{0:T(128)S(1)}, f32[64]{0:T(128)}, u32[]{:S(2)}) copy-start(f32[64]{0:T(128)} %param.19) | copy-start | bytes 772
  92.7 2.1 %copy-start.15 = (f32[64]{0:T(128)S(1)}, f32[64]{0:T(128)}, u32[]{:S(2)}) copy-start(f32[64]{0:T(128)} %param.18) | copy-start | bytes 772
  92.7 2.2 %copy-start.16 = (f32[128]{0:T(128)S(1)}, f32[128]{0:T(128)}, u32[]{:S(2)}) copy-start(f32[128]{0:T(128)} %param.21) | copy-start | bytes 1540
  92.7 2.9 %copy-start.1 = (bf16[64,128,128]{2,1,0:T(8,128)(2,1)S(1)}, bf16[64,128,128]{2,1,0:T(8,128)(2,1)}, u32[]{:S(2)}) copy-start(bf16[64,128,128]{2,1,0:T(8,128)(2,1)} %pair_ref.5) | copy-start | bytes 6291460
  92.7 2.9 %copy-start.4 = (f32[128]{0:T(128)S(1)}, f32[128]{0:T(128)}, u32[]{:S(2)}) copy-start(f32[128]{0:T(128)} %param.14) | copy-start | bytes 1540
  92.7 2.9 %copy-start.5 = (f32[128]{0:T(128)S(1)}, f32[128]{0:T(128)}, u32[]{:S(2)}) copy-start(f32[128]{0:T(128)} %param.15) | copy-start | bytes 1540
  95.7 5.5 %copy-start.8 = (bf16[1,9,128,128]{2,3,1,0:T(8,128)(2,1)S(1)}, bf16[1,9,128,128]{2,3,1,0:T(8,128)(2,1)}, u32[]{:S(2)}) copy-start(bf16[1,9,128,128]{2,3,1,0:T(8,128)(2,1)} %copy.22) | copy-start | bytes 884740
  99.1 2.0 copy-start.3
  143.4 1.6 copy-start.2
  154.9 20.4 %copy-start = (bf16[64,128,128]{2,1,0:T(8,128)(2,1)}, bf16[64,128,128]{2,1,0:T(8,128)(2,1)S(1)}, u32[]{:S(2)}) copy-start(bf16[64,128,128]{2,1,0:T(8,128)(2,1)S(1)} %update.1.sym_ref) | copy-start | bytes 6291460
  154.9 9.4 %collective-permute-start.1 = (bf16[6,128,128]{2,1,0:T(8,128)(2,1)S(1)}, bf16[6,128,128]{2,1,0:T(8,128)(2,1)S(1)}, u32[]{:S(2)}, u32[]{:S(2)}) collective-permute-start(bf16[6,128,128]{2,1,0:T(8,128)(2,1)S(1)} %get-tuple-element.8), channel_id=1, source_target_pairs={{0,8},{8,16},{16,24},{24,32},{32,40},{40,48},{48,56},{56,64},{64,7... | collective-permute-start | bytes 589832 | tf_op jit(solution)/shard_map/ppermute | solution.py:584
  156.8 9.2 %collective-permute-start.2 = (bf16[6,128,128]{2,1,0:T(8,128)(2,1)S(1)}, bf16[6,128,128]{2,1,0:T(8,128)(2,1)S(1)}, u32[]{:S(2)}, u32[]{:S(2)}) collective-permute-start(bf16[6,128,128]{2,1,0:T(8,128)(2,1)S(1)} %get-tuple-element.7), channel_id=1, source_target_pairs={{8,0},{16,8},{24,16},{32,24},{40,32},{48,40},{56,48},{64,56},{72,6... | collective-permute-start | bytes 589832 | tf_op jit(solution)/shard_map/ppermute | solution.py:584
  164.3 13.3 %copy-start.10 = (bf16[6,128,128]{2,1,0:T(8,128)(2,1)}, bf16[6,128,128]{2,1,0:T(8,128)(2,1)S(1)}, u32[]{:S(2)}) copy-start(bf16[6,128,128]{2,1,0:T(8,128)(2,1)S(1)} %collective-permute-done.1.top_ref) | copy-start | bytes 589828
  166.1 11.6 %copy-start.11 = (bf16[6,128,128]{2,1,0:T(8,128)(2,1)}, bf16[6,128,128]{2,1,0:T(8,128)(2,1)S(1)}, u32[]{:S(2)}) copy-start(bf16[6,128,128]{2,1,0:T(8,128)(2,1)S(1)} %collective-permute-done.2.bottom_ref) | copy-start | bytes 589828
  166.8 18.4 %collective-permute-start.4 = (bf16[76,8,128]{2,1,0:T(8,128)(2,1)}, bf16[76,8,128]{2,1,0:T(8,128)(2,1)S(1)}, u32[]{:S(2)}, u32[]{:S(2)}) collective-permute-start(bf16[76,8,128]{2,1,0:T(8,128)(2,1)} %pad_maximum_fusion.2), channel_id=1, source_target_pairs={{1,0},{2,1},{3,2},{4,3},{5,4},{6,5},{7,6},{9,8},{10,9},{11,10},{12... | collective-permute-start | bytes 466952 | tf_op jit(solution)/shard_map/ppermute | solution.py:584
  171.6 13.7 %collective-permute-start.3 = (bf16[76,8,128]{2,1,0:T(8,128)(2,1)}, bf16[76,8,128]{2,1,0:T(8,128)(2,1)}, u32[]{:S(2)}, u32[]{:S(2)}) collective-permute-start(bf16[76,8,128]{2,1,0:T(8,128)(2,1)} %pad_maximum_fusion.1), channel_id=1, source_target_pairs={{0,1},{1,2},{2,3},{3,4},{4,5},{5,6},{6,7},{8,9},{9,10},{10,11},{11... | collective-permute-start | bytes 466952 | tf_op jit(solution)/shard_map/ppermute | solution.py:584
  175.3 2.4 %copy-start.6 = (bf16[4,128,768]{2,1,0:T(8,128)(2,1)S(1)}, bf16[4,128,768]{2,1,0:T(8,128)(2,1)}, u32[]{:S(2)}) copy-start(bf16[4,128,768]{2,1,0:T(8,128)(2,1)} %copy.21) | copy-start | bytes 2359300
  185.2 0.7 copy-start.12

commit v5 on v4

--- a/solution.py
+++ b/solution.py
@@ -60,7 +60,7 @@
     cell_copy(step).start()
     cells = pair_ref[...].astype(F32).reshape(STEP * COLS, CH)
     normed = normalize(cells, gain_ref[...], shift_ref[...]).astype(BF)
-    bias = jnp.transpose(jnp.broadcast_to(bias_ref[:, : 4 * HID], (COLS, 4 * HID)))
+    bias = jnp.transpose(jnp.broadcast_to(bias_ref[...][None], (COLS, 4 * HID + CH))[:, : 4 * HID])
     projected = lax.dot_general(
         weight_ref[:, : 4 * HID], normed, (((0,), (1,)), ((), ())), preferred_element_type=F32
     )
@@ -96,7 +96,7 @@
             whole(1, CH),
             whole(1, CH),
             whole(CH, 4 * HID + CH),
-            whole(1, 4 * HID + CH),
+            whole(4 * HID + CH),
         ],
         out_specs=pl.BlockSpec(memory_space=pl.ANY),
         scratch_shapes=[
@@ -146,7 +146,7 @@
     )(received)
 
 
-PLANE_VMEM = 60
+PLANE_VMEM = 16
 PRODUCT_VMEM = 60
 
 
@@ -378,7 +378,7 @@
         out_shape=jax.ShapeDtypeStruct((ROWS, COLS, CH), BF),
         in_specs=[block, whole(2, CH), whole(2, CH)],
         out_specs=block,
-        compiler_params=pltpu.CompilerParams(vmem_limit_bytes=60 * MIB),
+        compiler_params=pltpu.CompilerParams(vmem_limit_bytes=24 * MIB),
         cost_estimate=pl.CostEstimate(
             flops=16 * ROWS * COLS * CH, bytes_accessed=4 * ROWS * COLS * CH, transcendentals=ROWS * COLS
         ),
@@ -393,7 +393,7 @@
 FIRST_WIDE = COLS + 2 * SIDE
 GROUP_B, GROUP_C = 4, 8
 INNER_B, SLOTS_C = 9, 2
-CONV_VMEM = 62
+CONV_VMEM = 40
 
 
 def convolution_kernel(
@@ -589,7 +589,7 @@
     conv_gain, conv_shift, convolution_weight, convolution_bias,
 ):
     gain, shift = norm_gain[None], norm_shift[None]
-    sent = factors(pair, gain, shift, proj_weight, proj_bias.reshape(1, 4 * HID + CH))
+    sent = factors(pair, gain, shift, proj_weight, proj_bias)
     received = lax.all_to_all(
         sent.reshape(128, 2, ROWS, COLS), ("row", "col"), split_axis=0, concat_axis=0, tiled=True
     ).reshape(NR, NC, 2, ROWS, COLS)
@@ -599,6 +599,8 @@
         back.reshape(128, 2, ROWS, COLS), ("row", "col"), split_axis=0, concat_axis=0, tiled=True
     )
     gate, gate_bias = proj_weight[:, 4 * HID :], proj_bias[None, 4 * HID :]
+    paired = jnp.stack([paired_weight(convolution_weight[0]), paired_weight(convolution_weight[1])])
+    gate, paired = lax.optimization_barrier((gate, paired))
     sym = update(
         pair, gates(pair, gain, shift, gate, gate_bias), returned, gain, shift, gate, gate_bias,
         *output_weight(out_weight, out_bias, mid_gain, mid_shift),
@@ -611,7 +613,7 @@
     place = jnp.stack([lax.axis_index("row") * ROWS, lax.axis_index("col") * COLS]).astype(jnp.int32)
     return convolutions(
         place, sym, activations(sym, conv_gain, conv_shift), top, bottom, low, high, conv_gain, conv_shift, convolution_bias,
-        jnp.stack([paired_weight(convolution_weight[0]), paired_weight(convolution_weight[1])]),
+        paired,
     )
 
 

time: 206 us -> 194 us (0.942); the launches traced: 202 us -> 193 us
  Pallas kernels: 50.2 us -> 44.6 us
  waiting for transfers between devices: 48.6 us -> 53.7 us
  local copies, waits for them, and re-layouts: 13.2 us -> 9.17 us
  other arithmetic: 5.66 us -> 1.72 us
    ppermute x2, waiting for transfers between devices: 1.37 us -> 6.81 us  [neighbours(): lax.ppermute(high_strip, axis, forward)]
    concatenate x2, local copies, waits for them, and re-layouts: 3.54 us -> 0.56 us  [paired_weight(): return jnp.concatenate([near, far], axis=2).reshape(4 * CH, 6 * CH)]
    pallas_call x1, Pallas kernels: 5.13 us -> 2.72 us  [activations(): pl.pallas_call(activation_kernel, grid=(ROWS // STEP,), out_shape=jax.Sha...]
    unnamed x34 -> x32, local copies, waits for them, and re-layouts: 5.61 us -> 6.6 us
  transfers between devices with their start and end apart: 6 -> 6, of which waited for: 4 -> 5; matrix products, arithmetic and copies ran while one was open for 6% -> 2% of each run, Pallas kernels for 4% -> 3%
where the time goes in v5:
time: 194 us; the launch traced here: 193 us
  blocking collectives  61.4 us (32%)
  waiting for transfers between devices  53.7 us (28%)
  Pallas kernels  44.6 us (23%)
  starting transfers between devices  22 us (11%)
  local copies, waits for them, and re-layouts  9.17 us (5%)
    all_to_all x1, blocking collectives, local(): lax.all_to_all(sent.reshape(128, 2, ROWS, COLS), ('row', 'col'), split_ax...  61.4 us
    all_to_all x1, waiting for transfers between devices, local(): lax.all_to_all(back.reshape(128, 2, ROWS, COLS), ('row', 'col'), split_ax...  41 us
    pallas_call x1, Pallas kernels, convolutions(): pl.pallas_call(convolution_kernel, out_shape=jax.ShapeDtypeStruct((ROWS,...  14.4 us
    ppermute x2, starting transfers between devices, neighbours(): lax.ppermute(low_strip, axis, backward)  10.1 us
    pallas_call x1, Pallas kernels, update(): pl.pallas_call(update_kernel, grid=(ROWS // USTEP,), out_shape=jax.ShapeD...  9.92 us
    all_to_all x1, starting transfers between devices, local(): lax.all_to_all(back.reshape(128, 2, ROWS, COLS), ('row', 'col'), split_ax...  8.01 us
    pallas_call x1, Pallas kernels, factors(): pl.pallas_call(factor_kernel, grid=(steps,), out_shape=jax.ShapeDtypeStru...  7.73 us
    ppermute x2, waiting for transfers between devices, neighbours(): lax.ppermute(high_strip, axis, forward)  6.81 us
  transfers between devices with their start and end apart: 6, of which 5 were waited for; matrix products, arithmetic and copies ran while one was open for 2% of the time, Pallas kernels for 3%

profile of v5, /device:TPU:10, one launch (start us, length us, event | category | flops | bytes accessed | tf_op | source)
XLA Modules:
  0.0 193.0 jit_solution(3924796183643616133)
XLA Ops:
  0.0 7.7 %factors.1 = bf16[8,2,4,2,2,64,128]{6,5,4,3,2,1,0:T(8,128)(2,1)} custom-call(bf16[64,128,128]{2,1,0:T(8,128)(2,1)} %pair_ref.5, f32[1,128]{1,0:T(1,128)} %bitcast.32, f32[1,128]{1,0:T(1,128)} %bitcast.35, bf16[128,384]{1,0:T(8,128)(2,1)} %weight_ref.1, f32[384]{0:T(512)} %bias_ref.2), custom_call_target="tpu_custom_call" | custom-call | tf_op jit(solution)/shard_map/factors/pallas_call | solution.py:90
  7.7 61.4 %all_to_all.10 = bf16[128,2,64,128]{3,2,1,0:T(8,128)(2,1)S(1)} all-to-all(bf16[128,2,64,128]{3,2,1,0:T(8,128)(2,1)} %bitcast.40), channel_id=1, replica_groups=mesh['row'=16,'col'=8] {'row','col'}, dimensions={0} | all-to-all | bytes 8388608 | tf_op jit(solution)/shard_map/all_to_all | solution.py:593
  69.1 0.0 copy-start
  69.1 0.4 plane.1
  69.6 1.6 copy-done
  71.2 0.0 collective-permute-start
  71.2 4.2 %collective-permute-done.other_ref = bf16[16,8,64,128]{3,2,1,0:T(8,128)(2,1)S(1)} collective-permute-done((bf16[16,8,64,128]{3,2,1,0:T(8,128)(2,1)S(1)}, bf16[16,8,64,128]{3,2,1,0:T(8,128)(2,1)S(1)}, u32[]{:S(2)}, u32[]{:S(2)}) %collective-permute-start) | collective-permute-done | bytes 2097184 | tf_op jit(solution)/shard_map/ppermute | solution.py:596
  75.3 0.0 copy-start.10
  75.3 1.3 copy-done.10
  76.6 6.0 %product.1 = bf16[8,2,8,2,64,128]{5,4,3,2,1,0:T(8,128)(2,1)} custom-call(bf16[8,2,8,2,64,128]{5,4,3,2,1,0:T(8,128)(2,1)} %bitcast.30, bf16[16,8,64,128]{3,2,1,0:T(8,128)(2,1)} %copy-done.10), custom_call_target="tpu_custom_call" | custom-call | tf_op jit(solution)/shard_map/product/pallas_call | solution.py:225
  82.7 0.0 copy-start.11
  82.7 8.0 %all-to-all-start.1 = ((bf16[128,2,64,128]{3,2,1,0:T(8,128)(2,1)}), bf16[128,2,64,128]{3,2,1,0:T(8,128)(2,1)}, u32[]{:S(2)}, u32[]{:S(2)}) async-start(bf16[128,2,64,128]{3,2,1,0:T(8,128)(2,1)} %bitcast.39), calls=%async_computation.1 | async-start | bytes 8388608 | tf_op jit(solution)/shard_map/all_to_all | solution.py:598
  90.7 0.8 slice.36.weight_ref.gate_ref
  91.5 0.0 copy-done.11
  91.5 0.2 copy.20
  91.7 0.1 fusion.5
  91.8 0.3 copy.21
  92.1 0.2 copy.18
  92.4 0.1 fusion.4
  92.5 0.3 copy.19
  92.8 0.0 copy-start.12
  92.8 0.0 copy-start.13
  92.8 0.0 copy-start.14
  92.8 0.0 copy-start.15
  92.8 0.0 copy-start.1
  92.8 0.0 copy-start.5
  92.8 0.0 copy-start.6
  92.8 1.3 pad_maximum_fusion.weight_hbm
  94.1 0.0 copy-done.12
  94.1 0.0 copy-done.13
  94.1 0.0 copy-done.14
  94.1 0.1 fusion.10
  94.2 0.0 copy-done.15
  94.2 0.7 slice_bitcast_fusion.bias_ref.gate_bias_ref
  94.9 0.1 copy-done.1
  95.0 0.0 copy-done.5
  95.0 0.0 copy-done.6
  95.0 3.4 %gates.1.own_gate_ref = f32[64,128,128]{2,1,0:T(8,128)S(1)} custom-call(bf16[64,128,128]{2,1,0:T(8,128)(2,1)S(1)} %copy-done.1, f32[1,128]{1,0:T(1,128)S(1)} %bitcast.33, f32[1,128]{1,0:T(1,128)S(1)} %bitcast.36, bf16[128,128]{1,0:T(8,128)(2,1)S(1)} %slice.36.weight_ref.gate_ref, f32[1,128]{1,0:T(1,128)S(1)} %slice_bitcast_fusion.bias_ref.gate_bias_ref), custom_call_target="tpu_custom_call" | custom-call | flops 268435456 | bytes 6291456 | tf_op jit(solution)/shard_map/gates/pallas_call | solution.py:256
  98.4 0.0 copy-start.3
  98.4 2.0 %copy-done.3 = f32[64,128,128]{2,1,0:T(8,128)} copy-done((f32[64,128,128]{2,1,0:T(8,128)}, f32[64,128,128]{2,1,0:T(8,128)S(1)}, u32[]{:S(2)}) %copy-start.3) | copy-done | bytes 4194328
  100.4 41.0 %all-to-all-done.1.mirror_ref = bf16[128,2,64,128]{3,2,1,0:T(8,128)(2,1)} async-done(((bf16[128,2,64,128]{3,2,1,0:T(8,128)(2,1)}), bf16[128,2,64,128]{3,2,1,0:T(8,128)(2,1)}, u32[]{:S(2)}, u32[]{:S(2)}) %all-to-all-start.1) | async-done | bytes 4194336 | tf_op jit(solution)/shard_map/all_to_all | solution.py:598
  141.4 0.0 copy-start.2
  141.4 1.6 copy-done.2
  143.0 9.9 %update.1.sym_ref = bf16[64,128,128]{2,1,0:T(8,128)(2,1)S(1)} custom-call(bf16[64,128,128]{2,1,0:T(8,128)(2,1)S(1)} %copy-done.2, f32[64,128,128]{2,1,0:T(8,128)} %copy-done.3, bf16[8,2,8,2,64,128]{5,4,3,2,1,0:T(8,128)(2,1)} %bitcast.21.tri_ref, bf16[128,2,64,128]{3,2,1,0:T(8,128)(2,1)} %all-to-all-done.1.mirror_ref, f32[1,128]{1,0:T(1,128)S(1)} %bitcast.34, ...), custom_call_target="tpu_custom_call" | custom-call | tf_op jit(solution)/shard_map/update/pallas_call | solution.py:330
  152.9 0.0 copy-start.7
  152.9 0.0 copy-start.8
  153.0 1.9 collective-permute-start.1
  154.9 6.0 %collective-permute-start.2 = (bf16[6,128,128]{2,1,0:T(8,128)(2,1)S(1)}, bf16[6,128,128]{2,1,0:T(8,128)(2,1)S(1)}, u32[]{:S(2)}, u32[]{:S(2)}) collective-permute-start(bf16[6,128,128]{2,1,0:T(8,128)(2,1)S(1)} %get-tuple-element.11), channel_id=1, source_target_pairs={{8,0},{16,8},{24,16},{32,24},{40,32},{48,40},{56,48},{64,56},{72,6... | collective-permute-start | bytes 589832 | tf_op jit(solution)/shard_map/ppermute | solution.py:584
  161.0 1.4 collective-permute-done.1.top_ref
  162.4 1.7 collective-permute-done.2.bottom_ref
  164.1 4.1 %collective-permute-start.4 = (bf16[76,8,128]{2,1,0:T(8,128)(2,1)S(1)}, bf16[76,8,128]{2,1,0:T(8,128)(2,1)S(1)}, u32[]{:S(2)}, u32[]{:S(2)}) collective-permute-start(bf16[76,8,128]{2,1,0:T(8,128)(2,1)S(1)} %pad_maximum_fusion.2), channel_id=1, source_target_pairs={{1,0},{2,1},{3,2},{4,3},{5,4},{6,5},{7,6},{9,8},{10,9},{11,10},{12... | collective-permute-start | bytes 466952 | tf_op jit(solution)/shard_map/ppermute | solution.py:584
  168.3 1.9 collective-permute-start.3
  170.2 0.1 pad_add_fusion.place_ref
  170.3 0.0 copy-done.7
  170.3 0.0 copy-done.8
  170.3 0.0 copy-start.4
  170.3 0.0 copy-start.9
  170.3 2.7 %activations.1.act_ref = bf16[64,128,128]{2,1,0:T(8,128)(2,1)S(1)} custom-call(bf16[64,128,128]{2,1,0:T(8,128)(2,1)S(1)} %update.1.sym_ref, f32[2,128]{1,0:T(2,128)S(1)} %copy-done.7, f32[2,128]{1,0:T(2,128)S(1)} %copy-done.8), custom_call_target="tpu_custom_call" | custom-call | flops 16777216 | bytes 4194304 | tf_op jit(solution)/shard_map/activations/pallas_call | solution.py:375
  173.0 0.0 collective-permute-done.4.high_ref
  173.0 5.4 %collective-permute-done.3.low_ref = bf16[76,8,128]{2,1,0:T(8,128)(2,1)S(1)} collective-permute-done((bf16[76,8,128]{2,1,0:T(8,128)(2,1)S(1)}, bf16[76,8,128]{2,1,0:T(8,128)(2,1)S(1)}, u32[]{:S(2)}, u32[]{:S(2)}) %collective-permute-start.3) | collective-permute-done | bytes 155680 | tf_op jit(solution)/shard_map/ppermute | solution.py:584
  178.5 0.0 copy-done.4
  178.5 0.0 copy-done.9
  178.5 14.4 %convolutions.1 = bf16[64,128,128]{2,1,0:T(8,128)(2,1)} custom-call(s32[2]{0:T(128)S(1)} %pad_add_fusion.place_ref, bf16[64,128,128]{2,1,0:T(8,128)(2,1)S(1)} %update.1.sym_ref, bf16[64,128,128]{2,1,0:T(8,128)(2,1)S(1)} %activations.1.act_ref, bf16[6,128,128]{2,1,0:T(8,128)(2,1)S(1)} %collective-permute-done.1.top_ref, ...), custom_call_target="tpu_custom_call" | custom-call | tf_op jit(solution)/shard_map/convolutions/pallas_call | solution.py:548
  (10 shorter events, 0.2 us)
Async XLA Ops:
  69.1 2.0 %copy-start = (bf16[128,2,64,128]{3,2,1,0:T(8,128)(2,1)}, bf16[128,2,64,128]{3,2,1,0:T(8,128)(2,1)S(1)}, u32[]{:S(2)}) copy-start(bf16[128,2,64,128]{3,2,1,0:T(8,128)(2,1)S(1)} %all_to_all.10) | copy-start | bytes 12582916
  71.2 4.2 %collective-permute-start = (bf16[16,8,64,128]{3,2,1,0:T(8,128)(2,1)S(1)}, bf16[16,8,64,128]{3,2,1,0:T(8,128)(2,1)S(1)}, u32[]{:S(2)}, u32[]{:S(2)}) collective-permute-start(bf16[16,8,64,128]{3,2,1,0:T(8,128)(2,1)S(1)} %plane.1), channel_id=1, source_target_pairs={{0,8},{8,0},{16,24},{24,16},{32,40},{40,32},{48,56},{56,48},{64,72... | collective-permute-start | bytes 6291464 | tf_op jit(solution)/shard_map/ppermute | solution.py:596
  75.3 1.3 copy-start.10
  82.7 8.8 %copy-start.11 = (bf16[2,9,128,128]{3,2,1,0:T(8,128)(2,1)S(1)}, bf16[2,9,128,128]{3,2,1,0:T(8,128)(2,1)}, u32[]{:S(2)}) copy-start(bf16[2,9,128,128]{3,2,1,0:T(8,128)(2,1)} %param.24) | copy-start | bytes 1769476
  82.7 58.7 %all-to-all-start.1 = ((bf16[128,2,64,128]{3,2,1,0:T(8,128)(2,1)}), bf16[128,2,64,128]{3,2,1,0:T(8,128)(2,1)}, u32[]{:S(2)}, u32[]{:S(2)}) async-start(bf16[128,2,64,128]{3,2,1,0:T(8,128)(2,1)} %bitcast.39), calls=%async_computation.1 | async-start | bytes 8388608 | tf_op jit(solution)/shard_map/all_to_all | solution.py:598
  92.8 1.4 copy-start.12
  92.8 1.4 copy-start.13
  92.8 1.3 copy-start.14
  92.8 1.4 copy-start.15
  92.8 2.2 %copy-start.1 = (bf16[64,128,128]{2,1,0:T(8,128)(2,1)S(1)}, bf16[64,128,128]{2,1,0:T(8,128)(2,1)}, u32[]{:S(2)}) copy-start(bf16[64,128,128]{2,1,0:T(8,128)(2,1)} %pair_ref.5) | copy-start | bytes 6291460
  92.8 2.2 %copy-start.5 = (f32[128]{0:T(128)S(1)}, f32[128]{0:T(128)}, u32[]{:S(2)}) copy-start(f32[128]{0:T(128)} %param.14) | copy-start | bytes 1540
  92.8 2.2 %copy-start.6 = (f32[128]{0:T(128)S(1)}, f32[128]{0:T(128)}, u32[]{:S(2)}) copy-start(f32[128]{0:T(128)} %param.15) | copy-start | bytes 1540
  98.4 2.0 %copy-start.3 = (f32[64,128,128]{2,1,0:T(8,128)}, f32[64,128,128]{2,1,0:T(8,128)S(1)}, u32[]{:S(2)}) copy-start(f32[64,128,128]{2,1,0:T(8,128)S(1)} %gates.1.own_gate_ref) | copy-start | bytes 12582916
  141.4 1.6 copy-start.2
  152.9 17.4 %copy-start.7 = (f32[2,128]{1,0:T(2,128)S(1)}, f32[2,128]{1,0:T(2,128)}, u32[]{:S(2)}) copy-start(f32[2,128]{1,0:T(2,128)} %gain_ref.3) | copy-start | bytes 3076
  152.9 17.4 %copy-start.8 = (f32[2,128]{1,0:T(2,128)S(1)}, f32[2,128]{1,0:T(2,128)}, u32[]{:S(2)}) copy-start(f32[2,128]{1,0:T(2,128)} %shift_ref.3) | copy-start | bytes 3076
  153.0 9.4 %collective-permute-start.1 = (bf16[6,128,128]{2,1,0:T(8,128)(2,1)S(1)}, bf16[6,128,128]{2,1,0:T(8,128)(2,1)S(1)}, u32[]{:S(2)}, u32[]{:S(2)}) collective-permute-start(bf16[6,128,128]{2,1,0:T(8,128)(2,1)S(1)} %get-tuple-element.12), channel_id=1, source_target_pairs={{0,8},{8,16},{16,24},{24,32},{32,40},{40,48},{48,56},{56,64},{64,7... | collective-permute-start | bytes 589832 | tf_op jit(solution)/shard_map/ppermute | solution.py:584
  154.9 9.2 %collective-permute-start.2 = (bf16[6,128,128]{2,1,0:T(8,128)(2,1)S(1)}, bf16[6,128,128]{2,1,0:T(8,128)(2,1)S(1)}, u32[]{:S(2)}, u32[]{:S(2)}) collective-permute-start(bf16[6,128,128]{2,1,0:T(8,128)(2,1)S(1)} %get-tuple-element.11), channel_id=1, source_target_pairs={{8,0},{16,8},{24,16},{32,24},{40,32},{48,40},{56,48},{64,56},{72,6... | collective-permute-start | bytes 589832 | tf_op jit(solution)/shard_map/ppermute | solution.py:584
  164.1 8.9 %collective-permute-start.4 = (bf16[76,8,128]{2,1,0:T(8,128)(2,1)S(1)}, bf16[76,8,128]{2,1,0:T(8,128)(2,1)S(1)}, u32[]{:S(2)}, u32[]{:S(2)}) collective-permute-start(bf16[76,8,128]{2,1,0:T(8,128)(2,1)S(1)} %pad_maximum_fusion.2), channel_id=1, source_target_pairs={{1,0},{2,1},{3,2},{4,3},{5,4},{6,5},{7,6},{9,8},{10,9},{11,10},{12... | collective-permute-start | bytes 466952 | tf_op jit(solution)/shard_map/ppermute | solution.py:584
  168.3 10.2 %collective-permute-start.3 = (bf16[76,8,128]{2,1,0:T(8,128)(2,1)S(1)}, bf16[76,8,128]{2,1,0:T(8,128)(2,1)S(1)}, u32[]{:S(2)}, u32[]{:S(2)}) collective-permute-start(bf16[76,8,128]{2,1,0:T(8,128)(2,1)S(1)} %pad_maximum_fusion.1), channel_id=1, source_target_pairs={{0,1},{1,2},{2,3},{3,4},{4,5},{5,6},{6,7},{8,9},{9,10},{10,11},{11... | collective-permute-start | bytes 466952 | tf_op jit(solution)/shard_map/ppermute | solution.py:584
  170.3 8.2 %copy-start.4 = (bf16[2,512,768]{2,1,0:T(8,128)(2,1)S(1)}, bf16[2,512,768]{2,1,0:T(8,128)(2,1)}, u32[]{:S(2)}) copy-start(bf16[2,512,768]{2,1,0:T(8,128)(2,1)} %pad_maximum_fusion.weight_hbm) | copy-start | bytes 4718596
  170.3 8.2 %copy-start.9 = (f32[2,128]{1,0:T(2,128)S(1)}, f32[2,128]{1,0:T(2,128)}, u32[]{:S(2)}) copy-start(f32[2,128]{1,0:T(2,128)} %bias_ref.3) | copy-start | bytes 3076

commit v6 on v5

--- a/solution.py
+++ b/solution.py
@@ -111,48 +111,59 @@
     )(pair, gain, shift, weight, bias)
 
 
-def plane_kernel(received_ref, out_ref, hold_ref, in_sems, out_sems):
-    parts = [slice(k * NR // 4, (k + 1) * NR // 4) for k in range(4)]
-    inward = [
-        pltpu.make_async_copy(received_ref.at[part, :, 0], hold_ref.at[part], in_sems.at[k])
-        for k, part in enumerate(parts)
+SPLIT_VMEM = 16
+PRODUCT_VMEM = 62
+
+
+def split_kernel(
+    received_ref, cells_out_ref, plane_out_ref, cells_ref, plane_ref, cell_sems, plane_sem, out_sems
+):
+    cells = [
+        pltpu.make_async_copy(
+            received_ref.at[col, e, :, 1, side * 32 : side * 32 + 32, :],
+            cells_ref.at[:, side, col, e * 32 : e * 32 + 32, :],
+            cell_sems.at[col, e, side],
+        )
+        for col in range(NC)
+        for e in range(2)
+        for side in range(2)
     ]
-    outward = [
-        pltpu.make_async_copy(hold_ref.at[part], out_ref.at[part], out_sems.at[k])
-        for k, part in enumerate(parts)
-    ]
-    for copy in inward:
+    own = pltpu.make_async_copy(received_ref.at[:, :, :, 0], plane_ref, plane_sem)
+    for copy in cells + [own]:
         copy.start()
-    for k in range(4):
-        inward[k].wait()
-        outward[k].start()
-    for copy in outward:
+    for copy in cells:
         copy.wait()
-
-
-def plane(received):
-    return pl.pallas_call(
-        plane_kernel,
-        out_shape=jax.ShapeDtypeStruct((NR, NC, ROWS, COLS), BF),
-        in_specs=[pl.BlockSpec(memory_space=pl.ANY)],
-        out_specs=pl.BlockSpec(memory_space=pl.ANY),
+    cells_out = pltpu.make_async_copy(cells_ref, cells_out_ref, out_sems.at[0])
+    cells_out.start()
+    own.wait()
+    plane_out = pltpu.make_async_copy(plane_ref, plane_out_ref, out_sems.at[1])
+    plane_out.start()
+    cells_out.wait()
+    plane_out.wait()
+
+
+def split(received):
+    anywhere = pl.BlockSpec(memory_space=pl.ANY)
+    half = NR // 2
+    return pl.pallas_call(
+        split_kernel,
+        out_shape=[jax.ShapeDtypeStruct((half, 2, NC, ROWS, COLS), BF)] * 2,
+        in_specs=[anywhere],
+        out_specs=[anywhere, anywhere],
         scratch_shapes=[
-            pltpu.VMEM((NR, NC, ROWS, COLS), BF),
-            pltpu.SemaphoreType.DMA((4,)),
-            pltpu.SemaphoreType.DMA((4,)),
-        ],
-        compiler_params=pltpu.CompilerParams(vmem_limit_bytes=PLANE_VMEM * MIB),
-        name="plane",
-    )(received)
-
-
-PLANE_VMEM = 16
-PRODUCT_VMEM = 60
+            pltpu.VMEM((half, 2, NC, ROWS, COLS), BF),
+            pltpu.VMEM((half, 2, NC, ROWS, COLS), BF),
+            pltpu.SemaphoreType.DMA((NC, 2, 2)),
+            pltpu.SemaphoreType.DMA(()),
+            pltpu.SemaphoreType.DMA((2,)),
+        ],
+        compiler_params=pltpu.CompilerParams(vmem_limit_bytes=SPLIT_VMEM * MIB),
+        name="split",
+    )(received.reshape(half, 2, NC, 2, ROWS, COLS))
 
 
 def product_kernel(
-    received_ref, other_ref, out_ref, lhs_ref, rhs_ref, result_ref, cells_ref,
-    lhs_sems, rhs_sems, cell_sems, out_sems, cell_out_sem,
+    own_ref, other_ref, out_ref, lhs_ref, rhs_ref, result_ref, lhs_sems, rhs_sems, out_sems
 ):
     half = NR // 2
 
@@ -161,30 +172,18 @@
 
     lhs = [
         pltpu.make_async_copy(
-            received_ref.at[:, side, col, 0],
-            lhs_ref.at[side, :, :, columns(col)],
-            lhs_sems.at[side, col],
+            own_ref.at[:, side, col], lhs_ref.at[side, :, :, columns(col)], lhs_sems.at[side, col]
         )
         for side in range(2)
         for col in range(NC)
     ]
     rhs = [
         pltpu.make_async_copy(
-            other_ref.at[:, col], rhs_ref.at[:, :, columns(col)], rhs_sems.at[col]
+            other_ref.at[:, :, col], rhs_ref.at[:, :, :, columns(col)], rhs_sems.at[col]
         )
         for col in range(NC)
     ]
-    cells = [
-        pltpu.make_async_copy(
-            received_ref.at[col, e, :, 1, side * 32 : side * 32 + 32, :],
-            cells_ref.at[:, side, col, e * 32 : e * 32 + 32, :],
-            cell_sems.at[col, e, side],
-        )
-        for col in range(NC)
-        for e in range(2)
-        for side in range(2)
-    ]
-    for copy in rhs + lhs + cells:
+    for copy in rhs + lhs:
         copy.start()
     for copy in rhs:
         copy.wait()
@@ -196,7 +195,7 @@
         for block in range(4):
             result = lax.dot_general(
                 own,
-                rhs_ref[4 * block : 4 * block + 4].reshape(256, NC * COLS),
+                rhs_ref[2 * block : 2 * block + 2].reshape(4 * ROWS, NC * COLS),
                 NT,
                 preferred_element_type=F32,
             ).astype(BF)
@@ -205,49 +204,43 @@
                     half, ROWS, COLS
                 )
         copy = pltpu.make_async_copy(
-            result_ref.at[side], out_ref.at[:, side, :, 0], out_sems.at[side]
+            result_ref.at[side], out_ref.at[:, side], out_sems.at[side]
         )
         copy.start()
         outs.append(copy)
-        if side == 0:
-            for moved in cells:
-                moved.wait()
-            copy = pltpu.make_async_copy(cells_ref, out_ref.at[:, :, :, 1], cell_out_sem)
-            copy.start()
-            outs.append(copy)
     for copy in outs:
         copy.wait()
 
 
-def product(received, other):
+def product(own, other):
     anywhere = pl.BlockSpec(memory_space=pl.ANY)
     half = NR // 2
     return pl.pallas_call(
         product_kernel,
-        out_shape=jax.ShapeDtypeStruct((half, 2, NC, 2, ROWS, COLS), BF),
+        out_shape=jax.ShapeDtypeStruct((half, 2, NC, ROWS, COLS), BF),
         in_specs=[anywhere, anywhere],
         out_specs=anywhere,
         scratch_shapes=[
             pltpu.VMEM((2, half, ROWS, NC * COLS), BF),
-            pltpu.VMEM((NR, ROWS, NC * COLS), BF),
+            pltpu.VMEM((half, 2, ROWS, NC * COLS), BF),
             pltpu.VMEM((2, half, NC, ROWS, COLS), BF),
-            pltpu.VMEM((half, 2, NC, ROWS, COLS), BF),
             pltpu.SemaphoreType.DMA((2, NC)),
             pltpu.SemaphoreType.DMA((NC,)),
-            pltpu.SemaphoreType.DMA((NC, 2, 2)),
             pltpu.SemaphoreType.DMA((2,)),
-            pltpu.SemaphoreType.DMA(()),
         ],
         compiler_params=pltpu.CompilerParams(vmem_limit_bytes=PRODUCT_VMEM * MIB),
+        cost_estimate=pl.CostEstimate(
+            flops=2 * 1024**3, bytes_accessed=6 * MIB, transcendentals=0
+        ),
         name="product",
-    )(received.reshape(half, 2, NC, 2, ROWS, COLS), other)
+    )(own, other)
 
 
 def gate_kernel(pair_ref, gain_ref, shift_ref, weight_ref, bias_ref, out_ref):
     cells = pair_ref[...].astype(F32).reshape(STEP * COLS, CH)
     normed = normalize(cells, gain_ref[...], shift_ref[...]).astype(BF)
     gate = jnp.dot(normed, weight_ref[...], preferred_element_type=F32) + bias_ref[...]
-    out_ref[...] = sigmoid(gate).reshape(STEP, COLS, CH)
+    out_ref[...] = sigmoid(gate).astype(BF).reshape(STEP, COLS, CH)
 
 
 def gates(pair, gain, shift, weight, bias):
@@ -256,65 +249,101 @@
     return pl.pallas_call(
         gate_kernel,
         grid=(ROWS // STEP,),
-        out_shape=jax.ShapeDtypeStruct((ROWS, COLS, CH), F32),
+        out_shape=jax.ShapeDtypeStruct((ROWS, COLS, CH), BF),
         in_specs=[block, whole(1, CH), whole(1, CH), whole(CH, CH), whole(1, CH)],
         out_specs=block,
         compiler_params=pltpu.CompilerParams(vmem_limit_bytes=24 * MIB),
         cost_estimate=pl.CostEstimate(
-            flops=2 * ROWS * COLS * CH * CH, bytes_accessed=6 * ROWS * COLS * CH, transcendentals=ROWS * COLS * CH
+            flops=2 * ROWS * COLS * CH * CH, bytes_accessed=4 * ROWS * COLS * CH, transcendentals=ROWS * COLS * CH
         ),
         name="gates",
     )(pair, gain, shift, weight, bias)
 
 
+PITCH = 24
+MGROUP = 8
+
+
+def mirror_kernel(
+    mirror_ref, gain_ref, shift_ref, weight_ref, bias_ref, out_ref, gate_ref, cells_ref
+):
+    for e in range(2):
+        for j in range(64):
+            at = (e * 64 + j) * PITCH
+            cells_ref[at : at + STEP, :] = mirror_ref[j, 0, e, 0].astype(F32)
+    for part in range(STEP // MGROUP):
+        rows = [
+            cells_ref[pl.ds(part * MGROUP + k, COLS, stride=PITCH), :] for k in range(MGROUP)
+        ]
+        cells = jnp.concatenate(rows, axis=0)
+        here = slice(part * MGROUP, (part + 1) * MGROUP)
+        out_ref[here] = cells.astype(BF).reshape(MGROUP, COLS, CH)
+        normed = normalize(cells, gain_ref[...], shift_ref[...]).astype(BF)
+        gate = jnp.dot(normed, weight_ref[...], preferred_element_type=F32) + bias_ref[...]
+        gate_ref[here] = sigmoid(gate).astype(BF).reshape(MGROUP, COLS, CH)
+
+
+def mirror_gates(mirrored, gain, shift, weight, bias):
+    whole = lambda *shape: pl.BlockSpec(shape, lambda s: (0,) * len(shape))
+    block = pl.BlockSpec((STEP, COLS, CH), lambda s: (s, 0, 0))
+    return pl.pallas_call(
+        mirror_kernel,
+        grid=(ROWS // STEP,),
+        out_shape=[
+            jax.ShapeDtypeStruct((ROWS, COLS, CH), BF),
+            jax.ShapeDtypeStruct((ROWS, COLS, CH), BF),
+        ],
+        in_specs=[
+            pl.BlockSpec((64, 1, 2, 1, STEP, CH), lambda s: (0, s // 2, 0, s % 2, 0, 0)),
+            whole(1, CH),
+            whole(1, CH),
+            whole(CH, CH),
+            whole(1, CH),
+        ],
+        out_specs=[block, block],
+        scratch_shapes=[pltpu.VMEM((COLS * PITCH, CH), F32)],
+        compiler_params=pltpu.CompilerParams(vmem_limit_bytes=24 * MIB),
+        cost_estimate=pl.CostEstimate(
+            flops=2 * ROWS * COLS * CH * CH, bytes_accessed=8 * ROWS * COLS * CH, transcendentals=ROWS * COLS * CH
+        ),
+        name="mirror_gates",
+    )(mirrored.reshape(64, 2, 2, 2, STEP, CH), gain, shift, weight, bias)
+
+
 USTEP = 16
 UNROLL_U = 1
 UGROUP = 8
-PITCH = 72
+UPDATE_VMEM = 50
 
 
 def update_kernel(
-    pair_ref, own_gate_ref, tri_ref, mirror_ref, gain_ref, shift_ref, gate_ref, gate_bias_ref,
-    out_weight_ref, out_bias_ref, sym_ref, cells_ref, lay_ref,
+    pair_ref, own_gate_ref, cells_ref, gate_ref, tri_ref, out_weight_ref, out_bias_ref, sym_ref,
+    lay_ref,
 ):
-    step = pl.program_id(0)
-
-    @pl.when(step == 0)
-    def _():
-        for d in range(128):
-            for e in range(2):
-                at = (e * 64 + d // 2) * PITCH + (d % 2) * 32
-                cells_ref[at : at + 32, :] = mirror_ref[d, 0, e * 32 : e * 32 + 32, :].astype(F32)
-
-    tri = tri_ref[:, :, :, 0].astype(F32)
+    tri = tri_ref[...].astype(F32)
     mean = jnp.mean(tri, axis=(0, 2), keepdims=True)
     centred = tri - mean
     spread = jnp.mean(centred * centred, axis=(0, 2), keepdims=True)
     lay_ref[...] = (centred * lax.rsqrt(spread + EPS)).reshape(2 * HID * USTEP, COLS)
+    size = UGROUP * COLS
+
+    def rows(ref, first):
+        return ref[pl.ds(first, UGROUP)].astype(F32).reshape(size, CH)
 
     def body(part, carry):
         first = part * UGROUP
-        change, cells = [], []
-        for k in range(UGROUP):
-            mid = lay_ref[pl.ds(first + k, 2 * HID, stride=USTEP), :].astype(BF)
-            change.append(
-                lax.dot_general(mid, out_weight_ref[...], TN, preferred_element_type=F32)
+        change = [
+            lax.dot_general(
+                lay_ref[pl.ds(first + k, 2 * HID, stride=USTEP), :].astype(BF),
+                out_weight_ref[...],
+                TN,
+                preferred_element_type=F32,
             )
-            cells.append(
-                cells_ref[pl.ds(step * USTEP + first + k, COLS, stride=PITCH), :]
-            )
+            for k in range(UGROUP)
+        ]
         change = jnp.concatenate(change, axis=0) + out_bias_ref[...]
-        cells = jnp.concatenate(cells, axis=0)
-        size = UGROUP * COLS
-        own = (
-            pair_ref[pl.ds(first, UGROUP)].astype(F32).reshape(size, CH)
-            + own_gate_ref[pl.ds(first, UGROUP)].reshape(size, CH) * change[:, :CH]
-        )
-        normed = normalize(cells, gain_ref[...], shift_ref[...]).astype(BF)
-        gate = sigmoid(
-            jnp.dot(normed, gate_ref[...], preferred_element_type=F32) + gate_bias_ref[...]
-        )
-        mirrored = cells + gate * change[:, CH:]
+        own = rows(pair_ref, first) + rows(own_gate_ref, first) * change[:, :CH]
+        mirrored = rows(cells_ref, first) + rows(gate_ref, first) * change[:, CH:]
         total = own.astype(BF).astype(F32) + mirrored.astype(BF).astype(F32)
         sym_ref[pl.ds(first, UGROUP)] = (total * 0.5).astype(BF).reshape(UGROUP, COLS, CH)
         return carry
@@ -322,10 +351,8 @@
     lax.fori_loop(0, USTEP // UGROUP, body, 0, unroll=UNROLL_U)
 
 
-def update(pair, own_gate, received, gain, shift, gate, gate_bias, out_weight, out_bias):
+def update(pair, own_gate, cells, gate, returned, out_weight, out_bias):
     whole = lambda *shape: pl.BlockSpec(shape, lambda s: (0,) * len(shape))
-    tri = received.reshape(8, 2, 8, 2, ROWS, COLS)
-    cells = received.reshape(128, 2, ROWS, COLS)
     block = pl.BlockSpec((USTEP, COLS, CH), lambda s: (s, 0, 0))
     return pl.pallas_call(
         update_kernel,
@@ -334,23 +361,17 @@
         in_specs=[
             block,
             block,
-            pl.BlockSpec((8, 2, 8, 1, USTEP, COLS), lambda s: (0, 0, 0, 0, s, 0)),
-            pl.BlockSpec((128, 1, ROWS, COLS), lambda s: (0, 1, 0, 0)),
-            whole(1, CH),
-            whole(1, CH),
-            whole(CH, CH),
-            whole(1, CH),
+            block,
+            block,
+            pl.BlockSpec((8, 2, 8, USTEP, COLS), lambda s: (0, 0, 0, s, 0)),
             whole(2 * HID, 2 * CH),
             whole(1, 2 * CH),
         ],
         out_specs=block,
-        scratch_shapes=[
-            pltpu.VMEM((COLS * PITCH, CH), F32),
-            pltpu.VMEM((2 * HID * USTEP, COLS), F32),
-        ],
-        compiler_params=pltpu.CompilerParams(vmem_limit_bytes=48 * MIB),
+        scratch_shapes=[pltpu.VMEM((2 * HID * USTEP, COLS), F32)],
+        compiler_params=pltpu.CompilerParams(vmem_limit_bytes=UPDATE_VMEM * MIB),
         name="update",
-    )(pair, own_gate, tri, cells, gain, shift, gate, gate_bias, out_weight, out_bias)
+    )(pair, own_gate, cells, gate, returned.reshape(8, 2, 8, ROWS, COLS), out_weight, out_bias)
 
 
 def output_weight(weight, bias, gain, shift):
@@ -590,19 +611,22 @@
 ):
     gain, shift = norm_gain[None], norm_shift[None]
     sent = factors(pair, gain, shift, proj_weight, proj_bias)
-    received = lax.all_to_all(
-        sent.reshape(128, 2, ROWS, COLS), ("row", "col"), split_axis=0, concat_axis=0, tiled=True
-    ).reshape(NR, NC, 2, ROWS, COLS)
-    other = lax.ppermute(plane(received), "row", [(i, i ^ 1) for i in range(NR)])
-    back = product(received, other)
-    returned = lax.all_to_all(
-        back.reshape(128, 2, ROWS, COLS), ("row", "col"), split_axis=0, concat_axis=0, tiled=True
+    exchange = lambda v: lax.all_to_all(
+        v, ("row", "col"), split_axis=0, concat_axis=0, tiled=True
     )
+    received = exchange(sent.reshape(128, 2, ROWS, COLS))
+    cells, own = split(received)
+    mirrored = exchange(cells.reshape(128, ROWS, COLS))
+    other = lax.ppermute(own, "row", [(i, i ^ 1) for i in range(NR)])
+    returned = exchange(product(own, other).reshape(128, ROWS, COLS))
     gate, gate_bias = proj_weight[:, 4 * HID :], proj_bias[None, 4 * HID :]
     paired = jnp.stack([paired_weight(convolution_weight[0]), paired_weight(convolution_weight[1])])
     gate, paired = lax.optimization_barrier((gate, paired))
     sym = update(
-        pair, gates(pair, gain, shift, gate, gate_bias), returned, gain, shift, gate, gate_bias,
+        pair,
+        gates(pair, gain, shift, gate, gate_bias),
+        *mirror_gates(mirrored, gain, shift, gate, gate_bias),
+        returned,
         *output_weight(out_weight, out_bias, mid_gain, mid_shift),
     )
     top, bottom = neighbours(sym[:HALO], sym[ROWS - HALO :], "row")

time: 194 us -> 193 us (level)
  waiting for transfers between devices: 53.7 us -> 38.3 us
  starting transfers between devices: 22 us -> 30 us
  Pallas kernels: 44.6 us -> 48.8 us
    all_to_all x1 -> x2, waiting for transfers between devices: 41 us -> 30.3 us  [local(): lax.all_to_all(v, ('row', 'col'), split_axis=0, concat_axis=0, tiled=True)]
    all_to_all x1 -> x2, starting transfers between devices: 8.01 us -> 15.6 us  [local(): lax.all_to_all(v, ('row', 'col'), split_axis=0, concat_axis=0, tiled=True)]
    pallas_call x1 -> x2, Pallas kernels: 0.41 us -> 7.47 us  [the longest x1 5.02 us: mirror_gates(): pl.pallas_call(mirror_kernel, grid=(ROWS // STEP,), out_shape=[jax.ShapeD...]
    ppermute x1, waiting for transfers between devices: 4.16 us -> 0.01 us  [local(): other = lax.ppermute(own, 'row', [(i, i ^ 1) for i in range(NR)])]
    pallas_call x1, Pallas kernels: 9.92 us -> 7.46 us  [update(): pl.pallas_call(update_kernel, grid=(ROWS // USTEP,), out_shape=jax.ShapeD...]
  transfers between devices with their start and end apart: 6 -> 7, of which waited for: 5 -> 5; matrix products, arithmetic and copies ran while one was open for 2% -> 4% of each run, Pallas kernels for 3% -> 9%
where the time goes in v6:
time: 193 us; the launch traced here: 192 us
  blocking collectives  61.4 us (32%)
  Pallas kernels  48.8 us (25%)
  waiting for transfers between devices  38.3 us (20%)
  starting transfers between devices  30 us (16%)
  local copies, waits for them, and re-layouts  9.67 us (5%)
  other arithmetic  3.15 us (2%)
    all_to_all x1, blocking collectives, local(): lax.all_to_all(v, ('row', 'col'), split_axis=0, concat_axis=0, tiled=True)  61.4 us
    all_to_all x2, waiting for transfers between devices, local(): lax.all_to_all(v, ('row', 'col'), split_axis=0, concat_axis=0, tiled=True)  30.3 us
    all_to_all x2, starting transfers between devices, local(): lax.all_to_all(v, ('row', 'col'), split_axis=0, concat_axis=0, tiled=True)  15.6 us
    pallas_call x1, Pallas kernels, convolutions(): pl.pallas_call(convolution_kernel, out_shape=jax.ShapeDtypeStruct((ROWS,...  14.2 us
    ppermute x2, starting transfers between devices, neighbours(): lax.ppermute(low_strip, axis, backward)  10.3 us
    pallas_call x1, Pallas kernels, factors(): pl.pallas_call(factor_kernel, grid=(steps,), out_shape=jax.ShapeDtypeStru...  7.71 us
    pallas_call x1, Pallas kernels, update(): pl.pallas_call(update_kernel, grid=(ROWS // USTEP,), out_shape=jax.ShapeD...  7.46 us
    ppermute x2, waiting for transfers between devices, neighbours(): lax.ppermute(high_strip, axis, forward)  6.25 us
  transfers between devices with their start and end apart: 7, of which 5 were waited for; matrix products, arithmetic and copies ran while one was open for 4% of the time, Pallas kernels for 9%

profile of v6, /device:TPU:10, one launch (start us, length us, event | category | flops | bytes accessed | tf_op | source)
XLA Modules:
  0.0 191.9 jit_solution(612698390737826212)
XLA Ops:
  0.0 7.7 %factors.1 = bf16[8,2,4,2,2,64,128]{6,5,4,3,2,1,0:T(8,128)(2,1)} custom-call(bf16[64,128,128]{2,1,0:T(8,128)(2,1)} %pair_ref.5, f32[1,128]{1,0:T(1,128)} %bitcast.32, f32[1,128]{1,0:T(1,128)} %bitcast.35, bf16[128,384]{1,0:T(8,128)(2,1)} %weight_ref.1, f32[384]{0:T(512)} %bias_ref.2), custom_call_target="tpu_custom_call" | custom-call | tf_op jit(solution)/shard_map/factors/pallas_call | solution.py:90
  7.7 61.4 %all_to_all.15 = bf16[128,2,64,128]{3,2,1,0:T(8,128)(2,1)S(1)} all-to-all(bf16[128,2,64,128]{3,2,1,0:T(8,128)(2,1)} %bitcast.39), channel_id=1, replica_groups=mesh['row'=16,'col'=8] {'row','col'}, dimensions={0} | all-to-all | bytes 8388608 | tf_op jit(solution)/shard_map/all_to_all | solution.py:614
  69.1 2.4 %split.1 = (bf16[8,2,8,64,128]{4,3,2,1,0:T(8,128)(2,1)}, bf16[8,2,8,64,128]{4,3,2,1,0:T(8,128)(2,1)S(1)}) custom-call(bf16[8,2,8,2,64,128]{5,4,3,2,1,0:T(8,128)(2,1)S(1)} %bitcast.30), custom_call_target="tpu_custom_call" | custom-call | tf_op jit(solution)/shard_map/split/pallas_call | solution.py:148
  71.6 0.0 copy-start.10
  71.6 0.1 collective-permute-start
  71.7 1.3 copy-done.10
  72.9 7.8 %all-to-all-start.1 = ((bf16[128,64,128]{2,1,0:T(8,128)(2,1)}), bf16[128,64,128]{2,1,0:T(8,128)(2,1)}, u32[]{:S(2)}, u32[]{:S(2)}) async-start(bf16[128,64,128]{2,1,0:T(8,128)(2,1)} %bitcast.19), calls=%async_computation.1 | async-start | bytes 4194304 | tf_op jit(solution)/shard_map/all_to_all | solution.py:614
  80.8 0.0 collective-permute-done.other_ref
  80.8 5.8 %product.1 = bf16[8,2,8,64,128]{4,3,2,1,0:T(8,128)(2,1)} custom-call(bf16[8,2,8,64,128]{4,3,2,1,0:T(8,128)(2,1)} %copy-done.10, bf16[8,2,8,64,128]{4,3,2,1,0:T(8,128)(2,1)} %collective-permute-done.other_ref), custom_call_target="tpu_custom_call" | custom-call | flops 2147483648 | bytes 6291456 | tf_op jit(solution)/shard_map/product/pallas_call | solution.py:218
  86.5 22.3 %all-to-all-done.1 = bf16[128,64,128]{2,1,0:T(8,128)(2,1)} async-done(((bf16[128,64,128]{2,1,0:T(8,128)(2,1)}), bf16[128,64,128]{2,1,0:T(8,128)(2,1)}, u32[]{:S(2)}, u32[]{:S(2)}) %all-to-all-start.1) | async-done | bytes 2097184 | tf_op jit(solution)/shard_map/all_to_all | solution.py:614
  108.8 0.0 copy-start.11
  108.8 7.8 %all-to-all-start.2 = ((bf16[128,64,128]{2,1,0:T(8,128)(2,1)}), bf16[128,64,128]{2,1,0:T(8,128)(2,1)}, u32[]{:S(2)}, u32[]{:S(2)}) async-start(bf16[128,64,128]{2,1,0:T(8,128)(2,1)} %bitcast.42), calls=%async_computation.2 | async-start | bytes 4194304 | tf_op jit(solution)/shard_map/all_to_all | solution.py:614
  116.7 0.8 slice.36.weight_ref
  117.4 0.0 copy-done.11
  117.5 0.2 copy.20
  117.7 0.1 fusion.5
  117.8 1.2 copy.21
  119.0 0.2 copy.18
  119.2 0.1 fusion.4
  119.3 0.0 copy-start.12
  119.3 0.0 copy-start.13
  119.3 0.0 copy-start.14
  119.3 0.0 copy-start.15
  119.4 0.0 copy-start
  119.4 0.0 copy-start.5
  119.4 0.0 copy-start.6
  119.4 1.2 copy.19
  120.6 2.7 %pad_maximum_fusion.weight_hbm = bf16[2,512,768]{2,1,0:T(8,128)(2,1)} fusion(bf16[1,512,768]{2,1,0:T(8,128)(2,1)} %bitcast.40, bf16[1,512,768]{2,1,0:T(8,128)(2,1)} %bitcast.41), kind=kLoop, calls=%fused_computation.6 | loop fusion | flops 786432 | bytes 3145728 | tf_op jit(solution)/shard_map/stack | solution.py:623
  123.3 0.0 copy-done.12
  123.3 0.0 copy-done.13
  123.3 0.0 copy-done.14
  123.3 0.1 fusion.10
  123.4 0.0 copy-done.15
  123.4 0.7 slice_bitcast_fusion.bias_ref
  124.1 0.0 copy-done
  124.1 0.0 copy-done.5
  124.1 0.0 copy-done.6
  124.1 3.5 %gates.1.own_gate_ref = bf16[64,128,128]{2,1,0:T(8,128)(2,1)S(1)} custom-call(bf16[64,128,128]{2,1,0:T(8,128)(2,1)S(1)} %copy-done, f32[1,128]{1,0:T(1,128)S(1)} %bitcast.33, f32[1,128]{1,0:T(1,128)S(1)} %bitcast.36, bf16[128,128]{1,0:T(8,128)(2,1)S(1)} %slice.36.weight_ref, f32[1,128]{1,0:T(1,128)S(1)} %slice_bitcast_fusion.bias_ref), custom_call_target="tpu_custom_call" | custom-call | flops 268435456 | bytes 4194304 | tf_op jit(solution)/shard_map/gates/pallas_call | solution.py:249
  127.6 0.0 copy-start.1
  127.6 1.3 copy-done.1
  128.9 5.0 %mirror_gates.1 = (bf16[64,128,128]{2,1,0:T(8,128)(2,1)S(1)}, bf16[64,128,128]{2,1,0:T(8,128)(2,1)S(1)}) custom-call(bf16[64,2,2,2,16,128]{5,4,3,2,1,0:T(8,128)(2,1)} %bitcast.20.mirror_ref, f32[1,128]{1,0:T(1,128)S(1)} %bitcast.34, f32[1,128]{1,0:T(1,128)S(1)} %bitcast.37, bf16[128,128]{1,0:T(8,128)(2,1)S(1)} %slice.36.weight_ref, ...), custom_call_target="tpu_custom_call" | custom-call | flops 268435456 | bytes 8388608 | tf_op jit(solution)/shard_map/mirror_gates/pallas_call | solution.py:289
  133.9 0.0 copy-start.3
  134.0 1.3 copy-done.3
  135.2 0.0 copy-start.4
  135.3 1.4 copy-done.4
  136.6 8.1 %all-to-all-done.2 = bf16[128,64,128]{2,1,0:T(8,128)(2,1)} async-done(((bf16[128,64,128]{2,1,0:T(8,128)(2,1)}), bf16[128,64,128]{2,1,0:T(8,128)(2,1)}, u32[]{:S(2)}, u32[]{:S(2)}) %all-to-all-start.2) | async-done | bytes 2097184 | tf_op jit(solution)/shard_map/all_to_all | solution.py:614
  144.7 0.0 copy-start.7
  144.7 0.0 copy-start.8
  144.7 7.5 %update.1.sym_ref = bf16[64,128,128]{2,1,0:T(8,128)(2,1)S(1)} custom-call(bf16[64,128,128]{2,1,0:T(8,128)(2,1)} %pair_ref.5, bf16[64,128,128]{2,1,0:T(8,128)(2,1)} %copy-done.1, bf16[64,128,128]{2,1,0:T(8,128)(2,1)} %copy-done.3, bf16[64,128,128]{2,1,0:T(8,128)(2,1)} %copy-done.4, bf16[8,2,8,64,128]{4,3,2,1,0:T(8,128)(2,1)} %bitcast.22.tri_ref, ...), custom_call_target="tpu_custom_call" | custom-call | tf_op jit(solution)/shard_map/update/pallas_call | solution.py:357
  152.2 1.9 %collective-permute-start.1 = (bf16[6,128,128]{2,1,0:T(8,128)(2,1)S(1)}, bf16[6,128,128]{2,1,0:T(8,128)(2,1)S(1)}, u32[]{:S(2)}, u32[]{:S(2)}) collective-permute-start(bf16[6,128,128]{2,1,0:T(8,128)(2,1)S(1)} %get-tuple-element.20), channel_id=1, source_target_pairs={{0,8},{8,16},{16,24},{24,32},{32,40},{40,48},{48,56},{56,64},{64,7... | collective-permute-start | bytes 589832 | tf_op jit(solution)/shard_map/ppermute | solution.py:605
  154.1 6.0 %collective-permute-start.2 = (bf16[6,128,128]{2,1,0:T(8,128)(2,1)S(1)}, bf16[6,128,128]{2,1,0:T(8,128)(2,1)S(1)}, u32[]{:S(2)}, u32[]{:S(2)}) collective-permute-start(bf16[6,128,128]{2,1,0:T(8,128)(2,1)S(1)} %get-tuple-element.19), channel_id=1, source_target_pairs={{8,0},{16,8},{24,16},{32,24},{40,32},{48,40},{56,48},{64,56},{72,6... | collective-permute-start | bytes 589832 | tf_op jit(solution)/shard_map/ppermute | solution.py:605
  160.2 1.4 collective-permute-done.1.top_ref
  161.6 1.7 collective-permute-done.2.bottom_ref
  163.4 4.2 %collective-permute-start.4 = (bf16[76,8,128]{2,1,0:T(8,128)(2,1)S(1)}, bf16[76,8,128]{2,1,0:T(8,128)(2,1)S(1)}, u32[]{:S(2)}, u32[]{:S(2)}) collective-permute-start(bf16[76,8,128]{2,1,0:T(8,128)(2,1)S(1)} %pad_maximum_fusion.2), channel_id=1, source_target_pairs={{1,0},{2,1},{3,2},{4,3},{5,4},{6,5},{7,6},{9,8},{10,9},{11,10},{12... | collective-permute-start | bytes 466952 | tf_op jit(solution)/shard_map/ppermute | solution.py:605
  167.7 2.1 %collective-permute-start.3 = (bf16[76,8,128]{2,1,0:T(8,128)(2,1)S(1)}, bf16[76,8,128]{2,1,0:T(8,128)(2,1)S(1)}, u32[]{:S(2)}, u32[]{:S(2)}) collective-permute-start(bf16[76,8,128]{2,1,0:T(8,128)(2,1)S(1)} %pad_maximum_fusion.1), channel_id=1, source_target_pairs={{0,1},{1,2},{2,3},{3,4},{4,5},{5,6},{6,7},{8,9},{9,10},{10,11},{11... | collective-permute-start | bytes 466952 | tf_op jit(solution)/shard_map/ppermute | solution.py:605
  169.8 0.1 pad_add_fusion.place_ref
  169.9 0.0 copy-done.7
  169.9 0.0 copy-done.8
  169.9 2.7 %activations.1.act_ref = bf16[64,128,128]{2,1,0:T(8,128)(2,1)S(1)} custom-call(bf16[64,128,128]{2,1,0:T(8,128)(2,1)S(1)} %update.1.sym_ref, f32[2,128]{1,0:T(2,128)S(1)} %copy-done.7, f32[2,128]{1,0:T(2,128)S(1)} %copy-done.8), custom_call_target="tpu_custom_call" | custom-call | flops 16777216 | bytes 4194304 | tf_op jit(solution)/shard_map/activations/pallas_call | solution.py:396
  172.6 0.0 collective-permute-done.4.high_ref
  172.6 4.9 %collective-permute-done.3.low_ref = bf16[76,8,128]{2,1,0:T(8,128)(2,1)S(1)} collective-permute-done((bf16[76,8,128]{2,1,0:T(8,128)(2,1)S(1)}, bf16[76,8,128]{2,1,0:T(8,128)(2,1)S(1)}, u32[]{:S(2)}, u32[]{:S(2)}) %collective-permute-start.3) | collective-permute-done | bytes 155680 | tf_op jit(solution)/shard_map/ppermute | solution.py:605
  177.5 0.0 copy-done.2
  177.5 0.0 copy-done.9
  177.5 14.2 %convolutions.1 = bf16[64,128,128]{2,1,0:T(8,128)(2,1)} custom-call(s32[2]{0:T(128)S(1)} %pad_add_fusion.place_ref, bf16[64,128,128]{2,1,0:T(8,128)(2,1)S(1)} %update.1.sym_ref, bf16[64,128,128]{2,1,0:T(8,128)(2,1)S(1)} %activations.1.act_ref, bf16[6,128,128]{2,1,0:T(8,128)(2,1)S(1)} %collective-permute-done.1.top_ref, ...), custom_call_target="tpu_custom_call" | custom-call | tf_op jit(solution)/shard_map/convolutions/pallas_call | solution.py:569
  (12 shorter events, 0.2 us)
Async XLA Ops:
  71.6 1.4 copy-start.10
  71.6 9.2 %collective-permute-start = (bf16[8,2,8,64,128]{4,3,2,1,0:T(8,128)(2,1)S(1)}, bf16[8,2,8,64,128]{4,3,2,1,0:T(8,128)(2,1)}, u32[]{:S(2)}, u32[]{:S(2)}) collective-permute-start(bf16[8,2,8,64,128]{4,3,2,1,0:T(8,128)(2,1)S(1)} %get-tuple-element.15.own_ref), channel_id=1, source_target_pairs={{0,8},{8,0},{16,24},{24,16},{32,40},{40,32},{48,56},{56,48},{64,72... | collective-permute-start | bytes 6291464 | tf_op jit(solution)/shard_map/ppermute | solution.py:620
  72.9 35.9 %all-to-all-start.1 = ((bf16[128,64,128]{2,1,0:T(8,128)(2,1)}), bf16[128,64,128]{2,1,0:T(8,128)(2,1)}, u32[]{:S(2)}, u32[]{:S(2)}) async-start(bf16[128,64,128]{2,1,0:T(8,128)(2,1)} %bitcast.19), calls=%async_computation.1 | async-start | bytes 4194304 | tf_op jit(solution)/shard_map/all_to_all | solution.py:614
  108.8 8.6 %copy-start.11 = (bf16[2,9,128,128]{3,2,1,0:T(8,128)(2,1)S(1)}, bf16[2,9,128,128]{3,2,1,0:T(8,128)(2,1)}, u32[]{:S(2)}) copy-start(bf16[2,9,128,128]{3,2,1,0:T(8,128)(2,1)} %param.24) | copy-start | bytes 1769476
  108.8 35.9 %all-to-all-start.2 = ((bf16[128,64,128]{2,1,0:T(8,128)(2,1)}), bf16[128,64,128]{2,1,0:T(8,128)(2,1)}, u32[]{:S(2)}, u32[]{:S(2)}) async-start(bf16[128,64,128]{2,1,0:T(8,128)(2,1)} %bitcast.42), calls=%async_computation.2 | async-start | bytes 4194304 | tf_op jit(solution)/shard_map/all_to_all | solution.py:614
  119.3 4.0 %copy-start.12 = (bf16[64,128]{1,0:T(8,128)(2,1)S(1)}, bf16[64,128]{1,0:T(8,128)(2,1)}, u32[]{:S(2)}) copy-start(bf16[64,128]{1,0:T(8,128)(2,1)} %param.20) | copy-start | bytes 49156
  119.3 4.0 %copy-start.13 = (f32[64]{0:T(128)S(1)}, f32[64]{0:T(128)}, u32[]{:S(2)}) copy-start(f32[64]{0:T(128)} %param.19) | copy-start | bytes 772
  119.3 4.0 %copy-start.14 = (f32[64]{0:T(128)S(1)}, f32[64]{0:T(128)}, u32[]{:S(2)}) copy-start(f32[64]{0:T(128)} %param.18) | copy-start | bytes 772
  119.3 4.0 %copy-start.15 = (f32[128]{0:T(128)S(1)}, f32[128]{0:T(128)}, u32[]{:S(2)}) copy-start(f32[128]{0:T(128)} %param.21) | copy-start | bytes 1540
  119.4 4.7 %copy-start = (bf16[64,128,128]{2,1,0:T(8,128)(2,1)S(1)}, bf16[64,128,128]{2,1,0:T(8,128)(2,1)}, u32[]{:S(2)}) copy-start(bf16[64,128,128]{2,1,0:T(8,128)(2,1)} %pair_ref.5) | copy-start | bytes 6291460
  119.4 4.7 %copy-start.5 = (f32[128]{0:T(128)S(1)}, f32[128]{0:T(128)}, u32[]{:S(2)}) copy-start(f32[128]{0:T(128)} %param.14) | copy-start | bytes 1540
  119.4 4.7 %copy-start.6 = (f32[128]{0:T(128)S(1)}, f32[128]{0:T(128)}, u32[]{:S(2)}) copy-start(f32[128]{0:T(128)} %param.15) | copy-start | bytes 1540
  127.6 1.3 copy-start.1
  133.9 1.3 copy-start.3
  135.2 1.4 copy-start.4
  144.7 25.2 %copy-start.7 = (f32[2,128]{1,0:T(2,128)S(1)}, f32[2,128]{1,0:T(2,128)}, u32[]{:S(2)}) copy-start(f32[2,128]{1,0:T(2,128)} %gain_ref.3) | copy-start | bytes 3076
  144.7 25.2 %copy-start.8 = (f32[2,128]{1,0:T(2,128)S(1)}, f32[2,128]{1,0:T(2,128)}, u32[]{:S(2)}) copy-start(f32[2,128]{1,0:T(2,128)} %shift_ref.3) | copy-start | bytes 3076
  152.2 9.4 %collective-permute-start.1 = (bf16[6,128,128]{2,1,0:T(8,128)(2,1)S(1)}, bf16[6,128,128]{2,1,0:T(8,128)(2,1)S(1)}, u32[]{:S(2)}, u32[]{:S(2)}) collective-permute-start(bf16[6,128,128]{2,1,0:T(8,128)(2,1)S(1)} %get-tuple-element.20), channel_id=1, source_target_pairs={{0,8},{8,16},{16,24},{24,32},{32,40},{40,48},{48,56},{56,64},{64,7... | collective-permute-start | bytes 589832 | tf_op jit(solution)/shard_map/ppermute | solution.py:605
  154.1 9.2 %collective-permute-start.2 = (bf16[6,128,128]{2,1,0:T(8,128)(2,1)S(1)}, bf16[6,128,128]{2,1,0:T(8,128)(2,1)S(1)}, u32[]{:S(2)}, u32[]{:S(2)}) collective-permute-start(bf16[6,128,128]{2,1,0:T(8,128)(2,1)S(1)} %get-tuple-element.19), channel_id=1, source_target_pairs={{8,0},{16,8},{24,16},{32,24},{40,32},{48,40},{56,48},{64,56},{72,6... | collective-permute-start | bytes 589832 | tf_op jit(solution)/shard_map/ppermute | solution.py:605
  163.4 9.2 %collective-permute-start.4 = (bf16[76,8,128]{2,1,0:T(8,128)(2,1)S(1)}, bf16[76,8,128]{2,1,0:T(8,128)(2,1)S(1)}, u32[]{:S(2)}, u32[]{:S(2)}) collective-permute-start(bf16[76,8,128]{2,1,0:T(8,128)(2,1)S(1)} %pad_maximum_fusion.2), channel_id=1, source_target_pairs={{1,0},{2,1},{3,2},{4,3},{5,4},{6,5},{7,6},{9,8},{10,9},{11,10},{12... | collective-permute-start | bytes 466952 | tf_op jit(solution)/shard_map/ppermute | solution.py:605
  167.7 9.8 %collective-permute-start.3 = (bf16[76,8,128]{2,1,0:T(8,128)(2,1)S(1)}, bf16[76,8,128]{2,1,0:T(8,128)(2,1)S(1)}, u32[]{:S(2)}, u32[]{:S(2)}) collective-permute-start(bf16[76,8,128]{2,1,0:T(8,128)(2,1)S(1)} %pad_maximum_fusion.1), channel_id=1, source_target_pairs={{0,1},{1,2},{2,3},{3,4},{4,5},{5,6},{6,7},{8,9},{9,10},{10,11},{11... | collective-permute-start | bytes 466952 | tf_op jit(solution)/shard_map/ppermute | solution.py:605
  169.9 7.6 %copy-start.2 = (bf16[2,512,768]{2,1,0:T(8,128)(2,1)S(1)}, bf16[2,512,768]{2,1,0:T(8,128)(2,1)}, u32[]{:S(2)}) copy-start(bf16[2,512,768]{2,1,0:T(8,128)(2,1)} %pad_maximum_fusion.weight_hbm) | copy-start | bytes 4718596
  169.9 7.6 %copy-start.9 = (f32[2,128]{1,0:T(2,128)S(1)}, f32[2,128]{1,0:T(2,128)}, u32[]{:S(2)}) copy-start(f32[2,128]{1,0:T(2,128)} %bias_ref.3) | copy-start | bytes 3076

commit v7 on v6

--- a/solution.py
+++ b/solution.py
@@ -111,55 +111,101 @@
     )(pair, gain, shift, weight, bias)
 
 
-SPLIT_VMEM = 16
+REGROUP_VMEM = 16
+PLANE_VMEM = 16
 PRODUCT_VMEM = 62
-
-
-def split_kernel(
-    received_ref, cells_out_ref, plane_out_ref, cells_ref, plane_ref, cell_sems, plane_sem, out_sems
-):
-    cells = [
-        pltpu.make_async_copy(
-            received_ref.at[col, e, :, 1, side * 32 : side * 32 + 32, :],
-            cells_ref.at[:, side, col, e * 32 : e * 32 + 32, :],
-            cell_sems.at[col, e, side],
-        )
+PIECES = 4
+
+
+def regroup_kernel(received_ref, out_ref, cells_ref, in_sems, out_sems):
+    inward = [
+        [
+            pltpu.make_async_copy(
+                received_ref.at[col, e, :, 1, side * 32 : side * 32 + 32, :],
+                cells_ref.at[:, side, col, e * 32 : e * 32 + 32, :],
+                in_sems.at[col, e, side],
+            )
+            for e in range(2)
+            for side in range(2)
+        ]
         for col in range(NC)
-        for e in range(2)
-        for side in range(2)
     ]
-    own = pltpu.make_async_copy(received_ref.at[:, :, :, 0], plane_ref, plane_sem)
-    for copy in cells + [own]:
+    for copies in inward:
+        for copy in copies:
+            copy.start()
+    outward = []
+    width = NC // PIECES
+    for piece in range(PIECES):
+        part = slice(piece * width, (piece + 1) * width)
+        for copies in inward[part]:
+            for copy in copies:
+                copy.wait()
+        copy = pltpu.make_async_copy(
+            cells_ref.at[:, :, part], out_ref.at[:, :, part], out_sems.at[piece]
+        )
         copy.start()
-    for copy in cells:
+        outward.append(copy)
+    for copy in outward:
         copy.wait()
-    cells_out = pltpu.make_async_copy(cells_ref, cells_out_ref, out_sems.at[0])
-    cells_out.start()
-    own.wait()
-    plane_out = pltpu.make_async_copy(plane_ref, plane_out_ref, out_sems.at[1])
-    plane_out.start()
-    cells_out.wait()
-    plane_out.wait()
-
-
-def split(received):
+
+
+def regroup(received):
     anywhere = pl.BlockSpec(memory_space=pl.ANY)
     half = NR // 2
     return pl.pallas_call(
-        split_kernel,
-        out_shape=[jax.ShapeDtypeStruct((half, 2, NC, ROWS, COLS), BF)] * 2,
+        regroup_kernel,
+        out_shape=jax.ShapeDtypeStruct((half, 2, NC, ROWS, COLS), BF),
         in_specs=[anywhere],
-        out_specs=[anywhere, anywhere],
+        out_specs=anywhere,
         scratch_shapes=[
             pltpu.VMEM((half, 2, NC, ROWS, COLS), BF),
+            pltpu.SemaphoreType.DMA((NC, 2, 2)),
+            pltpu.SemaphoreType.DMA((PIECES,)),
+        ],
+        compiler_params=pltpu.CompilerParams(vmem_limit_bytes=REGROUP_VMEM * MIB),
+        name="regroup",
+    )(received)
+
+
+def plane_kernel(received_ref, out_ref, hold_ref, in_sems, out_sems):
+    inward = [
+        pltpu.make_async_copy(
+            received_ref.at[2 * k : 2 * k + 2, :, :, 0], hold_ref.at[2 * k : 2 * k + 2], in_sems.at[k]
+        )
+        for k in range(4)
+    ]
+    outward = [
+        pltpu.make_async_copy(
+            hold_ref.at[2 * k : 2 * k + 2], out_ref.at[2 * k : 2 * k + 2], out_sems.at[k]
+        )
+        for k in range(4)
+    ]
+    for copy in inward:
+        copy.start()
+    for k in range(4):
+        inward[k].wait()
+        outward[k].start()
+    for copy in outward:
+        copy.wait()
+
+
+def plane(received):
+    anywhere = pl.BlockSpec(memory_space=pl.ANY)
+    half = NR // 2
+    return pl.pallas_call(
+        plane_kernel,
+        out_shape=jax.ShapeDtypeStruct((half, 2, NC, ROWS, COLS), BF),
+        in_specs=[anywhere],
+        out_specs=anywhere,
+        scratch_shapes=[
             pltpu.VMEM((half, 2, NC, ROWS, COLS), BF),
-            pltpu.SemaphoreType.DMA((NC, 2, 2)),
-            pltpu.SemaphoreType.DMA(()),
-            pltpu.SemaphoreType.DMA((2,)),
-        ],
-        compiler_params=pltpu.CompilerParams(vmem_limit_bytes=SPLIT_VMEM * MIB),
-        name="split",
-    )(received.reshape(half, 2, NC, 2, ROWS, COLS))
+            pltpu.SemaphoreType.DMA((4,)),
+            pltpu.SemaphoreType.DMA((4,)),
+        ],
+        compiler_params=pltpu.CompilerParams(vmem_limit_bytes=PLANE_VMEM * MIB),
+        cost_estimate=pl.CostEstimate(flops=0, bytes_accessed=4 * MIB, transcendentals=0),
+        name="plane",
+    )(received)
 
 
 def product_kernel(
@@ -312,7 +358,7 @@
 
 USTEP = 16
 UNROLL_U = 1
-UGROUP = 8
+UGROUP = 16
 UPDATE_VMEM = 50
 
 
@@ -413,7 +459,7 @@
 FIRST_TALL = ROWS + 2 * SECOND_DILATION
 FIRST_WIDE = COLS + 2 * SIDE
 GROUP_B, GROUP_C = 4, 8
-INNER_B, SLOTS_C = 9, 2
+INNER_B, SLOTS_C = 18, 4
 CONV_VMEM = 40
 
 
@@ -615,8 +661,10 @@
         v, ("row", "col"), split_axis=0, concat_axis=0, tiled=True
     )
     received = exchange(sent.reshape(128, 2, ROWS, COLS))
-    cells, own = split(received)
+    received = received.reshape(NR // 2, 2, NC, 2, ROWS, COLS)
+    cells = regroup(received)
     mirrored = exchange(cells.reshape(128, ROWS, COLS))
+    own = plane(lax.optimization_barrier((received, cells))[0])
     other = lax.ppermute(own, "row", [(i, i ^ 1) for i in range(NR)])
     returned = exchange(product(own, other).reshape(128, ROWS, COLS))
     gate, gate_bias = proj_weight[:, 4 * HID :], proj_bias[None, 4 * HID :]

time: 193 us -> 192 us (level)
  no operation moved by 1% of the time
where the time goes in v7:
time: 192 us; the launch traced here: 191 us
  blocking collectives  61.4 us (32%)
  Pallas kernels  48.1 us (25%)
  waiting for transfers between devices  38.4 us (20%)
  starting transfers between devices  30.1 us (16%)
  local copies, waits for them, and re-layouts  9.68 us (5%)
  other arithmetic  3.15 us (2%)
    all_to_all x1, blocking collectives, local(): lax.all_to_all(v, ('row', 'col'), split_axis=0, concat_axis=0, tiled=True)  61.4 us
    all_to_all x2, waiting for transfers between devices, local(): lax.all_to_all(v, ('row', 'col'), split_axis=0, concat_axis=0, tiled=True)  30.4 us
    all_to_all x2, starting transfers between devices, local(): lax.all_to_all(v, ('row', 'col'), split_axis=0, concat_axis=0, tiled=True)  15.7 us
    pallas_call x1, Pallas kernels, convolutions(): pl.pallas_call(convolution_kernel, out_shape=jax.ShapeDtypeStruct((ROWS,...  13.9 us
    ppermute x2, starting transfers between devices, neighbours(): lax.ppermute(low_strip, axis, backward)  10.3 us
    pallas_call x1, Pallas kernels, factors(): pl.pallas_call(factor_kernel, grid=(steps,), out_shape=jax.ShapeDtypeStru...  7.74 us
    pallas_call x1, Pallas kernels, update(): pl.pallas_call(update_kernel, grid=(ROWS // USTEP,), out_shape=jax.ShapeD...  7.17 us
    ppermute x2, waiting for transfers between devices, neighbours(): lax.ppermute(high_strip, axis, forward)  6.25 us
  transfers between devices with their start and end apart: 7, of which 5 were waited for; matrix products, arithmetic and copies ran while one was open for 4% of the time, Pallas kernels for 9%

profile of v7, /device:TPU:10, one launch (start us, length us, event | category | flops | bytes accessed | tf_op | source)
XLA Modules:
  0.0 191.3 jit_solution(2893599981108756711)
XLA Ops:
  0.0 7.7 %factors.1 = bf16[8,2,4,2,2,64,128]{6,5,4,3,2,1,0:T(8,128)(2,1)} custom-call(bf16[64,128,128]{2,1,0:T(8,128)(2,1)} %pair_ref.5, f32[1,128]{1,0:T(1,128)} %bitcast.33, f32[1,128]{1,0:T(1,128)} %bitcast.36, bf16[128,384]{1,0:T(8,128)(2,1)} %weight_ref.1, f32[384]{0:T(512)} %bias_ref.2), custom_call_target="tpu_custom_call" | custom-call | tf_op jit(solution)/shard_map/factors/pallas_call | solution.py:90
  7.7 61.4 %all_to_all.15 = bf16[128,2,64,128]{3,2,1,0:T(8,128)(2,1)S(1)} all-to-all(bf16[128,2,64,128]{3,2,1,0:T(8,128)(2,1)} %bitcast.40), channel_id=1, replica_groups=mesh['row'=16,'col'=8] {'row','col'}, dimensions={0} | all-to-all | bytes 8388608 | tf_op jit(solution)/shard_map/all_to_all | solution.py:660
  69.2 2.0 %regroup.1 = bf16[8,2,8,64,128]{4,3,2,1,0:T(8,128)(2,1)} custom-call(bf16[8,2,8,2,64,128]{5,4,3,2,1,0:T(8,128)(2,1)S(1)} %bitcast.30), custom_call_target="tpu_custom_call" | custom-call | tf_op jit(solution)/shard_map/regroup/pallas_call | solution.py:155
  71.2 0.4 plane.1.own_ref
  71.6 0.0 copy-start.5
  71.6 0.1 collective-permute-start
  71.7 1.3 copy-done.5
  73.0 7.8 %all-to-all-start.1 = ((bf16[128,64,128]{2,1,0:T(8,128)(2,1)}), bf16[128,64,128]{2,1,0:T(8,128)(2,1)}, u32[]{:S(2)}, u32[]{:S(2)}) async-start(bf16[128,64,128]{2,1,0:T(8,128)(2,1)} %bitcast.19), calls=%async_computation.1 | async-start | bytes 4194304 | tf_op jit(solution)/shard_map/all_to_all | solution.py:660
  80.8 0.0 collective-permute-done.other_ref
  80.8 5.7 %product.1 = bf16[8,2,8,64,128]{4,3,2,1,0:T(8,128)(2,1)} custom-call(bf16[8,2,8,64,128]{4,3,2,1,0:T(8,128)(2,1)} %copy-done.5, bf16[8,2,8,64,128]{4,3,2,1,0:T(8,128)(2,1)} %collective-permute-done.other_ref), custom_call_target="tpu_custom_call" | custom-call | flops 2147483648 | bytes 6291456 | tf_op jit(solution)/shard_map/product/pallas_call | solution.py:264
  86.5 22.4 %all-to-all-done.1 = bf16[128,64,128]{2,1,0:T(8,128)(2,1)} async-done(((bf16[128,64,128]{2,1,0:T(8,128)(2,1)}), bf16[128,64,128]{2,1,0:T(8,128)(2,1)}, u32[]{:S(2)}, u32[]{:S(2)}) %all-to-all-start.1) | async-done | bytes 2097184 | tf_op jit(solution)/shard_map/all_to_all | solution.py:660
  108.8 0.0 copy-start.11
  108.8 7.8 %all-to-all-start.2 = ((bf16[128,64,128]{2,1,0:T(8,128)(2,1)}), bf16[128,64,128]{2,1,0:T(8,128)(2,1)}, u32[]{:S(2)}, u32[]{:S(2)}) async-start(bf16[128,64,128]{2,1,0:T(8,128)(2,1)} %bitcast.43), calls=%async_computation.2 | async-start | bytes 4194304 | tf_op jit(solution)/shard_map/all_to_all | solution.py:660
  116.7 0.8 slice.36.weight_ref
  117.5 0.0 copy-done.11
  117.5 0.2 copy.20
  117.7 0.1 fusion.5
  117.8 1.2 copy.21
  119.0 0.2 copy.18
  119.2 0.1 fusion.4
  119.3 0.0 copy-start.12
  119.3 0.0 copy-start.13
  119.4 0.0 copy-start.14
  119.4 0.0 copy-start.15
  119.4 0.0 copy-start
  119.4 0.0 copy-start.6
  119.4 0.0 copy-start.7
  119.4 1.2 copy.19
  120.6 2.7 %pad_maximum_fusion.weight_hbm = bf16[2,512,768]{2,1,0:T(8,128)(2,1)} fusion(bf16[1,512,768]{2,1,0:T(8,128)(2,1)} %bitcast.41, bf16[1,512,768]{2,1,0:T(8,128)(2,1)} %bitcast.42), kind=kLoop, calls=%fused_computation.6 | loop fusion | flops 786432 | bytes 3145728 | tf_op jit(solution)/shard_map/stack | solution.py:671
  123.3 0.0 copy-done.12
  123.3 0.0 copy-done.13
  123.3 0.0 copy-done.14
  123.3 0.1 fusion.10
  123.4 0.0 copy-done.15
  123.4 0.7 slice_bitcast_fusion.bias_ref
  124.1 0.0 copy-done
  124.1 0.0 copy-done.6
  124.1 0.0 copy-done.7
  124.1 3.5 %gates.1.own_gate_ref = bf16[64,128,128]{2,1,0:T(8,128)(2,1)S(1)} custom-call(bf16[64,128,128]{2,1,0:T(8,128)(2,1)S(1)} %copy-done, f32[1,128]{1,0:T(1,128)S(1)} %bitcast.34, f32[1,128]{1,0:T(1,128)S(1)} %bitcast.37, bf16[128,128]{1,0:T(8,128)(2,1)S(1)} %slice.36.weight_ref, f32[1,128]{1,0:T(1,128)S(1)} %slice_bitcast_fusion.bias_ref), custom_call_target="tpu_custom_call" | custom-call | flops 268435456 | bytes 4194304 | tf_op jit(solution)/shard_map/gates/pallas_call | solution.py:295
  127.6 0.0 copy-start.1
  127.6 1.3 copy-done.1
  128.9 5.0 %mirror_gates.1 = (bf16[64,128,128]{2,1,0:T(8,128)(2,1)S(1)}, bf16[64,128,128]{2,1,0:T(8,128)(2,1)S(1)}) custom-call(bf16[64,2,2,2,16,128]{5,4,3,2,1,0:T(8,128)(2,1)} %bitcast.20.mirror_ref, f32[1,128]{1,0:T(1,128)S(1)} %bitcast.35, f32[1,128]{1,0:T(1,128)S(1)} %bitcast.38, bf16[128,128]{1,0:T(8,128)(2,1)S(1)} %slice.36.weight_ref, ...), custom_call_target="tpu_custom_call" | custom-call | flops 268435456 | bytes 8388608 | tf_op jit(solution)/shard_map/mirror_gates/pallas_call | solution.py:335
  134.0 0.0 copy-start.3
  134.0 1.3 copy-done.3
  135.3 0.0 copy-start.4
  135.3 1.4 copy-done.4
  136.7 8.1 %all-to-all-done.2 = bf16[128,64,128]{2,1,0:T(8,128)(2,1)} async-done(((bf16[128,64,128]{2,1,0:T(8,128)(2,1)}), bf16[128,64,128]{2,1,0:T(8,128)(2,1)}, u32[]{:S(2)}, u32[]{:S(2)}) %all-to-all-start.2) | async-done | bytes 2097184 | tf_op jit(solution)/shard_map/all_to_all | solution.py:660
  144.7 0.0 copy-start.9
  144.7 7.2 %update.1.sym_ref = bf16[64,128,128]{2,1,0:T(8,128)(2,1)S(1)} custom-call(bf16[64,128,128]{2,1,0:T(8,128)(2,1)} %pair_ref.5, bf16[64,128,128]{2,1,0:T(8,128)(2,1)} %copy-done.1, bf16[64,128,128]{2,1,0:T(8,128)(2,1)} %copy-done.3, bf16[64,128,128]{2,1,0:T(8,128)(2,1)} %copy-done.4, bf16[8,2,8,64,128]{4,3,2,1,0:T(8,128)(2,1)} %bitcast.22.tri_ref, ...), custom_call_target="tpu_custom_call" | custom-call | tf_op jit(solution)/shard_map/update/pallas_call | solution.py:403
  152.0 1.9 %collective-permute-start.1 = (bf16[6,128,128]{2,1,0:T(8,128)(2,1)S(1)}, bf16[6,128,128]{2,1,0:T(8,128)(2,1)S(1)}, u32[]{:S(2)}, u32[]{:S(2)}) collective-permute-start(bf16[6,128,128]{2,1,0:T(8,128)(2,1)S(1)} %get-tuple-element.18), channel_id=1, source_target_pairs={{0,8},{8,16},{16,24},{24,32},{32,40},{40,48},{48,56},{56,64},{64,7... | collective-permute-start | bytes 589832 | tf_op jit(solution)/shard_map/ppermute | solution.py:651
  153.9 6.0 %collective-permute-start.2 = (bf16[6,128,128]{2,1,0:T(8,128)(2,1)S(1)}, bf16[6,128,128]{2,1,0:T(8,128)(2,1)S(1)}, u32[]{:S(2)}, u32[]{:S(2)}) collective-permute-start(bf16[6,128,128]{2,1,0:T(8,128)(2,1)S(1)} %get-tuple-element.17), channel_id=1, source_target_pairs={{8,0},{16,8},{24,16},{32,24},{40,32},{48,40},{56,48},{64,56},{72,6... | collective-permute-start | bytes 589832 | tf_op jit(solution)/shard_map/ppermute | solution.py:651
  160.0 1.4 collective-permute-done.1.top_ref
  161.4 1.7 collective-permute-done.2.bottom_ref
  163.1 4.2 %collective-permute-start.4 = (bf16[76,8,128]{2,1,0:T(8,128)(2,1)S(1)}, bf16[76,8,128]{2,1,0:T(8,128)(2,1)S(1)}, u32[]{:S(2)}, u32[]{:S(2)}) collective-permute-start(bf16[76,8,128]{2,1,0:T(8,128)(2,1)S(1)} %pad_maximum_fusion.2), channel_id=1, source_target_pairs={{1,0},{2,1},{3,2},{4,3},{5,4},{6,5},{7,6},{9,8},{10,9},{11,10},{12... | collective-permute-start | bytes 466952 | tf_op jit(solution)/shard_map/ppermute | solution.py:651
  167.4 2.1 %collective-permute-start.3 = (bf16[76,8,128]{2,1,0:T(8,128)(2,1)S(1)}, bf16[76,8,128]{2,1,0:T(8,128)(2,1)S(1)}, u32[]{:S(2)}, u32[]{:S(2)}) collective-permute-start(bf16[76,8,128]{2,1,0:T(8,128)(2,1)S(1)} %pad_maximum_fusion.1), channel_id=1, source_target_pairs={{0,1},{1,2},{2,3},{3,4},{4,5},{5,6},{6,7},{8,9},{9,10},{10,11},{11... | collective-permute-start | bytes 466952 | tf_op jit(solution)/shard_map/ppermute | solution.py:651
  169.5 0.1 pad_add_fusion.place_ref
  169.6 0.0 copy-done.8
  169.6 0.0 copy-done.9
  169.6 2.7 %activations.1.act_ref = bf16[64,128,128]{2,1,0:T(8,128)(2,1)S(1)} custom-call(bf16[64,128,128]{2,1,0:T(8,128)(2,1)S(1)} %update.1.sym_ref, f32[2,128]{1,0:T(2,128)S(1)} %copy-done.8, f32[2,128]{1,0:T(2,128)S(1)} %copy-done.9), custom_call_target="tpu_custom_call" | custom-call | flops 16777216 | bytes 4194304 | tf_op jit(solution)/shard_map/activations/pallas_call | solution.py:442
  172.4 0.0 collective-permute-done.4.high_ref
  172.4 4.9 %collective-permute-done.3.low_ref = bf16[76,8,128]{2,1,0:T(8,128)(2,1)S(1)} collective-permute-done((bf16[76,8,128]{2,1,0:T(8,128)(2,1)S(1)}, bf16[76,8,128]{2,1,0:T(8,128)(2,1)S(1)}, u32[]{:S(2)}, u32[]{:S(2)}) %collective-permute-start.3) | collective-permute-done | bytes 155680 | tf_op jit(solution)/shard_map/ppermute | solution.py:651
  177.3 0.0 copy-done.2
  177.3 0.0 copy-done.10
  177.3 13.9 %convolutions.1 = bf16[64,128,128]{2,1,0:T(8,128)(2,1)} custom-call(s32[2]{0:T(128)S(1)} %pad_add_fusion.place_ref, bf16[64,128,128]{2,1,0:T(8,128)(2,1)S(1)} %update.1.sym_ref, bf16[64,128,128]{2,1,0:T(8,128)(2,1)S(1)} %activations.1.act_ref, bf16[6,128,128]{2,1,0:T(8,128)(2,1)S(1)} %collective-permute-done.1.top_ref, ...), custom_call_target="tpu_custom_call" | custom-call | tf_op jit(solution)/shard_map/convolutions/pallas_call | solution.py:615
  (13 shorter events, 0.2 us)
Async XLA Ops:
  71.6 1.4 copy-start.5
  71.6 9.2 %collective-permute-start = (bf16[8,2,8,64,128]{4,3,2,1,0:T(8,128)(2,1)S(1)}, bf16[8,2,8,64,128]{4,3,2,1,0:T(8,128)(2,1)}, u32[]{:S(2)}, u32[]{:S(2)}) collective-permute-start(bf16[8,2,8,64,128]{4,3,2,1,0:T(8,128)(2,1)S(1)} %plane.1.own_ref), channel_id=1, source_target_pairs={{0,8},{8,0},{16,24},{24,16},{32,40},{40,32},{48,56},{56,48},{64,72... | collective-permute-start | bytes 6291464 | tf_op jit(solution)/shard_map/ppermute | solution.py:668
  73.0 35.9 %all-to-all-start.1 = ((bf16[128,64,128]{2,1,0:T(8,128)(2,1)}), bf16[128,64,128]{2,1,0:T(8,128)(2,1)}, u32[]{:S(2)}, u32[]{:S(2)}) async-start(bf16[128,64,128]{2,1,0:T(8,128)(2,1)} %bitcast.19), calls=%async_computation.1 | async-start | bytes 4194304 | tf_op jit(solution)/shard_map/all_to_all | solution.py:660
  108.8 8.6 %copy-start.11 = (bf16[2,9,128,128]{3,2,1,0:T(8,128)(2,1)S(1)}, bf16[2,9,128,128]{3,2,1,0:T(8,128)(2,1)}, u32[]{:S(2)}) copy-start(bf16[2,9,128,128]{3,2,1,0:T(8,128)(2,1)} %param.24) | copy-start | bytes 1769476
  108.8 35.9 %all-to-all-start.2 = ((bf16[128,64,128]{2,1,0:T(8,128)(2,1)}), bf16[128,64,128]{2,1,0:T(8,128)(2,1)}, u32[]{:S(2)}, u32[]{:S(2)}) async-start(bf16[128,64,128]{2,1,0:T(8,128)(2,1)} %bitcast.43), calls=%async_computation.2 | async-start | bytes 4194304 | tf_op jit(solution)/shard_map/all_to_all | solution.py:660
  119.3 4.0 %copy-start.12 = (bf16[64,128]{1,0:T(8,128)(2,1)S(1)}, bf16[64,128]{1,0:T(8,128)(2,1)}, u32[]{:S(2)}) copy-start(bf16[64,128]{1,0:T(8,128)(2,1)} %param.20) | copy-start | bytes 49156
  119.3 4.0 %copy-start.13 = (f32[64]{0:T(128)S(1)}, f32[64]{0:T(128)}, u32[]{:S(2)}) copy-start(f32[64]{0:T(128)} %param.19) | copy-start | bytes 772
  119.4 4.0 %copy-start.14 = (f32[64]{0:T(128)S(1)}, f32[64]{0:T(128)}, u32[]{:S(2)}) copy-start(f32[64]{0:T(128)} %param.18) | copy-start | bytes 772
  119.4 4.0 %copy-start.15 = (f32[128]{0:T(128)S(1)}, f32[128]{0:T(128)}, u32[]{:S(2)}) copy-start(f32[128]{0:T(128)} %param.21) | copy-start | bytes 1540
  119.4 4.7 %copy-start = (bf16[64,128,128]{2,1,0:T(8,128)(2,1)S(1)}, bf16[64,128,128]{2,1,0:T(8,128)(2,1)}, u32[]{:S(2)}) copy-start(bf16[64,128,128]{2,1,0:T(8,128)(2,1)} %pair_ref.5) | copy-start | bytes 6291460
  119.4 4.7 %copy-start.6 = (f32[128]{0:T(128)S(1)}, f32[128]{0:T(128)}, u32[]{:S(2)}) copy-start(f32[128]{0:T(128)} %param.14) | copy-start | bytes 1540
  119.4 4.7 %copy-start.7 = (f32[128]{0:T(128)S(1)}, f32[128]{0:T(128)}, u32[]{:S(2)}) copy-start(f32[128]{0:T(128)} %param.15) | copy-start | bytes 1540
  127.6 1.3 copy-start.1
  134.0 1.3 copy-start.3
  135.3 1.4 copy-start.4
  144.7 24.9 %copy-start.8 = (f32[2,128]{1,0:T(2,128)S(1)}, f32[2,128]{1,0:T(2,128)}, u32[]{:S(2)}) copy-start(f32[2,128]{1,0:T(2,128)} %gain_ref.3) | copy-start | bytes 3076
  144.7 24.9 %copy-start.9 = (f32[2,128]{1,0:T(2,128)S(1)}, f32[2,128]{1,0:T(2,128)}, u32[]{:S(2)}) copy-start(f32[2,128]{1,0:T(2,128)} %shift_ref.3) | copy-start | bytes 3076
  152.0 9.4 %collective-permute-start.1 = (bf16[6,128,128]{2,1,0:T(8,128)(2,1)S(1)}, bf16[6,128,128]{2,1,0:T(8,128)(2,1)S(1)}, u32[]{:S(2)}, u32[]{:S(2)}) collective-permute-start(bf16[6,128,128]{2,1,0:T(8,128)(2,1)S(1)} %get-tuple-element.18), channel_id=1, source_target_pairs={{0,8},{8,16},{16,24},{24,32},{32,40},{40,48},{48,56},{56,64},{64,7... | collective-permute-start | bytes 589832 | tf_op jit(solution)/shard_map/ppermute | solution.py:651
  153.9 9.2 %collective-permute-start.2 = (bf16[6,128,128]{2,1,0:T(8,128)(2,1)S(1)}, bf16[6,128,128]{2,1,0:T(8,128)(2,1)S(1)}, u32[]{:S(2)}, u32[]{:S(2)}) collective-permute-start(bf16[6,128,128]{2,1,0:T(8,128)(2,1)S(1)} %get-tuple-element.17), channel_id=1, source_target_pairs={{8,0},{16,8},{24,16},{32,24},{40,32},{48,40},{56,48},{64,56},{72,6... | collective-permute-start | bytes 589832 | tf_op jit(solution)/shard_map/ppermute | solution.py:651
  163.1 9.2 %collective-permute-start.4 = (bf16[76,8,128]{2,1,0:T(8,128)(2,1)S(1)}, bf16[76,8,128]{2,1,0:T(8,128)(2,1)S(1)}, u32[]{:S(2)}, u32[]{:S(2)}) collective-permute-start(bf16[76,8,128]{2,1,0:T(8,128)(2,1)S(1)} %pad_maximum_fusion.2), channel_id=1, source_target_pairs={{1,0},{2,1},{3,2},{4,3},{5,4},{6,5},{7,6},{9,8},{10,9},{11,10},{12... | collective-permute-start | bytes 466952 | tf_op jit(solution)/shard_map/ppermute | solution.py:651
  167.4 9.8 %collective-permute-start.3 = (bf16[76,8,128]{2,1,0:T(8,128)(2,1)S(1)}, bf16[76,8,128]{2,1,0:T(8,128)(2,1)S(1)}, u32[]{:S(2)}, u32[]{:S(2)}) collective-permute-start(bf16[76,8,128]{2,1,0:T(8,128)(2,1)S(1)} %pad_maximum_fusion.1), channel_id=1, source_target_pairs={{0,1},{1,2},{2,3},{3,4},{4,5},{5,6},{6,7},{8,9},{9,10},{10,11},{11... | collective-permute-start | bytes 466952 | tf_op jit(solution)/shard_map/ppermute | solution.py:651
  169.6 7.6 %copy-start.2 = (bf16[2,512,768]{2,1,0:T(8,128)(2,1)S(1)}, bf16[2,512,768]{2,1,0:T(8,128)(2,1)}, u32[]{:S(2)}) copy-start(bf16[2,512,768]{2,1,0:T(8,128)(2,1)} %pad_maximum_fusion.weight_hbm) | copy-start | bytes 4718596
  169.6 7.6 %copy-start.10 = (f32[2,128]{1,0:T(2,128)S(1)}, f32[2,128]{1,0:T(2,128)}, u32[]{:S(2)}) copy-start(f32[2,128]{1,0:T(2,128)} %bias_ref.3) | copy-start | bytes 3076

commit v8 on v7

--- a/solution.py
+++ b/solution.py
@@ -458,8 +458,8 @@
 WIDE = COLS + 4 * SIDE
 FIRST_TALL = ROWS + 2 * SECOND_DILATION
 FIRST_WIDE = COLS + 2 * SIDE
-GROUP_B, GROUP_C = 4, 8
-INNER_B, SLOTS_C = 18, 4
+GROUP_B, GROUP_C = 4, 16
+INNER_B, SLOTS_C = 18, 2
 CONV_VMEM = 40
 
 

time: 192 us -> 192 us (level)
  no operation moved by 1% of the time
where the time goes in v8:
time: 192 us; the launch traced here: 191 us
  blocking collectives  61.4 us (32%)
  Pallas kernels  48.1 us (25%)
  waiting for transfers between devices  38.4 us (20%)
  starting transfers between devices  30.1 us (16%)
  local copies, waits for them, and re-layouts  9.68 us (5%)
  other arithmetic  3.15 us (2%)
    all_to_all x1, blocking collectives, local(): lax.all_to_all(v, ('row', 'col'), split_axis=0, concat_axis=0, tiled=True)  61.4 us
    all_to_all x2, waiting for transfers between devices, local(): lax.all_to_all(v, ('row', 'col'), split_axis=0, concat_axis=0, tiled=True)  30.4 us
    all_to_all x2, starting transfers between devices, local(): lax.all_to_all(v, ('row', 'col'), split_axis=0, concat_axis=0, tiled=True)  15.7 us
    pallas_call x1, Pallas kernels, convolutions(): pl.pallas_call(convolution_kernel, out_shape=jax.ShapeDtypeStruct((ROWS,...  13.9 us
    ppermute x2, starting transfers between devices, neighbours(): lax.ppermute(low_strip, axis, backward)  10.3 us
    pallas_call x1, Pallas kernels, factors(): pl.pallas_call(factor_kernel, grid=(steps,), out_shape=jax.ShapeDtypeStru...  7.74 us
    pallas_call x1, Pallas kernels, update(): pl.pallas_call(update_kernel, grid=(ROWS // USTEP,), out_shape=jax.ShapeD...  7.17 us
    ppermute x2, waiting for transfers between devices, neighbours(): lax.ppermute(high_strip, axis, forward)  6.25 us
  transfers between devices with their start and end apart: 7, of which 5 were waited for; matrix products, arithmetic and copies ran while one was open for 4% of the time, Pallas kernels for 9%

profile of v8, /device:TPU:10, one launch (start us, length us, event | category | flops | bytes accessed | tf_op | source)
XLA Modules:
  0.0 191.3 jit_solution(5318415272703762402)
XLA Ops:
  0.0 7.7 %factors.1 = bf16[8,2,4,2,2,64,128]{6,5,4,3,2,1,0:T(8,128)(2,1)} custom-call(bf16[64,128,128]{2,1,0:T(8,128)(2,1)} %pair_ref.5, f32[1,128]{1,0:T(1,128)} %bitcast.33, f32[1,128]{1,0:T(1,128)} %bitcast.36, bf16[128,384]{1,0:T(8,128)(2,1)} %weight_ref.1, f32[384]{0:T(512)} %bias_ref.2), custom_call_target="tpu_custom_call" | custom-call | tf_op jit(solution)/shard_map/factors/pallas_call | solution.py:90
  7.7 61.4 %all_to_all.15 = bf16[128,2,64,128]{3,2,1,0:T(8,128)(2,1)S(1)} all-to-all(bf16[128,2,64,128]{3,2,1,0:T(8,128)(2,1)} %bitcast.40), channel_id=1, replica_groups=mesh['row'=16,'col'=8] {'row','col'}, dimensions={0} | all-to-all | bytes 8388608 | tf_op jit(solution)/shard_map/all_to_all | solution.py:660
  69.2 2.0 %regroup.1 = bf16[8,2,8,64,128]{4,3,2,1,0:T(8,128)(2,1)} custom-call(bf16[8,2,8,2,64,128]{5,4,3,2,1,0:T(8,128)(2,1)S(1)} %bitcast.30), custom_call_target="tpu_custom_call" | custom-call | tf_op jit(solution)/shard_map/regroup/pallas_call | solution.py:155
  71.2 0.4 plane.1.own_ref
  71.6 0.0 copy-start.5
  71.6 0.1 collective-permute-start
  71.7 1.3 copy-done.5
  73.0 7.8 %all-to-all-start.1 = ((bf16[128,64,128]{2,1,0:T(8,128)(2,1)}), bf16[128,64,128]{2,1,0:T(8,128)(2,1)}, u32[]{:S(2)}, u32[]{:S(2)}) async-start(bf16[128,64,128]{2,1,0:T(8,128)(2,1)} %bitcast.19), calls=%async_computation.1 | async-start | bytes 4194304 | tf_op jit(solution)/shard_map/all_to_all | solution.py:660
  80.8 0.0 collective-permute-done.other_ref
  80.8 5.7 %product.1 = bf16[8,2,8,64,128]{4,3,2,1,0:T(8,128)(2,1)} custom-call(bf16[8,2,8,64,128]{4,3,2,1,0:T(8,128)(2,1)} %copy-done.5, bf16[8,2,8,64,128]{4,3,2,1,0:T(8,128)(2,1)} %collective-permute-done.other_ref), custom_call_target="tpu_custom_call" | custom-call | flops 2147483648 | bytes 6291456 | tf_op jit(solution)/shard_map/product/pallas_call | solution.py:264
  86.5 22.4 %all-to-all-done.1 = bf16[128,64,128]{2,1,0:T(8,128)(2,1)} async-done(((bf16[128,64,128]{2,1,0:T(8,128)(2,1)}), bf16[128,64,128]{2,1,0:T(8,128)(2,1)}, u32[]{:S(2)}, u32[]{:S(2)}) %all-to-all-start.1) | async-done | bytes 2097184 | tf_op jit(solution)/shard_map/all_to_all | solution.py:660
  108.8 0.0 copy-start.11
  108.8 7.8 %all-to-all-start.2 = ((bf16[128,64,128]{2,1,0:T(8,128)(2,1)}), bf16[128,64,128]{2,1,0:T(8,128)(2,1)}, u32[]{:S(2)}, u32[]{:S(2)}) async-start(bf16[128,64,128]{2,1,0:T(8,128)(2,1)} %bitcast.43), calls=%async_computation.2 | async-start | bytes 4194304 | tf_op jit(solution)/shard_map/all_to_all | solution.py:660
  116.7 0.8 slice.36.weight_ref
  117.5 0.0 copy-done.11
  117.5 0.2 copy.20
  117.7 0.1 fusion.5
  117.8 1.2 copy.21
  119.0 0.2 copy.18
  119.2 0.1 fusion.4
  119.3 0.0 copy-start.12
  119.3 0.0 copy-start.13
  119.4 0.0 copy-start.14
  119.4 0.0 copy-start.15
  119.4 0.0 copy-start
  119.4 0.0 copy-start.6
  119.4 0.0 copy-start.7
  119.4 1.2 copy.19
  120.6 2.7 %pad_maximum_fusion.weight_hbm = bf16[2,512,768]{2,1,0:T(8,128)(2,1)} fusion(bf16[1,512,768]{2,1,0:T(8,128)(2,1)} %bitcast.41, bf16[1,512,768]{2,1,0:T(8,128)(2,1)} %bitcast.42), kind=kLoop, calls=%fused_computation.6 | loop fusion | flops 786432 | bytes 3145728 | tf_op jit(solution)/shard_map/stack | solution.py:671
  123.3 0.0 copy-done.12
  123.3 0.0 copy-done.13
  123.3 0.0 copy-done.14
  123.3 0.1 fusion.10
  123.4 0.0 copy-done.15
  123.4 0.7 slice_bitcast_fusion.bias_ref
  124.1 0.0 copy-done
  124.1 0.0 copy-done.6
  124.1 0.0 copy-done.7
  124.1 3.5 %gates.1.own_gate_ref = bf16[64,128,128]{2,1,0:T(8,128)(2,1)S(1)} custom-call(bf16[64,128,128]{2,1,0:T(8,128)(2,1)S(1)} %copy-done, f32[1,128]{1,0:T(1,128)S(1)} %bitcast.34, f32[1,128]{1,0:T(1,128)S(1)} %bitcast.37, bf16[128,128]{1,0:T(8,128)(2,1)S(1)} %slice.36.weight_ref, f32[1,128]{1,0:T(1,128)S(1)} %slice_bitcast_fusion.bias_ref), custom_call_target="tpu_custom_call" | custom-call | flops 268435456 | bytes 4194304 | tf_op jit(solution)/shard_map/gates/pallas_call | solution.py:295
  127.6 0.0 copy-start.1
  127.6 1.3 copy-done.1
  128.9 5.0 %mirror_gates.1 = (bf16[64,128,128]{2,1,0:T(8,128)(2,1)S(1)}, bf16[64,128,128]{2,1,0:T(8,128)(2,1)S(1)}) custom-call(bf16[64,2,2,2,16,128]{5,4,3,2,1,0:T(8,128)(2,1)} %bitcast.20.mirror_ref, f32[1,128]{1,0:T(1,128)S(1)} %bitcast.35, f32[1,128]{1,0:T(1,128)S(1)} %bitcast.38, bf16[128,128]{1,0:T(8,128)(2,1)S(1)} %slice.36.weight_ref, ...), custom_call_target="tpu_custom_call" | custom-call | flops 268435456 | bytes 8388608 | tf_op jit(solution)/shard_map/mirror_gates/pallas_call | solution.py:335
  134.0 0.0 copy-start.3
  134.0 1.3 copy-done.3
  135.3 0.0 copy-start.4
  135.3 1.4 copy-done.4
  136.7 8.1 %all-to-all-done.2 = bf16[128,64,128]{2,1,0:T(8,128)(2,1)} async-done(((bf16[128,64,128]{2,1,0:T(8,128)(2,1)}), bf16[128,64,128]{2,1,0:T(8,128)(2,1)}, u32[]{:S(2)}, u32[]{:S(2)}) %all-to-all-start.2) | async-done | bytes 2097184 | tf_op jit(solution)/shard_map/all_to_all | solution.py:660
  144.7 0.0 copy-start.9
  144.7 7.2 %update.1.sym_ref = bf16[64,128,128]{2,1,0:T(8,128)(2,1)S(1)} custom-call(bf16[64,128,128]{2,1,0:T(8,128)(2,1)} %pair_ref.5, bf16[64,128,128]{2,1,0:T(8,128)(2,1)} %copy-done.1, bf16[64,128,128]{2,1,0:T(8,128)(2,1)} %copy-done.3, bf16[64,128,128]{2,1,0:T(8,128)(2,1)} %copy-done.4, bf16[8,2,8,64,128]{4,3,2,1,0:T(8,128)(2,1)} %bitcast.22.tri_ref, ...), custom_call_target="tpu_custom_call" | custom-call | tf_op jit(solution)/shard_map/update/pallas_call | solution.py:403
  152.0 1.9 %collective-permute-start.1 = (bf16[6,128,128]{2,1,0:T(8,128)(2,1)S(1)}, bf16[6,128,128]{2,1,0:T(8,128)(2,1)S(1)}, u32[]{:S(2)}, u32[]{:S(2)}) collective-permute-start(bf16[6,128,128]{2,1,0:T(8,128)(2,1)S(1)} %get-tuple-element.18), channel_id=1, source_target_pairs={{0,8},{8,16},{16,24},{24,32},{32,40},{40,48},{48,56},{56,64},{64,7... | collective-permute-start | bytes 589832 | tf_op jit(solution)/shard_map/ppermute | solution.py:651
  153.9 6.0 %collective-permute-start.2 = (bf16[6,128,128]{2,1,0:T(8,128)(2,1)S(1)}, bf16[6,128,128]{2,1,0:T(8,128)(2,1)S(1)}, u32[]{:S(2)}, u32[]{:S(2)}) collective-permute-start(bf16[6,128,128]{2,1,0:T(8,128)(2,1)S(1)} %get-tuple-element.17), channel_id=1, source_target_pairs={{8,0},{16,8},{24,16},{32,24},{40,32},{48,40},{56,48},{64,56},{72,6... | collective-permute-start | bytes 589832 | tf_op jit(solution)/shard_map/ppermute | solution.py:651
  160.0 1.4 collective-permute-done.1.top_ref
  161.4 1.7 collective-permute-done.2.bottom_ref
  163.1 4.2 %collective-permute-start.4 = (bf16[76,8,128]{2,1,0:T(8,128)(2,1)S(1)}, bf16[76,8,128]{2,1,0:T(8,128)(2,1)S(1)}, u32[]{:S(2)}, u32[]{:S(2)}) collective-permute-start(bf16[76,8,128]{2,1,0:T(8,128)(2,1)S(1)} %pad_maximum_fusion.2), channel_id=1, source_target_pairs={{1,0},{2,1},{3,2},{4,3},{5,4},{6,5},{7,6},{9,8},{10,9},{11,10},{12... | collective-permute-start | bytes 466952 | tf_op jit(solution)/shard_map/ppermute | solution.py:651
  167.4 2.1 %collective-permute-start.3 = (bf16[76,8,128]{2,1,0:T(8,128)(2,1)S(1)}, bf16[76,8,128]{2,1,0:T(8,128)(2,1)S(1)}, u32[]{:S(2)}, u32[]{:S(2)}) collective-permute-start(bf16[76,8,128]{2,1,0:T(8,128)(2,1)S(1)} %pad_maximum_fusion.1), channel_id=1, source_target_pairs={{0,1},{1,2},{2,3},{3,4},{4,5},{5,6},{6,7},{8,9},{9,10},{10,11},{11... | collective-permute-start | bytes 466952 | tf_op jit(solution)/shard_map/ppermute | solution.py:651
  169.5 0.1 pad_add_fusion.place_ref
  169.6 0.0 copy-done.8
  169.6 0.0 copy-done.9
  169.6 2.7 %activations.1.act_ref = bf16[64,128,128]{2,1,0:T(8,128)(2,1)S(1)} custom-call(bf16[64,128,128]{2,1,0:T(8,128)(2,1)S(1)} %update.1.sym_ref, f32[2,128]{1,0:T(2,128)S(1)} %copy-done.8, f32[2,128]{1,0:T(2,128)S(1)} %copy-done.9), custom_call_target="tpu_custom_call" | custom-call | flops 16777216 | bytes 4194304 | tf_op jit(solution)/shard_map/activations/pallas_call | solution.py:442
  172.4 0.0 collective-permute-done.4.high_ref
  172.4 4.9 %collective-permute-done.3.low_ref = bf16[76,8,128]{2,1,0:T(8,128)(2,1)S(1)} collective-permute-done((bf16[76,8,128]{2,1,0:T(8,128)(2,1)S(1)}, bf16[76,8,128]{2,1,0:T(8,128)(2,1)S(1)}, u32[]{:S(2)}, u32[]{:S(2)}) %collective-permute-start.3) | collective-permute-done | bytes 155680 | tf_op jit(solution)/shard_map/ppermute | solution.py:651
  177.3 0.0 copy-done.2
  177.3 0.0 copy-done.10
  177.3 13.9 %convolutions.1 = bf16[64,128,128]{2,1,0:T(8,128)(2,1)} custom-call(s32[2]{0:T(128)S(1)} %pad_add_fusion.place_ref, bf16[64,128,128]{2,1,0:T(8,128)(2,1)S(1)} %update.1.sym_ref, bf16[64,128,128]{2,1,0:T(8,128)(2,1)S(1)} %activations.1.act_ref, bf16[6,128,128]{2,1,0:T(8,128)(2,1)S(1)} %collective-permute-done.1.top_ref, ...), custom_call_target="tpu_custom_call" | custom-call | tf_op jit(solution)/shard_map/convolutions/pallas_call | solution.py:615
  (13 shorter events, 0.2 us)
Async XLA Ops:
  71.6 1.4 copy-start.5
  71.6 9.2 %collective-permute-start = (bf16[8,2,8,64,128]{4,3,2,1,0:T(8,128)(2,1)S(1)}, bf16[8,2,8,64,128]{4,3,2,1,0:T(8,128)(2,1)}, u32[]{:S(2)}, u32[]{:S(2)}) collective-permute-start(bf16[8,2,8,64,128]{4,3,2,1,0:T(8,128)(2,1)S(1)} %plane.1.own_ref), channel_id=1, source_target_pairs={{0,8},{8,0},{16,24},{24,16},{32,40},{40,32},{48,56},{56,48},{64,72... | collective-permute-start | bytes 6291464 | tf_op jit(solution)/shard_map/ppermute | solution.py:668
  73.0 35.9 %all-to-all-start.1 = ((bf16[128,64,128]{2,1,0:T(8,128)(2,1)}), bf16[128,64,128]{2,1,0:T(8,128)(2,1)}, u32[]{:S(2)}, u32[]{:S(2)}) async-start(bf16[128,64,128]{2,1,0:T(8,128)(2,1)} %bitcast.19), calls=%async_computation.1 | async-start | bytes 4194304 | tf_op jit(solution)/shard_map/all_to_all | solution.py:660
  108.8 8.6 %copy-start.11 = (bf16[2,9,128,128]{3,2,1,0:T(8,128)(2,1)S(1)}, bf16[2,9,128,128]{3,2,1,0:T(8,128)(2,1)}, u32[]{:S(2)}) copy-start(bf16[2,9,128,128]{3,2,1,0:T(8,128)(2,1)} %param.24) | copy-start | bytes 1769476
  108.8 35.9 %all-to-all-start.2 = ((bf16[128,64,128]{2,1,0:T(8,128)(2,1)}), bf16[128,64,128]{2,1,0:T(8,128)(2,1)}, u32[]{:S(2)}, u32[]{:S(2)}) async-start(bf16[128,64,128]{2,1,0:T(8,128)(2,1)} %bitcast.43), calls=%async_computation.2 | async-start | bytes 4194304 | tf_op jit(solution)/shard_map/all_to_all | solution.py:660
  119.3 4.0 %copy-start.12 = (bf16[64,128]{1,0:T(8,128)(2,1)S(1)}, bf16[64,128]{1,0:T(8,128)(2,1)}, u32[]{:S(2)}) copy-start(bf16[64,128]{1,0:T(8,128)(2,1)} %param.20) | copy-start | bytes 49156
  119.3 4.0 %copy-start.13 = (f32[64]{0:T(128)S(1)}, f32[64]{0:T(128)}, u32[]{:S(2)}) copy-start(f32[64]{0:T(128)} %param.19) | copy-start | bytes 772
  119.4 4.0 %copy-start.14 = (f32[64]{0:T(128)S(1)}, f32[64]{0:T(128)}, u32[]{:S(2)}) copy-start(f32[64]{0:T(128)} %param.18) | copy-start | bytes 772
  119.4 4.0 %copy-start.15 = (f32[128]{0:T(128)S(1)}, f32[128]{0:T(128)}, u32[]{:S(2)}) copy-start(f32[128]{0:T(128)} %param.21) | copy-start | bytes 1540
  119.4 4.7 %copy-start = (bf16[64,128,128]{2,1,0:T(8,128)(2,1)S(1)}, bf16[64,128,128]{2,1,0:T(8,128)(2,1)}, u32[]{:S(2)}) copy-start(bf16[64,128,128]{2,1,0:T(8,128)(2,1)} %pair_ref.5) | copy-start | bytes 6291460
  119.4 4.7 %copy-start.6 = (f32[128]{0:T(128)S(1)}, f32[128]{0:T(128)}, u32[]{:S(2)}) copy-start(f32[128]{0:T(128)} %param.14) | copy-start | bytes 1540
  119.4 4.7 %copy-start.7 = (f32[128]{0:T(128)S(1)}, f32[128]{0:T(128)}, u32[]{:S(2)}) copy-start(f32[128]{0:T(128)} %param.15) | copy-start | bytes 1540
  127.6 1.3 copy-start.1
  134.0 1.3 copy-start.3
  135.3 1.4 copy-start.4
  144.7 24.9 %copy-start.8 = (f32[2,128]{1,0:T(2,128)S(1)}, f32[2,128]{1,0:T(2,128)}, u32[]{:S(2)}) copy-start(f32[2,128]{1,0:T(2,128)} %gain_ref.3) | copy-start | bytes 3076
  144.7 24.9 %copy-start.9 = (f32[2,128]{1,0:T(2,128)S(1)}, f32[2,128]{1,0:T(2,128)}, u32[]{:S(2)}) copy-start(f32[2,128]{1,0:T(2,128)} %shift_ref.3) | copy-start | bytes 3076
  152.0 9.4 %collective-permute-start.1 = (bf16[6,128,128]{2,1,0:T(8,128)(2,1)S(1)}, bf16[6,128,128]{2,1,0:T(8,128)(2,1)S(1)}, u32[]{:S(2)}, u32[]{:S(2)}) collective-permute-start(bf16[6,128,128]{2,1,0:T(8,128)(2,1)S(1)} %get-tuple-element.18), channel_id=1, source_target_pairs={{0,8},{8,16},{16,24},{24,32},{32,40},{40,48},{48,56},{56,64},{64,7... | collective-permute-start | bytes 589832 | tf_op jit(solution)/shard_map/ppermute | solution.py:651
  153.9 9.2 %collective-permute-start.2 = (bf16[6,128,128]{2,1,0:T(8,128)(2,1)S(1)}, bf16[6,128,128]{2,1,0:T(8,128)(2,1)S(1)}, u32[]{:S(2)}, u32[]{:S(2)}) collective-permute-start(bf16[6,128,128]{2,1,0:T(8,128)(2,1)S(1)} %get-tuple-element.17), channel_id=1, source_target_pairs={{8,0},{16,8},{24,16},{32,24},{40,32},{48,40},{56,48},{64,56},{72,6... | collective-permute-start | bytes 589832 | tf_op jit(solution)/shard_map/ppermute | solution.py:651
  163.1 9.2 %collective-permute-start.4 = (bf16[76,8,128]{2,1,0:T(8,128)(2,1)S(1)}, bf16[76,8,128]{2,1,0:T(8,128)(2,1)S(1)}, u32[]{:S(2)}, u32[]{:S(2)}) collective-permute-start(bf16[76,8,128]{2,1,0:T(8,128)(2,1)S(1)} %pad_maximum_fusion.2), channel_id=1, source_target_pairs={{1,0},{2,1},{3,2},{4,3},{5,4},{6,5},{7,6},{9,8},{10,9},{11,10},{12... | collective-permute-start | bytes 466952 | tf_op jit(solution)/shard_map/ppermute | solution.py:651
  167.4 9.8 %collective-permute-start.3 = (bf16[76,8,128]{2,1,0:T(8,128)(2,1)S(1)}, bf16[76,8,128]{2,1,0:T(8,128)(2,1)S(1)}, u32[]{:S(2)}, u32[]{:S(2)}) collective-permute-start(bf16[76,8,128]{2,1,0:T(8,128)(2,1)S(1)} %pad_maximum_fusion.1), channel_id=1, source_target_pairs={{0,1},{1,2},{2,3},{3,4},{4,5},{5,6},{6,7},{8,9},{9,10},{10,11},{11... | collective-permute-start | bytes 466952 | tf_op jit(solution)/shard_map/ppermute | solution.py:651
  169.6 7.6 %copy-start.2 = (bf16[2,512,768]{2,1,0:T(8,128)(2,1)S(1)}, bf16[2,512,768]{2,1,0:T(8,128)(2,1)}, u32[]{:S(2)}) copy-start(bf16[2,512,768]{2,1,0:T(8,128)(2,1)} %pad_maximum_fusion.weight_hbm) | copy-start | bytes 4718596
  169.6 7.6 %copy-start.10 = (f32[2,128]{1,0:T(2,128)S(1)}, f32[2,128]{1,0:T(2,128)}, u32[]{:S(2)}) copy-start(f32[2,128]{1,0:T(2,128)} %bias_ref.3) | copy-start | bytes 3076
